TPU v7x, 128 devices: a whole 4x4x4 slice. The times are simulated.
128 devices in a mesh: seq: 16 (over z, x_lo, core), dp: 8 (over x_hi, y).
Axes of the slice: x: 4 (x_hi: 2, x_lo: 2; x = x_hi * 2 + x_lo), y: 4, z: 4, core: 2. Of those that a mesh axis runs over, the one named last changes fastest.
Arguments:
- hidden_in: bfloat16 [8, 2048, 1024], P('dp', 'seq'), may hold values from -6 to 6
- out_cot: bfloat16 [8, 2048, 1024], P('dp', 'seq'), may hold values from -6 to 6
- in_weight: float32 [1024, 7168], P(('seq', 'dp')), may hold values from -0.1875 to 0.1875
- out_weight: float32 [5120, 1024], P(('seq', 'dp')), may hold values from -0.3125 to 0.3125
- vectors: float32 [13, 1024], P(None, ('seq', 'dp')), as said below
- in_first: float32 [1024, 7168], P(('seq', 'dp')), may hold values from -0.0017089844 to 0.0017089844
- in_second: float32 [1024, 7168], P(('seq', 'dp')), may hold values from 3.9694434e-08 to 6.3511095e-07
- out_first: float32 [5120, 1024], P(('seq', 'dp')), may hold values from -0.0017089844 to 0.0017089844
- out_second: float32 [5120, 1024], P(('seq', 'dp')), may hold values from 3.9694434e-08 to 6.3511095e-07
- vec_first: float32 [13, 1024], P(None, ('seq', 'dp')), may hold values from -0.0048828125 to 0.0048828125
- vec_second: float32 [13, 1024], P(None, ('seq', 'dp')), may hold values from 3.5724992e-07 to 5.7159987e-06
- lengths: int32 [8], P('dp'), may hold values from 1024 to 2048, as said below
- span_of: int32 [16, 2], replicated, may hold values from 0 to 31, as said below
Outputs:
- block_out: bfloat16 [8, 2048, 1024], P('dp', 'seq')
- input_grad: bfloat16 [8, 2048, 1024], P('dp', 'seq')
- grad_norm: float32 [], replicated
- new_in: float32 [1024, 7168], P(('seq', 'dp'))
- new_out: float32 [5120, 1024], P(('seq', 'dp'))
- new_vectors: float32 [13, 1024], P(None, ('seq', 'dp'))
- new_in_first: float32 [1024, 7168], P(('seq', 'dp'))
- new_out_first: float32 [5120, 1024], P(('seq', 'dp'))
- new_vec_first: float32 [13, 1024], P(None, ('seq', 'dp'))
- new_in_second: float32 [1024, 7168], P(('seq', 'dp'))
- new_out_second: float32 [5120, 1024], P(('seq', 'dp'))
- new_vec_second: float32 [13, 1024], P(None, ('seq', 'dp'))
- low_in: bfloat16 [1024, 7168], P(('seq', 'dp'))
- low_out: bfloat16 [5120, 1024], P(('seq', 'dp'))
- low_vectors: bfloat16 [13, 1024], P(None, ('seq', 'dp'))
Inputs may be any that keep to these rules, and one draw needn't show every extreme that they name: `lengths`: one row, drawn from the seed, holds 2048 real tokens. `span_of`: row s holds c and 31 - c; the first entries over all s are a permutation. `vectors`: rows 0 and 2 are the norms' gains, rows 1 and 3 their biases, the rest biases as the steps name them.
All inputs are finite; a program needn't handle non-finite values.
Results may differ from a plain program's by a relative error of at most 0.014.
Values may be sent and summed in bfloat16 or wider, within the bound.
A program may use at most 256 MiB of HBM per device.

v0:
```python
import math

import jax
import jax.numpy as jnp
from jax import lax
from jax.sharding import PartitionSpec as P

D = 1024
FF = 4096
HEADS = 16
HEAD = 64
ROT = 16
STEP = 5


NORM_EPS = 1e-05
NEG_FILL = -1e30
CLIP_NORM = 1.0
RATE_MATRIX = 0.02
RATE_VECTOR = 0.2
BETA_ONE = 0.5
BETA_TWO = 0.5
DECAY_RATE = 0.1
ADAM_EPS = 1e-08
THETA_BASE = 10000.0


def token_positions(span_of, tok_dev, shards):
    rows_all = jnp.arange(tok_dev * shards, dtype=jnp.int32)
    span_len = tok_dev // 2
    slot_ids = rows_all // tok_dev * 2 + rows_all % tok_dev // span_len
    table = span_of.reshape(-1)
    match = slot_ids[:, None] == jnp.arange(2 * shards, dtype=jnp.int32)[None, :]
    starts = jnp.sum(jnp.where(match, table[None, :], 0), axis=1)
    return starts * span_len + rows_all % span_len


def rotary_tables(positions, rot_dims):
    half_dims = rot_dims // 2
    freqs = THETA_BASE ** (-2.0 * jnp.arange(half_dims, dtype=jnp.float32) / rot_dims)
    angles = positions.astype(jnp.float32)[:, None] * freqs[None, :]
    return (jnp.cos(angles), jnp.sin(angles))


def rotate(values, cosine, sine_table, rot_dims):
    half_dims = rot_dims // 2
    first_half = values[..., :half_dims]
    second_half = values[..., half_dims:rot_dims]
    cos_part = cosine[:, None, :]
    sin_part = sine_table[:, None, :]
    return jnp.concatenate(
        [
            first_half * cos_part - second_half * sin_part,
            second_half * cos_part + first_half * sin_part,
            values[..., rot_dims:],
        ],
        axis=-1,
    )


def unrotate(grads, cosine, sine_table, rot_dims):
    half_dims = rot_dims // 2
    first_half = grads[..., :half_dims]
    second_half = grads[..., half_dims:rot_dims]
    cos_part = cosine[:, None, :]
    sin_part = sine_table[:, None, :]
    return jnp.concatenate(
        [
            first_half * cos_part + second_half * sin_part,
            second_half * cos_part - first_half * sin_part,
            grads[..., rot_dims:],
        ],
        axis=-1,
    )


def norm_back(scaled_grad, x_hat, inv_std):
    return inv_std * (
        scaled_grad
        - jnp.mean(scaled_grad, axis=-1, keepdims=True)
        - x_hat * jnp.mean(scaled_grad * x_hat, axis=-1, keepdims=True)
    )


def adam_step(weight, grad, first, second, factor, rate, decay):
    clipped = grad * factor
    first_new = BETA_ONE * first + (1.0 - BETA_ONE) * clipped
    second_new = BETA_TWO * second + (1.0 - BETA_TWO) * clipped * clipped
    first_hat = first_new / (1.0 - BETA_ONE**STEP)
    second_hat = second_new / (1.0 - BETA_TWO**STEP)
    weight_new = weight * (1.0 - rate * decay) - rate * first_hat / (
        jnp.sqrt(second_hat) + ADAM_EPS
    )
    return (weight_new, first_new, second_new)


def body(
    hidden_in,
    out_cot,
    in_weight,
    out_weight,
    vectors,
    in_first,
    in_second,
    out_first,
    out_second,
    vec_first,
    vec_second,
    lengths,
    span_of,
):
    tok_rows = hidden_in.shape[1]
    seq_count = lax.axis_size("seq")
    seq_index = lax.axis_index("seq")
    shard_index = lax.axis_index(("seq", "dp"))
    key_rows = tok_rows * seq_count
    scale_factor = HEAD ** (-0.5)
    group_size = 8
    head_groups = HEADS // group_size
    positions_all = token_positions(span_of, tok_rows, seq_count)
    my_positions = lax.dynamic_slice_in_dim(positions_all, seq_index * tok_rows, tok_rows)
    length = lengths[0]
    allowed = (positions_all[None, :] <= my_positions[:, None]) & (positions_all < length)[None, :]
    valid = (my_positions < length).astype(jnp.float32)
    in_low = in_weight.astype(jnp.bfloat16)
    out_low = out_weight.astype(jnp.bfloat16)
    vec_low = vectors.astype(jnp.bfloat16)
    in_full, out_full, vec_full = (
        lax.all_gather(in_low, ("seq", "dp"), axis=0, tiled=True),
        lax.all_gather(out_low, ("seq", "dp"), axis=0, tiled=True),
        lax.all_gather(vec_low, ("seq", "dp"), axis=1, tiled=True),
    )
    vec_used = vec_full.astype(jnp.float32)
    x_rows = hidden_in[0].astype(jnp.float32)
    row_mean = jnp.mean(x_rows, axis=-1, keepdims=True)
    centered = x_rows - row_mean
    inv_std = lax.rsqrt(jnp.mean(centered * centered, axis=-1, keepdims=True) + NORM_EPS)
    x_hat = centered * inv_std
    normed_a = (x_hat * vec_used[0] + vec_used[1]).astype(jnp.bfloat16)
    normed_m = (x_hat * vec_used[2] + vec_used[3]).astype(jnp.bfloat16)
    qkv_bias = jnp.concatenate([vec_used[4], vec_used[5], vec_used[6]])
    qkv = jnp.dot(normed_a, in_full[:, : 3 * D], preferred_element_type=jnp.float32) + qkv_bias
    pre = jnp.dot(normed_m, in_full[:, 3 * D :], preferred_element_type=jnp.float32) + vec_used[
        9:
    ].reshape(FF)
    cosine, sine_table = rotary_tables(my_positions, ROT)
    query = rotate(qkv[:, :D].reshape(tok_rows, HEADS, HEAD), cosine, sine_table, ROT).astype(
        jnp.bfloat16
    )
    key_low = (
        rotate(qkv[:, D : 2 * D].reshape(tok_rows, HEADS, HEAD), cosine, sine_table, ROT)
        .reshape(tok_rows, D)
        .astype(jnp.bfloat16)
    )
    value_low = qkv[:, 2 * D : 3 * D].astype(jnp.bfloat16)
    keys_flat, values_flat = (
        lax.all_gather(key_low, "seq", axis=0, tiled=True),
        lax.all_gather(value_low, "seq", axis=0, tiled=True),
    )
    keys_all = keys_flat.reshape(key_rows, HEADS, HEAD)
    values_all = values_flat.reshape(key_rows, HEADS, HEAD)

    def masked_scores(group_idx):
        head_first = group_idx * group_size
        query_part = query[:, head_first : head_first + group_size]
        key_part = keys_all[:, head_first : head_first + group_size]
        scores = (
            jnp.einsum("thd,nhd->htn", query_part, key_part, preferred_element_type=jnp.float32)
            * scale_factor
        )
        return jnp.where(allowed[None], scores, NEG_FILL)

    attn_parts = []
    lse_parts = []
    for group_idx in range(head_groups):
        head_first = group_idx * group_size
        scores = masked_scores(group_idx)
        row_max = jnp.max(scores, axis=-1, keepdims=True)
        exp_scores = jnp.exp(scores - row_max)
        totals = jnp.sum(exp_scores, axis=-1, keepdims=True)
        probs_low = (exp_scores / totals).astype(jnp.bfloat16)
        lse_parts.append(row_max[..., 0] + jnp.log(totals[..., 0]))
        attn_parts.append(
            jnp.einsum(
                "htn,nhd->thd",
                probs_low,
                values_all[:, head_first : head_first + group_size],
                preferred_element_type=jnp.float32,
            )
        )
    attended = jnp.concatenate(attn_parts, axis=1).reshape(tok_rows, D).astype(jnp.bfloat16)
    log_sums = jnp.concatenate(lse_parts, axis=0)
    normal_cdf = 0.5 * (1.0 + lax.erf(pre * (1.0 / math.sqrt(2.0))))
    activ = (pre * normal_cdf).astype(jnp.bfloat16)
    joined = jnp.concatenate([attended, activ], axis=1)
    block_out = (
        x_rows
        + jnp.dot(joined, out_full, preferred_element_type=jnp.float32)
        + vec_used[7]
        + vec_used[8]
    ).astype(jnp.bfloat16)
    in_back, out_back = (
        lax.all_gather(in_low, ("seq", "dp"), axis=0, tiled=True),
        lax.all_gather(out_low, ("seq", "dp"), axis=0, tiled=True),
    )
    cot_low = (out_cot[0].astype(jnp.float32) * valid[:, None]).astype(jnp.bfloat16)
    joined_grad = jnp.dot(cot_low, out_back.T, preferred_element_type=jnp.float32)
    attended_grad = joined_grad[:, :D].astype(jnp.bfloat16).reshape(tok_rows, HEADS, HEAD)
    activ_grad = joined_grad[:, D:]
    normal_pdf = jnp.exp(-0.5 * pre * pre) * (1.0 / math.sqrt(2.0 * math.pi))
    pre_grad = activ_grad * (normal_cdf + pre * normal_pdf)
    query_grads = []
    score_parts = []
    prob_parts = []
    for group_idx in range(head_groups):
        head_first = group_idx * group_size
        scores = masked_scores(group_idx)
        probs = jnp.where(
            allowed[None],
            jnp.exp(scores - log_sums[head_first : head_first + group_size][..., None]),
            0.0,
        )
        prob_grad = jnp.einsum(
            "thd,nhd->htn",
            attended_grad[:, head_first : head_first + group_size],
            values_all[:, head_first : head_first + group_size],
            preferred_element_type=jnp.float32,
        )
        delta = jnp.sum(probs * prob_grad, axis=-1, keepdims=True)
        score_grad = (probs * (prob_grad - delta)).astype(jnp.bfloat16)
        query_grads.append(
            jnp.einsum(
                "htn,nhd->thd",
                score_grad,
                keys_all[:, head_first : head_first + group_size],
                preferred_element_type=jnp.float32,
            )
            * scale_factor
        )
        score_parts.append(score_grad)
        prob_parts.append(probs.astype(jnp.bfloat16))
    score_all = jnp.concatenate(score_parts, axis=0)
    prob_all = jnp.concatenate(prob_parts, axis=0)
    query_grad = jnp.concatenate(query_grads, axis=1)
    key_part = (
        jnp.einsum("htn,thd->nhd", score_all, query, preferred_element_type=jnp.float32)
        * scale_factor
    )
    value_part = jnp.einsum(
        "htn,thd->nhd", prob_all, attended_grad, preferred_element_type=jnp.float32
    )
    kv_grad = lax.psum_scatter(
        jnp.concatenate(
            [
                key_part.reshape(tok_rows * lax.axis_size("seq"), D),
                value_part.reshape(tok_rows * lax.axis_size("seq"), D),
            ],
            axis=1,
        ),
        "seq",
        scatter_dimension=0,
        tiled=True,
    )
    query_pre = unrotate(query_grad, cosine, sine_table, ROT).reshape(tok_rows, D)
    key_pre = unrotate(
        kv_grad[:, :D].reshape(tok_rows, HEADS, HEAD), cosine, sine_table, ROT
    ).reshape(tok_rows, D)
    mixed_grad = jnp.concatenate([query_pre, key_pre, kv_grad[:, D:], pre_grad], axis=1).astype(
        jnp.bfloat16
    )
    normed_a_grad = jnp.dot(
        mixed_grad[:, : 3 * D], in_back[:, : 3 * D].T, preferred_element_type=jnp.float32
    )
    normed_m_grad = jnp.dot(
        mixed_grad[:, 3 * D :], in_back[:, 3 * D :].T, preferred_element_type=jnp.float32
    )
    input_grad = (
        cot_low.astype(jnp.float32)
        + norm_back(normed_a_grad * vec_used[0], x_hat, inv_std)
        + norm_back(normed_m_grad * vec_used[2], x_hat, inv_std)
    ).astype(jnp.bfloat16)
    mixed_sums = jnp.sum(mixed_grad.astype(jnp.float32), axis=0)
    cot_sum = jnp.sum(cot_low.astype(jnp.float32), axis=0)
    norm_sums = jnp.stack(
        [
            jnp.sum(normed_a_grad * x_hat, axis=0),
            jnp.sum(normed_a_grad, axis=0),
            jnp.sum(normed_m_grad * x_hat, axis=0),
            jnp.sum(normed_m_grad, axis=0),
        ],
        axis=0,
    )
    vec_local = jnp.concatenate(
        [
            norm_sums,
            mixed_sums[: 3 * D].reshape(3, D),
            cot_sum[None],
            cot_sum[None],
            mixed_sums[3 * D :].reshape(FF // D, D),
        ],
        axis=0,
    )
    part_a = lax.dot_general(
        normed_a,
        mixed_grad[:, : 3 * D],
        (((0,), (0,)), ((), ())),
        preferred_element_type=jnp.float32,
    )
    part_m = lax.dot_general(
        normed_m,
        mixed_grad[:, 3 * D :],
        (((0,), (0,)), ((), ())),
        preferred_element_type=jnp.float32,
    )
    grad_in = lax.psum_scatter(
        jnp.concatenate([part_a, part_m], axis=1), ("seq", "dp"), scatter_dimension=0, tiled=True
    )
    grad_out = lax.psum_scatter(
        lax.dot_general(
            joined, cot_low, (((0,), (0,)), ((), ())), preferred_element_type=jnp.float32
        ),
        ("seq", "dp"),
        scatter_dimension=0,
        tiled=True,
    )
    local_squares = jnp.sum(grad_in * grad_in) + jnp.sum(grad_out * grad_out)
    square_sum, vec_grad_full = lax.psum((local_squares, vec_local), ("seq", "dp"))
    grad_norm = jnp.sqrt(square_sum + jnp.sum(vec_grad_full * vec_grad_full))
    factor = jnp.minimum(1.0, CLIP_NORM / grad_norm)
    vec_cols = vectors.shape[1]
    grad_vec = lax.dynamic_slice_in_dim(vec_grad_full, shard_index * vec_cols, vec_cols, 1)
    new_in, new_in_first, new_in_second = adam_step(
        in_weight, grad_in, in_first, in_second, factor, RATE_MATRIX, DECAY_RATE
    )
    new_out, new_out_first, new_out_second = adam_step(
        out_weight, grad_out, out_first, out_second, factor, RATE_MATRIX, DECAY_RATE
    )
    new_vectors, new_vec_first, new_vec_second = adam_step(
        vectors, grad_vec, vec_first, vec_second, factor, RATE_VECTOR, 0.0
    )
    return (
        block_out[None],
        input_grad[None],
        grad_norm,
        new_in,
        new_out,
        new_vectors,
        new_in_first,
        new_out_first,
        new_vec_first,
        new_in_second,
        new_out_second,
        new_vec_second,
        new_in.astype(jnp.bfloat16),
        new_out.astype(jnp.bfloat16),
        new_vectors.astype(jnp.bfloat16),
    )


def solution(mesh):
    return jax.shard_map(
        body,
        mesh=mesh,
        in_specs=(
            P("dp", "seq", None),
            P("dp", "seq", None),
            P(("seq", "dp"), None),
            P(("seq", "dp"), None),
            P(None, ("seq", "dp")),
            P(("seq", "dp"), None),
            P(("seq", "dp"), None),
            P(("seq", "dp"), None),
            P(("seq", "dp"), None),
            P(None, ("seq", "dp")),
            P(None, ("seq", "dp")),
            P("dp"),
            P(),
        ),
        out_specs=(
            P("dp", "seq", None),
            P("dp", "seq", None),
            P(),
            P(("seq", "dp"), None),
            P(("seq", "dp"), None),
            P(None, ("seq", "dp")),
            P(("seq", "dp"), None),
            P(("seq", "dp"), None),
            P(None, ("seq", "dp")),
            P(("seq", "dp"), None),
            P(("seq", "dp"), None),
            P(None, ("seq", "dp")),
            P(("seq", "dp"), None),
            P(("seq", "dp"), None),
            P(None, ("seq", "dp")),
        ),
        check_vma=False,
    )
```

profile of v0, /device:TPU:1, one launch (start us, length us, event | category | flops | bytes accessed | tf_op | source)
XLA Modules:
  0.0 2483.3 jit_solution(18375216376040499850)
XLA Ops:
  7.2 1.6 convert_element_type.99
  8.9 1.6 convert_element_type.107
  13.0 305.5 %all_gather.17 = bf16[13,1024]{0,1:T(8,128)(2,1)S(1)} all-gather(bf16[13,8]{0,1:T(8,128)(2,1)S(1)} %convert_element_type.96), channel_id=1, replica_groups=mesh['seq'=16,'dp'=8] {'seq','dp'}, dimensions={1}, use_global_device_ids=true | all-gather | bytes 26832 | tf_op jit(solution)/shard_map/all_gather | solution.py:131
  318.5 2.4 slice_reduce_fusion.1
  322.1 1.2 fusion.82
  323.4 14.7 all-gather.5.cloned.1.call-done
  338.1 4.0 fusion.27
  344.5 1.8 slice.330
  346.7 313.3 %all-gather.11.cloned.1.call-done = bf16[5120,1024]{1,0:T(8,128)(2,1)} async-done(((bf16[40,1024]{1,0:T(8,128)(2,1)}), bf16[5120,1024]{1,0:T(8,128)(2,1)}) %all-gather.11.cloned.1.call-update) | async-done | bytes 10485776 | tf_op jit(solution)/shard_map/all_gather | solution.py:130
  660.0 7.6 fusion.126
  667.6 1.5 copy-done.9
  669.4 38.4 %all-gather.9.cloned.1.call-done = bf16[2048,1024]{0,1:T(8,128)(2,1)} async-done(((bf16[128,1024]{0,1:T(8,128)(2,1)}), bf16[2048,1024]{0,1:T(8,128)(2,1)}) %all-gather.9.cloned.1.call-update) | async-done | bytes 4194320 | tf_op jit(solution)/shard_map/all_gather | solution.py:157
  707.7 3.6 fusion.18
  711.4 4.2 copy-done.4
  715.6 2.6 fusion.8
  718.3 4.5 fusion.42
  722.8 24.4 all-gather.7.cloned.1.call-done
  747.2 6.5 copy.114
  753.7 10.8 multiply_reduce_fusion.1
  765.6 2.2 fusion.9
  767.8 5.9 multiply_reduce_fusion
  773.8 11.4 multiply_convert_fusion.1
  785.2 4.0 fusion.4
  789.2 9.2 copy.122
  798.4 8.0 broadcast_multiply_fusion
  806.5 9.4 copy.121
  815.9 11.7 pad_maximum_fusion.1
  828.5 6.6 fusion.37
  835.1 6.8 fusion.54
  841.9 2.5 fusion.55
  844.6 8.7 fusion.56
  853.6 8.2 fusion.120
  861.8 1.6 fusion.51
  864.0 1.6 fusion.50
  866.3 141.7 %reduce-scatter.4.cloned.1.call-done = f32[128,2048]{1,0:T(8,128)} async-done(((f32[2048,2048]{1,0:T(8,128)}), f32[128,2048]{1,0:T(8,128)}) %reduce-scatter.4.cloned.1.call-update) | async-done | bytes 1048592 | tf_op jit(solution)/shard_map/reduce_scatter | solution.py:252
  1011.8 1.9 fusion.85
  1013.7 17.7 pad_maximum_fusion
  1031.4 7.1 fusion.10
  1038.9 5.5 fusion.80
  1044.4 1.1 convert_reduce_fusion.1
  1045.9 632.3 %reduce-scatter.8.cloned.1.call-done = f32[40,1024]{1,0:T(8,128)} async-done(((f32[5120,1024]{1,0:T(8,128)}), f32[40,1024]{1,0:T(8,128)}) %reduce-scatter.8.cloned.1.call-update) | async-done | bytes 163856 | tf_op jit(solution)/shard_map/reduce_scatter | solution.py:318
  1678.1 1.6 multiply_reduce_fusion.6
  1679.7 698.6 %reduce-scatter.6.cloned.1.call-done = f32[8,7168]{1,0:T(8,128)} async-done(((f32[1024,7168]{1,0:T(8,128)}), f32[8,7168]{1,0:T(8,128)}) %reduce-scatter.6.cloned.1.call-update) | async-done | bytes 229392 | tf_op jit(solution)/shard_map/reduce_scatter | solution.py:315
  2378.3 1.6 multiply_reduce_fusion.5
  2381.3 6.3 fusion.49
  2387.6 80.8 %all-reduce = (f32[]{:T(128)}, f32[13,1024]{0,1:T(8,128)S(1)}) all-reduce(f32[]{:T(128)S(6)} %add.258, f32[13,1024]{0,1:T(8,128)S(1)} %copy.128), channel_id=1, replica_groups=mesh['seq'=16,'dp'=8] {'seq','dp'}, use_global_device_ids=true, to_apply=%region_18.19 | all-reduce | flops 13313 | bytes 106504 | tf_op jit(solution)/shard_map/psum | solution.py:327
  2471.2 1.9 fusion.130
  2473.1 2.0 fusion.132
  (145 shorter events, 15.7 us)
Async XLA Ops:
  7.2 330.9 %all-gather.5.cloned.1.call-start = ((), (), s32[]{:S(2)}) async-start(), calls=%async_computation.3 | async-start | bytes 14794752 | tf_op jit(solution)/shard_map/all_gather | solution.py:129
  8.8 651.2 %all-gather.11.cloned.1.call-start = ((), (), s32[]{:S(2)}) async-start(), calls=%async_computation.6 | async-start | bytes 10567680 | tf_op jit(solution)/shard_map/all_gather | solution.py:130
  10.5 697.2 %all-gather.9.cloned.1.call-start = ((), (), s32[]{:S(2)}) async-start(), calls=%async_computation.5 | async-start | bytes 4456448 | tf_op jit(solution)/shard_map/all_gather | solution.py:157
  320.9 17.2 copy-start.21
  320.9 17.2 copy-start.23
  322.0 338.0 %copy-start.10 = (bf16[1,128,1024]{2,1,0:T(8,128)(2,1)S(1)}, bf16[1,128,1024]{2,1,0:T(8,128)(2,1)}, u32[]{:S(2)}) copy-start(bf16[1,128,1024]{2,1,0:T(8,128)(2,1)} %param.14) | copy-start | bytes 786436
  323.4 344.2 %copy-start.25 = (f32[128,8]{0,1:T(8,128)}, f32[128,8]{0,1:T(8,128)S(1)}, u32[]{:S(2)}) copy-start(f32[128,8]{0,1:T(8,128)S(1)} %get-tuple-element.108) | copy-start | bytes 12292
  323.4 344.2 %copy-start.27 = (f32[128,8]{0,1:T(8,128)}, f32[128,8]{0,1:T(8,128)S(1)}, u32[]{:S(2)}) copy-start(f32[128,8]{0,1:T(8,128)S(1)} %get-tuple-element.109) | copy-start | bytes 12292
  342.1 1.2 copy-start.11
  344.5 402.7 %all-gather.7.cloned.1.call-start = ((), (), s32[]{:S(2)}) async-start(), calls=%async_computation.4 | async-start | bytes 4456448 | tf_op jit(solution)/shard_map/all_gather | solution.py:158
  346.3 661.6 %reduce-scatter.4.cloned.1.call-start = ((), (), s32[]{:S(2)}) async-start(), calls=%async_computation.7 | async-start | bytes 17825792 | tf_op jit(solution)/shard_map/reduce_scatter | solution.py:252
  667.6 1.5 copy-start.9
  711.3 4.3 copy-start.4
  711.4 6.9 copy-start
  753.7 11.9 copy-start.5
  764.5 3.3 copy-start.7
  765.6 8.2 slice-start
  767.8 6.0 slice-start.1
  827.5 0.9 copy-start.6
  827.6 850.6 %reduce-scatter.8.cloned.1.call-start = ((), (), s32[]{:S(2)}) async-start(), calls=%async_computation.9 | async-start | bytes 21135360 | tf_op jit(solution)/shard_map/reduce_scatter | solution.py:318
  828.5 6.6 copy-start.8
  828.5 13.4 slice-start.2
  835.1 9.5 copy-start.14
  835.1 6.8 slice-start.3
  844.6 8.7 copy-start.12
  853.3 1525.0 %reduce-scatter.6.cloned.1.call-start = ((), (), s32[]{:S(2)}) async-start(), calls=%async_computation.8 | async-start | bytes 29589504 | tf_op jit(solution)/shard_map/reduce_scatter | solution.py:315
  853.6 8.2 copy-start.1
  853.6 8.2 copy-start.3
  861.8 2.2 copy-start.2
  864.0 145.3 %copy-start.26 = (f32[128,8]{0,1:T(8,128)S(1)}, f32[128,8]{0,1:T(8,128)}, u32[]{:S(2)}) copy-start(f32[128,8]{0,1:T(8,128)} %copy-done.25) | copy-start | bytes 12292
  864.0 145.3 %copy-start.28 = (f32[128,8]{0,1:T(8,128)S(1)}, f32[128,8]{0,1:T(8,128)}, u32[]{:S(2)}) copy-start(f32[128,8]{0,1:T(8,128)} %copy-done.27) | copy-start | bytes 12292
  864.0 147.7 %copy-start.22 = (f32[1024]{0:T(1024)S(1)}, f32[1024]{0:T(1024)}, u32[]{:S(2)}) copy-start(f32[1024]{0:T(1024)} %copy-done.21) | copy-start | bytes 12292
  864.0 147.7 %copy-start.24 = (f32[1024]{0:T(1024)S(1)}, f32[1024]{0:T(1024)}, u32[]{:S(2)}) copy-start(f32[1024]{0:T(1024)} %copy-done.23) | copy-start | bytes 12292
  1038.8 5.6 copy-start.20
  1038.8 1342.4 %copy-start.13 = (bf16[128,1024]{1,0:T(8,128)(2,1)S(1)}, bf16[128,1024]{1,0:T(8,128)(2,1)}, u32[]{:S(2)}) copy-start(bf16[128,1024]{1,0:T(8,128)(2,1)} %copy-done.12) | copy-start | bytes 786436
  1038.8 1342.4 %copy-start.15 = (bf16[128,4096]{1,0:T(8,128)(2,1)S(1)}, bf16[128,4096]{1,0:T(8,128)(2,1)}, u32[]{:S(2)}) copy-start(bf16[128,4096]{1,0:T(8,128)(2,1)} %copy-done.14) | copy-start | bytes 3145732
  1038.8 1342.4 %copy-start.32 = (f32[1024]{0:T(1024)S(1)}, f32[1024]{0:T(1024)}, u32[]{:S(2)}) copy-start(f32[1024]{0:T(1024)} %get-tuple-element.53) | copy-start | bytes 12292
  1038.9 1342.4 %copy-start.33 = (f32[1024]{0:T(1024)S(1)}, f32[1024]{0:T(1024)}, u32[]{:S(2)}) copy-start(f32[1024]{0:T(1024)} %get-tuple-element.54) | copy-start | bytes 12292
  2381.2 89.3 %copy-start.29 = (f32[13,8]{0,1:T(8,128)S(1)}, f32[13,8]{0,1:T(8,128)}, u32[]{:S(2)}) copy-start(f32[13,8]{0,1:T(8,128)} %param.17) | copy-start | bytes 1252
  2381.2 89.3 %copy-start.30 = (f32[13,8]{0,1:T(8,128)S(1)}, f32[13,8]{0,1:T(8,128)}, u32[]{:S(2)}) copy-start(f32[13,8]{0,1:T(8,128)} %param.22) | copy-start | bytes 1252
  2381.2 89.3 %copy-start.31 = (f32[13,8]{0,1:T(8,128)S(1)}, f32[13,8]{0,1:T(8,128)}, u32[]{:S(2)}) copy-start(f32[13,8]{0,1:T(8,128)} %param.23) | copy-start | bytes 1252
  2381.2 89.9 %copy-start.18 = (f32[40,1024]{1,0:T(8,128)S(1)}, f32[40,1024]{1,0:T(8,128)}, u32[]{:S(2)}) copy-start(f32[40,1024]{1,0:T(8,128)} %reduce-scatter.8.cloned.1.call-done) | copy-start | bytes 491524
  2381.3 89.9 %copy-start.19 = (f32[40,1024]{1,0:T(8,128)S(1)}, f32[40,1024]{1,0:T(8,128)}, u32[]{:S(2)}) copy-start(f32[40,1024]{1,0:T(8,128)} %param.16) | copy-start | bytes 491524
  2381.3 91.8 %copy-start.16 = (f32[8,7168]{1,0:T(8,128)S(1)}, f32[8,7168]{1,0:T(8,128)}, u32[]{:S(2)}) copy-start(f32[8,7168]{1,0:T(8,128)} %reduce-scatter.6.cloned.1.call-done) | copy-start | bytes 688132
  2381.3 91.8 %copy-start.17 = (f32[8,7168]{1,0:T(8,128)S(1)}, f32[8,7168]{1,0:T(8,128)}, u32[]{:S(2)}) copy-start(f32[8,7168]{1,0:T(8,128)} %param.15) | copy-start | bytes 688132
Sparse Core Ops, SparseCore 0:
  10.3 327.7 all-gather.4
  340.4 319.5 all-gather.10
  662.2 45.4 all-gather.8
  709.9 37.3 all-gather.6
  827.7 180.2 reduce-scatter.3
  1010.2 667.8 reduce-scatter.7
  1680.6 697.6 reduce-scatter.5
where the time goes:
time: 2490 us; the launch traced here: 2480 us
  waiting for transfers between devices  1860 us (75%)
  blocking collectives  386 us (16%)
  matrix products  105 us (4%)
  other arithmetic  64.8 us (3%)
  local copies, waits for them, and re-layouts  43.6 us (2%)
    reduce_scatter x1, waiting for transfers between devices, body(): lax.psum_scatter(jnp.concatenate([part_a, part_m], axis=1), ('seq', 'dp')...  699 us
    reduce_scatter x1, waiting for transfers between devices, body(): lax.psum_scatter(lax.dot_general(joined, cot_low, (((0,), (0,)), ((), ())...  632 us
    all_gather x1, waiting for transfers between devices, body(): lax.all_gather(out_low, ('seq', 'dp'), axis=0, tiled=True)  313 us
    all_gather x1, blocking collectives, body(): lax.all_gather(vec_low, ('seq', 'dp'), axis=1, tiled=True)  306 us
    reduce_scatter x1, waiting for transfers between devices, body(): lax.psum_scatter(jnp.concatenate([key_part.reshape(tok_rows * lax.axis_si...  142 us
    psum x1, blocking collectives, body(): lax.psum((local_squares, vec_local), ('seq', 'dp'))  80.8 us
  transfers between devices with their start and end apart: 7, of which 7 were waited for; matrix products, arithmetic and copies ran while one was open for 4% of the time, Pallas kernels for 0%

commit v1 on v0

v1 whole, which is shorter than its diff:
```python
import functools
import math

import jax
import jax.numpy as jnp
import numpy as np
from jax import lax
from jax.experimental import pallas as pl
from jax.experimental.pallas import tpu as pltpu
from jax.sharding import PartitionSpec as P

D = 1024
FF = 4096
HEADS = 16
HEAD = 64
ROT = 16
STEP = 5
SEQ = 16
DP = 8
TOK = 128
ROW = 2048
SPAN = 64

NORM_EPS = 1e-05
NEG_FILL = -1e30
CLIP_NORM = 1.0
RATE_MATRIX = 0.02
RATE_VECTOR = 0.2
BETA_ONE = 0.5
BETA_TWO = 0.5
DECAY_RATE = 0.1
ADAM_EPS = 1e-08
THETA_BASE = 10000.0

F32 = jnp.float32
BF16 = jnp.bfloat16
MESH = pl.DeviceIdType.MESH
VMEM_LIMIT = 60 * 1024 * 1024


def head_of(s):
    if s < 4:
        return 5 * s
    return 5 * ((s - 4) // 4) + 1 + (s - 4) % 4


def hidden_pieces(s):
    if s < 3:
        return [20 * s + 5 * r + 8 for r in range(4)]
    if s == 3:
        return [0, 1, 2, 3]
    return [5 * s - 16 + r for r in range(4)]


def column_pieces():
    rows = []
    for s in range(SEQ):
        h = head_of(s)
        rows.append([h, 16 + h, 32 + h] + [48 + w for w in hidden_pieces(s)])
    return np.array(rows, np.int32)


PIECES = column_pieces()


def head_index(s):
    return jnp.where(s < 4, 5 * s, 5 * ((s - 4) // 4) + 1 + (s - 4) % 4)


def hidden_index(s, r):
    return jnp.where(s < 3, 20 * s + 5 * r + 8, jnp.where(s == 3, r, 5 * s - 16 + r))


def remote(src, dst, send, recv, **where):
    return pltpu.make_async_remote_copy(
        src_ref=src, dst_ref=dst, send_sem=send, recv_sem=recv, device_id=where, device_id_type=MESH
    )


def enter(me, dm):
    barrier = pltpu.get_barrier_semaphore()

    @pl.loop(1, SEQ)
    def _(k):
        pl.semaphore_signal(
            barrier, inc=1, device_id={"seq": lax.rem(me + k, SEQ)}, device_id_type=MESH
        )

    @pl.loop(1, DP)
    def _(k):
        pl.semaphore_signal(
            barrier, inc=1, device_id={"dp": lax.rem(dm + k, DP)}, device_id_type=MESH
        )

    pl.semaphore_wait(barrier, SEQ + DP - 2)


def gather_kernel(
    xh_ref,
    cot_ref,
    win_ref,
    wout_ref,
    xh_all,
    cot_all,
    win_all,
    wout_all,
    swap_all,
    local_sem,
    a_send,
    a_recv,
    l_send,
    l_recv,
    o_send,
    o_recv,
    x_send,
    x_recv,
    f_send,
    c_send,
    c_recv,
    g_send,
    w_send,
    w_recv,
):
    me = lax.axis_index("seq")
    dm = lax.axis_index("dp")
    sib = me + 1 - 2 * lax.rem(me, 2)
    own = [
        pltpu.make_async_copy(win_ref.at[me], win_all.at[dm, me], local_sem.at[0]),
        pltpu.make_async_copy(xh_ref, xh_all.at[me], local_sem.at[1]),
        pltpu.make_async_copy(wout_ref, wout_all.at[pl.ds(dm * 5, 5)], local_sem.at[2]),
        pltpu.make_async_copy(cot_ref, cot_all.at[me], local_sem.at[3]),
    ]
    for c in own:
        c.start()
    enter(me, dm)

    def a_copy(k):
        to = lax.rem(me + k, SEQ)
        return remote(win_ref.at[to], win_all.at[dm, me], a_send.at[k], a_recv.at[me], seq=to)

    def a_wait(k):
        frm = lax.rem(me + k, SEQ)
        return remote(win_ref.at[0], win_all.at[dm, frm], a_send.at[k], a_recv.at[frm], seq=frm)

    def l_copy(k, frm):
        to = lax.rem(dm + k, DP)
        return remote(win_all.at[frm], win_all.at[frm], l_send.at[k], l_recv.at[frm], dp=to)

    def o_copy(k, frm):
        to = lax.rem(dm + k, DP)
        return remote(
            wout_ref, wout_all.at[pl.ds(frm * 5, 5)], o_send.at[k], o_recv.at[frm], dp=to
        )

    def row_sends(src, dst, send, recv):
        remote(src, dst.at[me], send.at[0], recv.at[me], seq=sib).start()

        @pl.loop(1, 8)
        def _(j):
            to = lax.rem(me + 2 * j, SEQ)
            remote(src, dst.at[me], send.at[j], recv.at[me], seq=to).start()

    def row_forwards(src, dst, recv, fsend):
        @pl.loop(1, 8)
        def _(j):
            frm = lax.rem(me + 2 * j, SEQ)
            remote(src, dst.at[frm], fsend.at[j], recv.at[frm], seq=sib).wait_recv()
            remote(dst.at[frm], dst.at[frm], fsend.at[j], recv.at[frm], seq=sib).start()

    def row_finish(src, dst, send, recv, fsend):
        @pl.loop(0, 8)
        def _(j):
            frm = lax.rem(sib + 2 * j, SEQ)
            remote(src, dst.at[frm], send.at[j], recv.at[frm], seq=sib).wait_recv()
            remote(src, dst.at[me], send.at[j], recv.at[me], seq=sib).wait_send()

        @pl.loop(1, 8)
        def _(j):
            frm = lax.rem(me + 2 * j, SEQ)
            remote(dst.at[frm], dst.at[frm], fsend.at[j], recv.at[frm], seq=sib).wait_send()

    @pl.loop(1, SEQ)
    def _(k):
        a_copy(k).start()

    row_sends(xh_ref, xh_all, x_send, x_recv)

    @pl.loop(1, DP)
    def _(k):
        o_copy(k, dm).start()

    own[0].wait()

    @pl.loop(1, SEQ)
    def _(k):
        a_wait(k).wait_recv()

    @pl.loop(1, DP)
    def _(k):
        l_copy(k, dm).start()

    row_sends(cot_ref, cot_all, c_send, c_recv)
    row_forwards(xh_ref, xh_all, x_recv, f_send)

    own[2].wait()

    @pl.loop(1, DP)
    def _(k):
        o_copy(k, lax.rem(dm + k, DP)).wait_recv()

    def swap_few(r):
        return remote(
            wout_all.at[pl.ds(8 + 8 * r, 8)],
            swap_all.at[0],
            w_send.at[r],
            w_recv.at[0],
            seq=4 + 4 * me + r,
        )

    def swap_many():
        return remote(
            wout_all.at[pl.ds(32, 8)],
            swap_all.at[lax.rem(me, 4)],
            w_send.at[0],
            w_recv.at[lax.rem(me, 4)],
            seq=(me - 4) // 4,
        )

    @pl.when(me < 3)
    def _():
        for r in range(4):
            swap_few(r).start()

    @pl.when(me > 3)
    def _():
        swap_many().start()

    row_forwards(cot_ref, cot_all, c_recv, g_send)
    row_finish(xh_ref, xh_all, x_send, x_recv, f_send)
    row_finish(cot_ref, cot_all, c_send, c_recv, g_send)

    @pl.when(me < 3)
    def _():
        for r in range(4):
            remote(
                wout_all.at[pl.ds(32, 8)], swap_all.at[r], w_send.at[r], w_recv.at[r], seq=me
            ).wait_recv()
            swap_few(r).wait_send()

    @pl.when(me > 3)
    def _():
        swap_many().wait_send()
        remote(
            wout_all.at[pl.ds(32, 8)], swap_all.at[0], w_send.at[0], w_recv.at[0], seq=me
        ).wait_recv()

    @pl.loop(1, DP)
    def _(k):
        l_copy(k, lax.rem(dm + k, DP)).wait_recv()
        l_copy(k, dm).wait_send()
        o_copy(k, dm).wait_send()

    @pl.loop(1, SEQ)
    def _(k):
        a_copy(k).wait_send()

    own[1].wait()
    own[3].wait()


def gather_call(xh, cot, win, wout):
    any_spec = pl.BlockSpec(memory_space=pl.ANY)
    dma = pltpu.SemaphoreType.DMA
    return pl.pallas_call(
        gather_kernel,
        out_shape=(
            jax.ShapeDtypeStruct((SEQ, TOK, D), BF16),
            jax.ShapeDtypeStruct((SEQ, TOK, D), BF16),
            jax.ShapeDtypeStruct((DP, SEQ, 16, 256), BF16),
            jax.ShapeDtypeStruct((40, 16, 512), BF16),
            jax.ShapeDtypeStruct((4, 8, 16, 512), BF16),
        ),
        in_specs=[any_spec] * 4,
        out_specs=[any_spec] * 5,
        scratch_shapes=[
            dma((4,)),
            dma((SEQ,)),
            dma((SEQ,)),
            dma((DP,)),
            dma((DP,)),
            dma((DP,)),
            dma((DP,)),
            dma((8,)),
            dma((SEQ,)),
            dma((8,)),
            dma((8,)),
            dma((SEQ,)),
            dma((8,)),
            dma((4,)),
            dma((4,)),
        ],
        compiler_params=pltpu.CompilerParams(collective_id=0, has_side_effects=True),
        name="gather_rows_weights",
    )(xh, cot, win, wout)


def dot(a, b):
    return jnp.dot(a, b, preferred_element_type=F32)


def dot_nt(a, b):
    return lax.dot_general(a, b, (((1,), (1,)), ((), ())), preferred_element_type=F32)


def lane_iota(shape):
    return lax.broadcasted_iota(jnp.int32, shape, len(shape) - 1)


CH = 512
NCH = ROW // CH


def core_kernel(
    span_ref,
    inv_ref,
    len_ref,
    xh_ref,
    cot_ref,
    win_ref,
    wout_ref,
    swap_ref,
    cos_ref,
    sin_ref,
    po_ref,
    hg_ref,
    gin_ref,
    goa_ref,
    gof_ref,
    vec_ref,
    xs,
    cs,
    wqr,
    wfr,
    wqp,
    wfp,
    woa,
    wof,
    qt,
    qn,
    kt,
    kn,
    vt,
    vn,
    dot_t,
    dot_n,
    ot,
    lse,
    delta,
    act,
    act_t,
    dact,
    mixf,
    mixf_t,
    mixq,
    mixq_t,
    att,
    att_t,
    dqt,
    dkn,
    dvn,
    vg,
):
    me = lax.axis_index("seq")
    head = head_index(me)

    def unpack(sb, carry):
        cq, cf = carry
        tiles = [win_ref[d, sb].astype(F32) for d in range(DP)]
        ff = jnp.concatenate([t[:8] for t in tiles], axis=0)
        qk = jnp.concatenate([t[8:] for t in tiles], axis=0)
        rows = pl.ds(pl.multiple_of(sb * 64, 64), 64)
        gain_a, bias_a, gain_m, bias_m = (qk[:, 192 + i : 193 + i] for i in range(4))
        wfr[rows] = ff.astype(BF16)
        wqr[rows] = qk.astype(BF16)
        wfp[rows] = (ff * gain_m).astype(BF16)
        wqp[rows] = jnp.where(lane_iota(qk.shape) < 192, qk * gain_a, 0.0).astype(BF16)
        return (
            cq + jnp.sum(qk * bias_a, axis=0, keepdims=True),
            cf + jnp.sum(ff * bias_m, axis=0, keepdims=True),
        )

    zero_row = jnp.zeros((1, 256), F32)
    cq, cf = lax.fori_loop(0, SEQ, unpack, (zero_row, zero_row))

    slab = jnp.transpose(wqr[:, 128:256].astype(F32))
    vec_ref[...] = slab[64:80]

    hid = []
    for r in range(4):
        w = hidden_index(me, r)
        rows = pl.ds(pl.multiple_of(lax.rem(w, 16) * 64, 64), 64)
        part = wqr[rows, 128:256].astype(F32)
        lane = 64 + 9 + w // 16
        hid.append(jnp.sum(jnp.where(lane_iota(part.shape) == lane, part, 0.0), axis=1, keepdims=True))
    hid = jnp.concatenate(hid, axis=0)
    cf = cf + jnp.transpose(jnp.broadcast_to(hid, (256, 128)))[0:1]

    head_rows = pl.ds(pl.multiple_of(head * 64, 64), 64)
    head_vecs = wqr[head_rows, 128:256].astype(F32)
    bq, bk, bv = (head_vecs[:, 68 + i : 69 + i] for i in range(3))

    def unit(ref, index, dst, at):
        u = ref[index].astype(F32)
        return jnp.concatenate([u[:8], u[8:]], axis=1)

    def put_units(src, base, dst, count):
        @pl.loop(0, count // 2)
        def _(i):
            pair = [src[base + 2 * i + j].astype(F32) for j in range(2)]
            pair = [jnp.concatenate([u[:8], u[8:]], axis=1) for u in pair]
            dst[pl.ds(pl.multiple_of(i * 16, 16), 16)] = jnp.concatenate(pair, axis=0).astype(BF16)

    def put_swap(dst, rs):
        for r in range(rs):
            for i in range(4):
                pair = [swap_ref[r, 2 * i + j].astype(F32) for j in range(2)]
                pair = [jnp.concatenate([u[:8], u[8:]], axis=1) for u in pair]
                dst[r * 64 + i * 16 : r * 64 + i * 16 + 16] = jnp.concatenate(pair, axis=0).astype(
                    BF16
                )

    @pl.when(me < 4)
    def _():
        put_units(wout_ref, 0, woa, 8)

    @pl.when(me < 3)
    def _():
        put_swap(wof, 4)

    @pl.when(me == 3)
    def _():
        put_units(wout_ref, 8, wof, 32)

    @pl.when(me > 3)
    def _():
        put_swap(woa, 1)
        put_units(wout_ref, 0, wof, 32)

    @pl.loop(0, 32)
    def _(i):
        rows = pl.ds(pl.multiple_of(i * 64, 64), 64)
        xs[rows] = xh_ref[inv_ref[i]]
        cs[rows] = cot_ref[inv_ref[i]]

    aug = jnp.where(lax.broadcasted_iota(jnp.int32, (64, CH), 0) == 0, 1.0, 0.0)
    zeros_aug = jnp.zeros((64, CH), F32)

    def rotate_t(u, cosine, sine, sign):
        first, second = u[0:8], u[8:16]
        return jnp.concatenate(
            [
                first * cosine - sign * (second * sine),
                second * cosine + sign * (first * sine),
                u[16:],
            ],
            axis=0,
        )

    @pl.loop(0, NCH)
    def _(i):
        start = pl.multiple_of(i * CH, CH)
        rows = pl.ds(start, CH)
        xh = xs[rows]
        qkv = jnp.transpose(dot(xh, wqp[...]) + cq)
        cosine, sine = cos_ref[:, rows], sin_ref[:, rows]
        q = rotate_t(qkv[0:64] + bq, cosine, sine, 1.0) * 0.125
        k = rotate_t(qkv[64:128] + bk, cosine, sine, 1.0)
        v = qkv[128:192] + bv
        q_full = jnp.concatenate([q, aug], axis=0)
        past = (start + lane_iota((64, CH))) >= len_ref[0]
        k_full = jnp.concatenate([k, jnp.where(past, NEG_FILL, 0.0) * aug], axis=0)
        v_full = jnp.concatenate([v, zeros_aug], axis=0)
        qt[:, rows] = q_full.astype(BF16)
        kt[:, rows] = k.astype(BF16)
        vt[:, rows] = v.astype(BF16)
        qn[rows] = jnp.transpose(q_full).astype(BF16)
        kn[rows] = jnp.transpose(k_full).astype(BF16)
        vn[rows] = jnp.transpose(v_full).astype(BF16)
        pre = dot(xh, wfp[...]) + cf
        cdf = 0.5 * (1.0 + lax.erf(pre * (1.0 / math.sqrt(2.0))))
        pdf = jnp.exp(-0.5 * pre * pre) * (1.0 / math.sqrt(2.0 * math.pi))
        activ = pre * cdf
        act[rows] = activ.astype(BF16)
        act_t[:, rows] = jnp.transpose(activ).astype(BF16)
        dact[rows] = cdf + pre * pdf

    causal = lax.broadcasted_iota(jnp.int32, (CH, CH), 0) <= lane_iota((CH, CH))

    def scores(kc, qi):
        s = dot(kn[kc * CH : (kc + 1) * CH], qt[:, qi * CH : (qi + 1) * CH])
        if kc == qi:
            s = jnp.where(causal, s, NEG_FILL)
        return s

    for qi in range(NCH):
        lanes = slice(qi * CH, (qi + 1) * CH)
        parts = [scores(kc, qi) for kc in range(qi + 1)]
        top = functools.reduce(jnp.maximum, [jnp.max(s, axis=0, keepdims=True) for s in parts])
        total = jnp.zeros((1, CH), F32)
        out = jnp.zeros((64, CH), F32)
        for kc, s in enumerate(parts):
            p = jnp.exp(s - top)
            total = total + jnp.sum(p, axis=0, keepdims=True)
            out = out + dot(vt[:, kc * CH : (kc + 1) * CH], p.astype(BF16))
        out = out / total
        ot[:, lanes] = out
        lse[:, lanes] = jnp.broadcast_to(top + jnp.log(total), (8, CH))
        att_t[:, lanes] = out.astype(BF16)
        att[lanes] = jnp.transpose(out).astype(BF16)

    @pl.loop(0, NCH)
    def _(i):
        rows = pl.ds(pl.multiple_of(i * CH, CH), CH)
        cot = cs[rows]
        ag = dot_nt(cot, woa[...]).astype(BF16).astype(F32)
        ag_t = jnp.transpose(ag)
        dot_n[rows] = ag.astype(BF16)
        dot_t[:, rows] = ag_t.astype(BF16)
        delta[:, rows] = jnp.broadcast_to(jnp.sum(ag_t * ot[:, rows], axis=0, keepdims=True), (8, CH))
        pg = dot_nt(cot, wof[...]) * dact[rows]
        mixf[rows] = pg.astype(BF16)
        mixf_t[:, rows] = jnp.transpose(pg).astype(BF16)

    for qi in range(NCH):
        lanes = slice(qi * CH, (qi + 1) * CH)
        dq = jnp.zeros((64, CH), F32)
        for kc in range(qi + 1):
            keys = slice(kc * CH, (kc + 1) * CH)
            p = jnp.exp(scores(kc, qi) - lse[0:1, lanes])
            dp = dot(vn[keys, 0:64], dot_t[:, lanes])
            ds = (p * (dp - delta[0:1, lanes])).astype(BF16)
            dv = dot(p.astype(BF16), dot_n[lanes])
            dk = dot(ds, qn[lanes, 0:64])
            dq = dq + dot(kt[:, keys], ds)
            if kc == qi:
                dvn[keys] = dv
                dkn[keys] = dk
            else:
                dvn[keys] += dv
                dkn[keys] += dk
        dqt[:, lanes] = dq * 0.125

    @pl.loop(0, NCH)
    def _(i):
        rows = pl.ds(pl.multiple_of(i * CH, CH), CH)
        cosine, sine = cos_ref[:, rows], sin_ref[:, rows]
        dq = rotate_t(dqt[:, rows], cosine, sine, -1.0)
        dk = rotate_t(jnp.transpose(dkn[rows]), cosine, sine, -1.0)
        dv = jnp.transpose(dvn[rows])
        full = jnp.concatenate([dq, dk, dv, zeros_aug], axis=0)
        mixq_t[:, rows] = full.astype(BF16)
        mixq[rows] = jnp.transpose(full).astype(BF16)

    @pl.loop(0, SEQ)
    def _(s):
        def both(ref):
            return jnp.concatenate(
                [
                    ref[pl.ds(pl.multiple_of(span_ref[2 * s + j] * SPAN, SPAN), SPAN)]
                    for j in range(2)
                ],
                axis=0,
            )

        po_ref[s] = (dot(both(att), woa[...]) + dot(both(act), wof[...])).astype(BF16)
        hg_ref[s] = (dot_nt(both(mixq), wqp[...]) + dot_nt(both(mixf), wfp[...])).astype(BF16)

    goa = dot(att_t[...], cs[...]).reshape(8, 8, D)
    goa_ref[...] = jnp.concatenate([goa[:, :, :512], goa[:, :, 512:]], axis=1).astype(BF16)

    @pl.loop(0, 4)
    def _(i):
        rows = pl.ds(pl.multiple_of(i * 64, 64), 64)
        gof = dot(act_t[rows], cs[...]).reshape(8, 8, D)
        gof_ref[pl.ds(i * 8, 8)] = jnp.concatenate(
            [gof[:, :, :512], gof[:, :, 512:]], axis=1
        ).astype(BF16)

    sums_q = jnp.sum(mixq[...].astype(F32), axis=0, keepdims=True)
    sums_f = jnp.sum(mixf[...].astype(F32), axis=0, keepdims=True)
    cols_q = jnp.sum(mixq_t[...].astype(F32), axis=1, keepdims=True)
    cols_f = jnp.sum(mixf_t[...].astype(F32), axis=1, keepdims=True)
    cot_own = jnp.sum(cot_ref[2 * me].astype(F32), axis=0, keepdims=True) + jnp.sum(
        cot_ref[2 * me + 1].astype(F32), axis=0, keepdims=True
    )
    cot_cols = jnp.transpose(jnp.broadcast_to(cot_own, (128, D)))
    lanes_d = lane_iota((D, 128))
    vg[...] = jnp.where((lanes_d == 71) | (lanes_d == 72), cot_cols, 0.0)
    lanes_h = lane_iota((64, 128))
    for i in range(3):
        vg[head_rows] += jnp.where(lanes_h == 68 + i, cols_q[64 * i : 64 * i + 64], 0.0)
    for r in range(4):
        w = hidden_index(me, r)
        rows = pl.ds(pl.multiple_of(lax.rem(w, 16) * 64, 64), 64)
        vg[rows] += jnp.where(lanes_h == 64 + 9 + w // 16, cols_f[64 * r : 64 * r + 64], 0.0)

    @pl.loop(0, 4)
    def _(i):
        rows = pl.ds(pl.multiple_of(i * 256, 256), 256)
        hq = jnp.transpose(dot(mixq_t[...], xs[:, rows]))
        hf = jnp.transpose(dot(mixf_t[...], xs[:, rows]))
        raw_q = wqr[rows].astype(F32)
        raw_f = wfr[rows].astype(F32)
        gain_a, bias_a, gain_m, bias_m = (raw_q[:, 192 + j : 193 + j] for j in range(4))
        gq = gain_a * hq + bias_a * sums_q
        gf = gain_m * hf + bias_m * sums_f
        extra = vg[rows]
        lanes = lane_iota((256, 128))
        for j, col in enumerate((raw_q * hq, raw_q * sums_q, raw_f * hf, raw_f * sums_f)):
            extra = extra + jnp.where(lanes == 64 + j, jnp.sum(col, axis=1, keepdims=True), 0.0)
        gq = jnp.concatenate([gq[:, :128], gq[:, 128:] + extra], axis=1)
        for j in range(4):
            part_f = gf[64 * j : 64 * j + 64].reshape(8, 8, 256)
            part_q = gq[64 * j : 64 * j + 64].reshape(8, 8, 256)
            gin_ref[:, 4 * i + j] = jnp.concatenate([part_f, part_q], axis=1).astype(BF16)


def core_call(span, inv, length, xh, cot, win, wout, swap):
    half = ROT // 2
    freqs = THETA_BASE ** (-2.0 * np.arange(half, dtype=np.float32) / ROT)
    angles = jnp.arange(ROW, dtype=F32)[None, :] * jnp.asarray(freqs, F32)[:, None]
    smem = pl.BlockSpec(memory_space=pltpu.SMEM)
    vmem = pl.BlockSpec(memory_space=pltpu.VMEM)
    sds = jax.ShapeDtypeStruct

    def buf(shape, dtype=BF16):
        return pltpu.VMEM(shape, dtype)

    return pl.pallas_call(
        core_kernel,
        out_shape=(
            sds((SEQ, TOK, D), BF16),
            sds((SEQ, TOK, D), BF16),
            sds((DP, SEQ, 16, 256), BF16),
            sds((8, 16, 512), BF16),
            sds((32, 16, 512), BF16),
            sds((16, D), F32),
        ),
        in_specs=[smem] * 3 + [vmem] * 7,
        out_specs=[vmem] * 6,
        scratch_shapes=[
            buf((ROW, D)),
            buf((ROW, D)),
            buf((D, 256)),
            buf((D, 256)),
            buf((D, 256)),
            buf((D, 256)),
            buf((64, D)),
            buf((256, D)),
            buf((128, ROW)),
            buf((ROW, 128)),
            buf((64, ROW)),
            buf((ROW, 128)),
            buf((64, ROW)),
            buf((ROW, 128)),
            buf((64, ROW)),
            buf((ROW, 64)),
            buf((64, ROW), F32),
            buf((8, ROW), F32),
            buf((8, ROW), F32),
            buf((ROW, 256)),
            buf((256, ROW)),
            buf((ROW, 256), F32),
            buf((ROW, 256)),
            buf((256, ROW)),
            buf((ROW, 256)),
            buf((256, ROW)),
            buf((ROW, 64)),
            buf((64, ROW)),
            buf((64, ROW), F32),
            buf((ROW, 64), F32),
            buf((ROW, 64), F32),
            buf((D, 128), F32),
        ],
        compiler_params=pltpu.CompilerParams(vmem_limit_bytes=VMEM_LIMIT),
        name="layer_of_one_row",
    )(
        span,
        inv,
        length,
        xh.reshape(32, 64, D),
        cot.reshape(32, 64, D),
        win,
        wout,
        swap,
        jnp.cos(angles),
        jnp.sin(angles),
    )


def scatter_kernel(
    po_ref,
    hg_ref,
    gin_ref,
    goa_ref,
    gof_ref,
    out_sum,
    grad_sum,
    win_sum,
    wout_sum,
    square_ref,
    po_sib,
    hg_sib,
    po_pair,
    hg_pair,
    po_got,
    hg_got,
    gin_got,
    own_out,
    out_got,
    win_part,
    tile_a,
    tile_b,
    got_a,
    got_b,
    local_sem,
    ps_send,
    ps_recv,
    pg_send,
    pg_recv,
    hs_send,
    hs_recv,
    hgs_send,
    hgs_recv,
    g_send,
    g_recv,
    w_send,
    w_recv,
    o_send,
    o_recv,
    a_send,
    a_recv,
    ta_send,
    ta_recv,
    tb_send,
    tb_recv,
):
    me = lax.axis_index("seq")
    dm = lax.axis_index("dp")
    core = lax.rem(me, 2)
    chip = me // 2
    sib = me + 1 - 2 * core
    enter(me, dm)

    def g_copy(k, to, frm):
        return remote(gin_ref.at[to], gin_got.at[frm], g_send.at[k], g_recv.at[frm], dp=to)

    @pl.loop(1, DP)
    def _(k):
        g_copy(k, lax.rem(dm + k, DP), dm).start()

    def swap_few(r):
        return remote(
            gof_ref.at[pl.ds(8 * r, 8)],
            own_out.at[pl.ds(32, 8)],
            w_send.at[r],
            w_recv.at[0],
            seq=4 + 4 * me + r,
        )

    def swap_many():
        return remote(
            goa_ref,
            own_out.at[pl.ds(8 + 8 * lax.rem(me, 4), 8)],
            w_send.at[0],
            w_recv.at[lax.rem(me, 4)],
            seq=(me - 4) // 4,
        )

    keep_a = pltpu.make_async_copy(goa_ref, own_out.at[pl.ds(0, 8)], local_sem.at[0])
    keep_f3 = pltpu.make_async_copy(gof_ref, own_out.at[pl.ds(8, 32)], local_sem.at[1])
    keep_f = pltpu.make_async_copy(gof_ref, own_out.at[pl.ds(0, 32)], local_sem.at[1])

    @pl.when(me < 3)
    def _():
        for r in range(4):
            swap_few(r).start()

    @pl.when(me < 4)
    def _():
        keep_a.start()

    @pl.when(me == 3)
    def _():
        keep_f3.start()

    @pl.when(me > 3)
    def _():
        swap_many().start()
        keep_f.start()

    def sib_copy(src, dst, send, recv, j):
        return remote(src.at[2 * j + 1 - core], dst.at[j], send.at[j], recv.at[j], seq=sib)

    def chip_copy(src, dst, send, recv, j, frm):
        return remote(src.at[j], dst.at[frm], send.at[j], recv.at[frm], seq=2 * j + core)

    for src, dst, send, recv in (
        (po_ref, po_sib, ps_send, ps_recv),
        (hg_ref, hg_sib, hs_send, hs_recv),
    ):

        @pl.loop(0, 8)
        def _(k, src=src, dst=dst, send=send, recv=recv):
            sib_copy(src, dst, send, recv, lax.rem(chip + 1 + k, 8)).start()

    sets = (
        (po_ref, po_sib, po_pair, po_got, ps_send, ps_recv, pg_send, pg_recv, out_sum),
        (hg_ref, hg_sib, hg_pair, hg_got, hs_send, hs_recv, hgs_send, hgs_recv, grad_sum),
    )
    for src, dst, pair, got, send, recv, send2, recv2, total in sets:

        @pl.loop(0, 8)
        def _(k, src=src, dst=dst, pair=pair, got=got, send=send, recv=recv, send2=send2, recv2=recv2):
            j = lax.rem(chip + 1 + k, 8)
            sib_copy(src, dst, send, recv, j).wait_recv()
            pair[j] = (src[2 * j + core].astype(F32) + dst[j].astype(F32)).astype(BF16)

            @pl.when(j != chip)
            def _():
                chip_copy(pair, got, send2, recv2, j, chip).start()

    @pl.loop(1, DP)
    def _(k):
        g_copy(k, dm, lax.rem(dm + k, DP)).wait_recv()

    @pl.loop(0, SEQ)
    def _(s):
        total = gin_ref[dm, s].astype(F32)
        for k in range(1, DP):
            total = total + gin_got[lax.rem(dm + k, DP), s].astype(F32)
        win_part[s] = total

    def a_copy(k, to, frm):
        return remote(win_part.at[to], win_sum.at[frm], a_send.at[k], a_recv.at[frm], seq=to)

    @pl.loop(1, SEQ)
    def _(k):
        a_copy(k, lax.rem(me + k, SEQ), me).start()

    win_sum[me] = win_part[me]

    @pl.when(me < 3)
    def _():
        for r in range(4):
            swap_few(r).wait_send()
            remote(
                goa_ref, own_out.at[pl.ds(8 + 8 * r, 8)], w_send.at[r], w_recv.at[r], seq=me
            ).wait_recv()

    @pl.when(me < 4)
    def _():
        keep_a.wait()

    @pl.when(me == 3)
    def _():
        keep_f3.wait()

    @pl.when(me > 3)
    def _():
        swap_many().wait_send()
        keep_f.wait()
        remote(
            goa_ref, own_out.at[pl.ds(32, 8)], w_send.at[0], w_recv.at[0], seq=me
        ).wait_recv()

    def o_copy(k, to, frm):
        return remote(
            own_out.at[pl.ds(5 * to, 5)], out_got.at[frm], o_send.at[k], o_recv.at[frm], dp=to
        )

    @pl.loop(1, DP)
    def _(k):
        o_copy(k, lax.rem(dm + k, DP), dm).start()

    @pl.loop(1, DP)
    def _(k):
        o_copy(k, dm, lax.rem(dm + k, DP)).wait_recv()

    total = own_out[pl.ds(5 * dm, 5)].astype(F32)
    for k in range(1, DP):
        total = total + out_got[lax.rem(dm + k, DP)].astype(F32)
    wout_sum[...] = total
    squares = jnp.sum(total * total, axis=0)
    squares = jnp.sum(squares, axis=0, keepdims=True)

    @pl.loop(1, SEQ)
    def _(k):
        a_copy(k, me, lax.rem(me + k, SEQ)).wait_recv()

    all_in = win_sum[...]
    weights = jnp.where(
        (lax.broadcasted_iota(jnp.int32, all_in.shape, 1) < 8) | (lane_iota(all_in.shape) < 192),
        all_in,
        0.0,
    )
    in_squares = jnp.sum(jnp.sum(weights * weights, axis=0), axis=0, keepdims=True)
    vec_total = jnp.sum(all_in, axis=0)[8:, 128:]
    vec_total = jnp.where(lane_iota(vec_total.shape) >= 64, vec_total, 0.0)
    vec_squares = jnp.sum(vec_total * vec_total, axis=0, keepdims=True)
    row = (
        in_squares[:, :128]
        + in_squares[:, 128:]
        + vec_squares
        + squares[:, :128]
        + squares[:, 128:256]
        + squares[:, 256:384]
        + squares[:, 384:]
    )
    tile_a[...] = jnp.broadcast_to(row, (8, 128))

    def ta_copy(k, to, frm):
        return remote(tile_a, got_a.at[frm], ta_send.at[k], ta_recv.at[frm], seq=to)

    def tb_copy(k, to, frm):
        return remote(tile_b, got_b.at[frm], tb_send.at[k], tb_recv.at[frm], dp=to)

    @pl.loop(1, SEQ)
    def _(k):
        ta_copy(k, lax.rem(me + k, SEQ), me).start()

    got_a[me] = tile_a[...]

    @pl.loop(1, SEQ)
    def _(k):
        ta_copy(k, me, lax.rem(me + k, SEQ)).wait_recv()

    tile_b[...] = jnp.sum(got_a[...], axis=0)

    @pl.loop(1, DP)
    def _(k):
        tb_copy(k, lax.rem(dm + k, DP), dm).start()

    got_b[dm] = tile_b[...]

    @pl.loop(1, DP)
    def _(k):
        tb_copy(k, dm, lax.rem(dm + k, DP)).wait_recv()

    everything = jnp.sum(got_b[...], axis=0)
    square_ref[...] = jnp.broadcast_to(jnp.sum(everything, axis=1, keepdims=True), (8, 128))

    for src, dst, pair, got, send, recv, send2, recv2, total in sets:

        @pl.loop(1, 8)
        def _(k, pair=pair, got=got, send2=send2, recv2=recv2):
            frm = lax.rem(chip + k, 8)
            chip_copy(pair, got, send2, recv2, chip, frm).wait_recv()

        value = pair[chip].astype(F32)
        for k in range(1, 8):
            value = value + got[lax.rem(chip + k, 8)].astype(F32)
        total[...] = value

        @pl.loop(0, 8)
        def _(k, src=src, dst=dst, pair=pair, got=got, send=send, recv=recv, send2=send2, recv2=recv2):
            j = lax.rem(chip + 1 + k, 8)
            sib_copy(src, dst, send, recv, j).wait_send()

            @pl.when(j != chip)
            def _():
                chip_copy(pair, got, send2, recv2, j, chip).wait_send()

    @pl.loop(1, DP)
    def _(k):
        g_copy(k, lax.rem(dm + k, DP), dm).wait_send()
        o_copy(k, lax.rem(dm + k, DP), dm).wait_send()
        tb_copy(k, lax.rem(dm + k, DP), dm).wait_send()

    @pl.loop(1, SEQ)
    def _(k):
        a_copy(k, lax.rem(me + k, SEQ), me).wait_send()
        ta_copy(k, lax.rem(me + k, SEQ), me).wait_send()


def scatter_call(po, hg, gin, goa, gof):
    vmem = pl.BlockSpec(memory_space=pltpu.VMEM)
    sds = jax.ShapeDtypeStruct
    dma = pltpu.SemaphoreType.DMA
    buf = pltpu.VMEM
    return pl.pallas_call(
        scatter_kernel,
        out_shape=(
            sds((TOK, D), F32),
            sds((TOK, D), F32),
            sds((SEQ, 16, 256), F32),
            sds((5, 16, 512), F32),
            sds((8, 128), F32),
        ),
        in_specs=[vmem] * 5,
        out_specs=[vmem] * 5,
        scratch_shapes=[
            buf((8, TOK, D), BF16),
            buf((8, TOK, D), BF16),
            buf((8, TOK, D), BF16),
            buf((8, TOK, D), BF16),
            buf((8, TOK, D), BF16),
            buf((8, TOK, D), BF16),
            buf((DP, SEQ, 16, 256), BF16),
            buf((40, 16, 512), BF16),
            buf((DP, 5, 16, 512), BF16),
            buf((SEQ, 16, 256), F32),
            buf((8, 128), F32),
            buf((8, 128), F32),
            buf((SEQ, 8, 128), F32),
            buf((DP, 8, 128), F32),
            dma((2,)),
            dma((8,)),
            dma((8,)),
            dma((8,)),
            dma((8,)),
            dma((8,)),
            dma((8,)),
            dma((8,)),
            dma((8,)),
            dma((DP,)),
            dma((DP,)),
            dma((4,)),
            dma((4,)),
            dma((DP,)),
            dma((DP,)),
            dma((SEQ,)),
            dma((SEQ,)),
            dma((SEQ,)),
            dma((SEQ,)),
            dma((DP,)),
            dma((DP,)),
        ],
        compiler_params=pltpu.CompilerParams(
            collective_id=1, has_side_effects=True, vmem_limit_bytes=VMEM_LIMIT
        ),
        name="scatter_sums",
    )(po, hg, gin, goa, gof)


def norm_back(scaled_grad, x_hat, inv_std):
    return inv_std * (
        scaled_grad
        - jnp.mean(scaled_grad, axis=-1, keepdims=True)
        - x_hat * jnp.mean(scaled_grad * x_hat, axis=-1, keepdims=True)
    )


def adam_step(weight, grad, first, second, factor, rate, decay):
    clipped = grad * factor
    first_new = BETA_ONE * first + (1.0 - BETA_ONE) * clipped
    second_new = BETA_TWO * second + (1.0 - BETA_TWO) * clipped * clipped
    first_hat = first_new / (1.0 - BETA_ONE**STEP)
    second_hat = second_new / (1.0 - BETA_TWO**STEP)
    weight_new = weight * (1.0 - rate * decay) - rate * first_hat / (
        jnp.sqrt(second_hat) + ADAM_EPS
    )
    return (weight_new, first_new, second_new)


def pack_in(in_weight, vectors):
    low = in_weight.astype(BF16).reshape(8, 112, 64)
    pieces = jnp.stack(
        [jnp.stack([low[:, int(p)] for p in PIECES[s]], axis=1) for s in range(SEQ)], axis=0
    )
    qkv = pieces[:, :, :3].reshape(SEQ, 8, 192)
    hidden = pieces[:, :, 3:].reshape(SEQ, 8, 256)
    vec = jnp.pad(vectors.astype(BF16).T, ((0, 0), (0, 64 - vectors.shape[0])))
    qkv = jnp.concatenate([qkv, jnp.broadcast_to(vec[None], (SEQ, 8, 64))], axis=2)
    return jnp.concatenate([hidden, qkv], axis=1)


def unpack_in(total):
    hidden = total[:, :8].reshape(SEQ, 8, 4, 64)
    qkv = total[:, 8:, :192].reshape(SEQ, 8, 3, 64)
    pieces = jnp.concatenate([qkv, hidden], axis=2)
    where = {int(PIECES[s, j]): (s, j) for s in range(SEQ) for j in range(7)}
    grad = jnp.stack([pieces[where[p][0], :, where[p][1]] for p in range(112)], axis=1)
    vec = jnp.sum(total[:, 8:, 192:205], axis=0).T
    return grad.reshape(8, 7 * D), vec


def body(
    hidden_in,
    out_cot,
    in_weight,
    out_weight,
    vectors,
    in_first,
    in_second,
    out_first,
    out_second,
    vec_first,
    vec_second,
    lengths,
    span_of,
):
    seq_index = lax.axis_index("seq")
    span = span_of.reshape(32)
    inv = jnp.sum(
        jnp.where(
            span[None, :] == jnp.arange(32, dtype=jnp.int32)[:, None],
            jnp.arange(32, dtype=jnp.int32)[None, :],
            0,
        ),
        axis=1,
    )
    mine = lax.dynamic_slice_in_dim(span_of, seq_index, 1, 0)[0]
    position = (mine[:, None] * SPAN + jnp.arange(SPAN, dtype=jnp.int32)[None, :]).reshape(TOK)
    valid = (position < lengths[0]).astype(F32)
    x_rows = hidden_in[0].astype(F32)
    row_mean = jnp.mean(x_rows, axis=-1, keepdims=True)
    centered = x_rows - row_mean
    inv_std = lax.rsqrt(jnp.mean(centered * centered, axis=-1, keepdims=True) + NORM_EPS)
    x_hat = centered * inv_std
    cot_low = (out_cot[0].astype(F32) * valid[:, None]).astype(BF16)
    win = pack_in(in_weight, vectors)
    wout = (
        out_weight.astype(BF16).reshape(5, 8, 2, 512).transpose(0, 2, 1, 3).reshape(5, 16, 512)
    )
    xh_all, cot_all, win_all, wout_all, swap_all = gather_call(
        x_hat.astype(BF16), cot_low, win, wout
    )
    po, hg, gin, goa, gof, vec_full = core_call(
        span, inv, lengths, xh_all, cot_all, win_all, wout_all, swap_all
    )
    out_sum, grad_sum, win_sum, wout_sum, squares = scatter_call(po, hg, gin, goa, gof)
    block_out = (x_rows + out_sum + (vec_full[7] + vec_full[8])).astype(BF16)
    input_grad = (cot_low.astype(F32) + norm_back(grad_sum, x_hat, inv_std)).astype(BF16)
    grad_in, grad_vec = unpack_in(win_sum)
    grad_out = wout_sum.reshape(5, 2, 8, 512).transpose(0, 2, 1, 3).reshape(40, D)
    grad_norm = jnp.sqrt(squares[0, 0])
    factor = jnp.minimum(1.0, CLIP_NORM / grad_norm)
    new_in, new_in_first, new_in_second = adam_step(
        in_weight, grad_in, in_first, in_second, factor, RATE_MATRIX, DECAY_RATE
    )
    new_out, new_out_first, new_out_second = adam_step(
        out_weight, grad_out, out_first, out_second, factor, RATE_MATRIX, DECAY_RATE
    )
    new_vectors, new_vec_first, new_vec_second = adam_step(
        vectors, grad_vec, vec_first, vec_second, factor, RATE_VECTOR, 0.0
    )
    return (
        block_out[None],
        input_grad[None],
        grad_norm,
        new_in,
        new_out,
        new_vectors,
        new_in_first,
        new_out_first,
        new_vec_first,
        new_in_second,
        new_out_second,
        new_vec_second,
        new_in.astype(BF16),
        new_out.astype(BF16),
        new_vectors.astype(BF16),
    )


def solution(mesh):
    tokens = P("dp", "seq", None)
    matrix = P(("seq", "dp"), None)
    vector = P(None, ("seq", "dp"))
    return jax.shard_map(
        body,
        mesh=mesh,
        in_specs=(
            tokens,
            tokens,
            matrix,
            matrix,
            vector,
            matrix,
            matrix,
            matrix,
            matrix,
            vector,
            vector,
            P("dp"),
            P(),
        ),
        out_specs=(tokens, tokens, P()) + (matrix, matrix, vector) * 4,
        check_vma=False,
    )
```

time: 2490 us -> 378 us (0.15)
  waiting for transfers between devices: 1860 us -> 0 us
  blocking collectives: 386 us -> 0 us
  Pallas kernels: 0 us -> 239 us
  matrix products: 105 us -> 0 us
  local copies, waits for them, and re-layouts: 43.6 us -> 112 us
  other arithmetic: 64.8 us -> 21.6 us
    reduce_scatter x3 -> x0, waiting for transfers between devices: 1470 us -> none  [the longest x1 699 us: body(): lax.psum_scatter(jnp.concatenate([part_a, part_m], axis=1), ('seq', 'dp')...]
    all_gather x4 -> x0, waiting for transfers between devices: 391 us -> none  [the longest x1 313 us: body(): lax.all_gather(out_low, ('seq', 'dp'), axis=0, tiled=True)]
    all_gather x1 -> x0, blocking collectives: 306 us -> none  [body(): lax.all_gather(vec_low, ('seq', 'dp'), axis=1, tiled=True)]
    pallas_call x0 -> x3, Pallas kernels: none -> 239 us  [the longest x1 110 us: scatter_call(): pl.pallas_call(scatter_kernel, out_shape=(sds((TOK, D), F32), sds((TOK, D...]
    another operation x0 -> x116, local copies, waits for them, and re-layouts: none -> 105 us  [the longest x113 105 us: unpack_in(): jnp.stack([pieces[where[p][0], :, where[p][1]] for p in range(112)], axis=1)]
    dot_general x19 -> x0, matrix products: 105 us -> none  [the longest x2 16.7 us: body(): jnp.einsum('thd,nhd->htn', attended_grad[:, head_first:head_first + group...]
    psum x1 -> x0, blocking collectives: 80.8 us -> none  [body(): lax.psum((local_squares, vec_local), ('seq', 'dp'))]
    concatenate x6 -> x2, other arithmetic: 31.1 us -> 0.76 us  [the longest x1 0.68 us: pack_in(): return jnp.concatenate([hidden, qkv], axis=1)]
  transfers between devices with their start and end apart: 7 -> 0, of which waited for: 7 -> 0; matrix products, arithmetic and copies ran while one was open for 4% -> 0% of each run, Pallas kernels for 0% -> 0%
where the time goes in v1:
time: 378 us; the launch traced here: 376 us
  Pallas kernels  239 us (63%)
  local copies, waits for them, and re-layouts  112 us (30%)
  other arithmetic  21.6 us (6%)
    pallas_call x1, Pallas kernels, scatter_call(): pl.pallas_call(scatter_kernel, out_shape=(sds((TOK, D), F32), sds((TOK, D...  110 us
    another operation x113, local copies, waits for them, and re-layouts, unpack_in(): jnp.stack([pieces[where[p][0], :, where[p][1]] for p in range(112)], axis=1)  105 us
    pallas_call x1, Pallas kernels, gather_call(): pl.pallas_call(gather_kernel, out_shape=(jax.ShapeDtypeStruct((SEQ, TOK,...  81.2 us
    pallas_call x1, Pallas kernels, core_call(): pl.pallas_call(core_kernel, out_shape=(sds((SEQ, TOK, D), BF16), sds((SEQ...  48.3 us

profile of v1, /device:TPU:1, one launch (start us, length us, event | category | flops | bytes accessed | tf_op | source)
XLA Modules:
  0.0 376.2 jit_solution(7044038769137932419)
XLA Ops:
  2.4 1.1 convert_reduce_fusion
  3.5 1.2 fusion.12
  6.9 1.6 convert_element_type.67
  8.5 1.0 convert_element_type.65
  10.1 1.6 fusion.20
  13.4 1.0 fusion.6
  14.4 81.2 %gather_rows_weights.1 = (bf16[16,128,1024]{2,1,0:T(8,128)(2,1)}, bf16[16,128,1024]{2,1,0:T(8,128)(2,1)}, bf16[8,16,16,256]{3,2,1,0:T(8,128)(2,1)}, bf16[40,16,512]{2,1,0:T(8,128)(2,1)}, bf16[4,8,16,512]{3,2,1,0:T(8,128)(2,1)}) custom-call(bf16[128,1024]{1,0:T(8,128)(2,1)} %get-tuple-element.248.xh_ref, bf16[128,1024]{1,0:T(8,128)(2,1)} %get-tuple-element.249.cot_ref, ...), custom_call_target="tpu_custom_call" | custom-call | tf_op jit(solution)/shard_map/gather_rows_weights/pallas_call | solution.py:274
  95.7 48.3 %layer_of_one_row.1 = (bf16[16,128,1024]{2,1,0:T(8,128)(2,1)}, bf16[16,128,1024]{2,1,0:T(8,128)(2,1)}, bf16[8,16,16,256]{3,2,1,0:T(8,128)(2,1)}, bf16[8,16,512]{...) custom-call(s32[32]{0:T(128)} %copy-done.7, s32[32]{0:T(128)} %select_reduce_fusion.inv_ref, ...), custom_call_target="tpu_custom_call" | custom-call | tf_op jit(solution)/shard_map/layer_of_one_row/pallas_call | solution.py:639
  144.0 109.7 %scatter_sums.1 = (f32[128,1024]{1,0:T(8,128)}, f32[128,1024]{1,0:T(8,128)}, f32[16,16,256]{2,1,0:T(8,128)}, f32[5,16,512]{2,1,0:T(8,128)}, f32[8,128]{1,0:T(8,128)}) custom-call(bf16[16,128,1024]{2,1,0:T(8,128)(2,1)} %get-tuple-element.36.po_ref, bf16[16,128,1024]{2,1,0:T(8,128)(2,1)} %get-tuple-element.37.hg_ref, ...), custom_call_target="tpu_custom_call" | custom-call | tf_op jit(solution)/shard_map/scatter_sums/pallas_call | solution.py:991
  253.6 1.2 slice.705
  255.6 1.3 fusion.26
  256.9 0.9 slice_reduce_fusion
  258.6 2.2 fusion.17
  261.4 0.9 slice.755
  262.3 0.9 slice.706
  267.2 0.9 copy.600
  268.9 1.5 copy.592
  270.5 0.9 copy.591
  271.4 0.9 copy.590
  275.7 0.9 copy.585
  276.5 0.9 copy.584
  277.4 0.9 copy.583
  278.3 0.9 copy.582
  281.8 0.9 copy.578
  283.5 0.9 copy.576
  287.8 0.9 copy.569
  290.4 0.9 copy.566
  295.6 0.9 copy.560
  299.1 0.9 copy.554
  301.6 0.9 copy.551
  305.9 0.9 copy.618
  313.7 0.9 copy.609
  316.3 0.9 copy.606
  317.1 0.9 copy.605
  318.9 0.9 copy.603
  319.7 0.9 copy.602
  321.5 0.9 copy.655
  322.4 0.9 copy.654
  323.2 0.9 copy.653
  324.1 0.9 copy.652
  327.6 0.9 copy.648
  333.6 0.9 copy.641
  335.4 0.9 copy.637
  336.2 0.9 copy.636
  341.4 0.9 copy.630
  354.3 16.2 %stack.148 = f32[8,112,64]{1,2,0:T(8,128)S(1)} concatenate(f32[8,1,64]{1,2,0:T(8,128)} %copy.547, f32[8,1,64]{1,2,0:T(8,128)} %copy.548, f32[8,1,64]{1,2,0:T(8,128)} %copy.549, f32[8,1,64]{1,2,0:T(8,128)} %copy.550, f32[8,1,64]{1,2,0:T(8,128)} %copy.551, f32[8,1,64]{1,2,0:T(8,128)} %copy.552, f32[8,1,64]{1,2,0:T(8,128)} %copy.553, f32[8,1,64]{1,2,0:T(8,128)} %copy.554, ...), dimensions={1} | concatenate | bytes 458752 | tf_op jit(solution)/shard_map/stack | solution.py:1083
  370.9 2.0 fusion.29
  372.9 2.1 fusion.31
  (156 shorter events, 71.2 us)
Async XLA Ops:
  0.6 12.8 %copy-start = (bf16[1,128,1024]{2,1,0:T(8,128)(2,1)S(1)}, bf16[1,128,1024]{2,1,0:T(8,128)(2,1)}, u32[]{:S(2)}) copy-start(bf16[1,128,1024]{2,1,0:T(8,128)(2,1)} %param.14) | copy-start | bytes 786436
  0.7 12.8 %copy-start.2 = (bf16[1,128,1024]{2,1,0:T(8,128)(2,1)S(1)}, bf16[1,128,1024]{2,1,0:T(8,128)(2,1)}, u32[]{:S(2)}) copy-start(bf16[1,128,1024]{2,1,0:T(8,128)(2,1)} %param.15) | copy-start | bytes 786436
  6.3 89.4 %copy-start.7 = (s32[32]{0:T(128)}, s32[32]{0:T(128)S(1)}, u32[]{:S(2)}) copy-start(s32[32]{0:T(128)S(1)} %reshape.124.span_ref) | copy-start | bytes 388
  143.9 114.7 %copy-start.1 = (bf16[128,1024]{1,0:T(8,128)(2,1)S(1)}, bf16[128,1024]{1,0:T(8,128)(2,1)}, u32[]{:S(2)}) copy-start(bf16[128,1024]{1,0:T(8,128)(2,1)} %get-tuple-element.249.cot_ref) | copy-start | bytes 786436
  143.9 116.9 %copy-start.4 = (f32[13,8]{0,1:T(8,128)S(1)}, f32[13,8]{0,1:T(8,128)}, u32[]{:S(2)}) copy-start(f32[13,8]{0,1:T(8,128)} %param.18) | copy-start | bytes 1252
  143.9 116.9 %copy-start.5 = (f32[13,8]{0,1:T(8,128)S(1)}, f32[13,8]{0,1:T(8,128)}, u32[]{:S(2)}) copy-start(f32[13,8]{0,1:T(8,128)} %param.23) | copy-start | bytes 1252
  143.9 116.9 %copy-start.6 = (f32[13,8]{0,1:T(8,128)S(1)}, f32[13,8]{0,1:T(8,128)}, u32[]{:S(2)}) copy-start(f32[13,8]{0,1:T(8,128)} %param.24) | copy-start | bytes 1252
  253.6 11.0 %copy-start.3 = (f32[5,16,512]{2,1,0:T(8,128)S(1)}, f32[5,16,512]{2,1,0:T(8,128)}, u32[]{:S(2)}) copy-start(f32[5,16,512]{2,1,0:T(8,128)} %get-tuple-element.46) | copy-start | bytes 491524

commit v2 on v1

v2 whole, which is shorter than its diff:
```python
import functools
import math

import jax
import jax.numpy as jnp
import numpy as np
from jax import lax
from jax.experimental import pallas as pl
from jax.experimental.pallas import tpu as pltpu
from jax.sharding import PartitionSpec as P

D = 1024
FF = 4096
HEADS = 16
HEAD = 64
ROT = 16
STEP = 5
SEQ = 16
DP = 8
TOK = 128
ROW = 2048
SPAN = 64
VEC_ROWS = 13

NORM_EPS = 1e-05
NEG_FILL = -1e30
CLIP_NORM = 1.0
RATE_MATRIX = 0.02
RATE_VECTOR = 0.2
BETA_ONE = 0.5
BETA_TWO = 0.5
DECAY_RATE = 0.1
ADAM_EPS = 1e-08
THETA_BASE = 10000.0

F32 = jnp.float32
BF16 = jnp.bfloat16
MESH = pl.DeviceIdType.MESH
VMEM_LIMIT = 60 * 1024 * 1024


def head_of(s):
    if s < 4:
        return 5 * s
    return 5 * ((s - 4) // 4) + 1 + (s - 4) % 4


def hidden_pieces(s):
    if s < 3:
        return [20 * s + 5 * r + 8 for r in range(4)]
    if s == 3:
        return [0, 1, 2, 3]
    return [5 * s - 16 + r for r in range(4)]


def column_pieces():
    rows = []
    for s in range(SEQ):
        h = head_of(s)
        rows.append([h, 16 + h, 32 + h] + [48 + w for w in hidden_pieces(s)])
    return np.array(rows, np.int32)


PIECES = column_pieces()


def head_index(s):
    late = (s + 12) // 16
    return (1 - late) * (5 * s) + late * (5 * ((s - 4) // 4) + 1 + lax.rem(s, 4))


def hidden_index(s, r):
    late, not_few = (s + 12) // 16, (s + 13) // 16
    return (
        (1 - not_few) * (20 * s + 5 * r + 8) + (not_few - late) * r + late * (5 * s - 16 + r)
    )


def remote(src, dst, send, recv, where):
    return pltpu.make_async_remote_copy(
        src_ref=src, dst_ref=dst, send_sem=send, recv_sem=recv, device_id=where, device_id_type=MESH
    )


def greet(me, dm):
    barrier = pltpu.get_barrier_semaphore()

    @pl.loop(1, SEQ)
    def _(k):
        pl.semaphore_signal(
            barrier, inc=1, device_id={"seq": lax.rem(me + k, SEQ)}, device_id_type=MESH
        )

    @pl.loop(1, DP)
    def _(k):
        pl.semaphore_signal(
            barrier, inc=1, device_id={"dp": lax.rem(dm + k, DP)}, device_id_type=MESH
        )


def await_greetings():
    pl.semaphore_wait(pltpu.get_barrier_semaphore(), SEQ + DP - 2)


class Tree:
    def __init__(self, axis, piece, me, turn, mate, sib, send, recv, over_mate):
        self.axis, self.piece, self.me, self.turn, self.mate, self.sib = (
            axis,
            piece,
            me,
            turn,
            mate,
            sib,
        )
        self.send, self.recv, self.over_mate = send, recv, over_mate
        self.started = []

    def put(self, slot, h, to):
        part = self.piece(slot, h)
        copy = remote(
            part, part, self.send.at[len(self.started)], self.recv.at[slot, h], {self.axis: to}
        )
        copy.start()
        self.started.append(copy)

    def hand(self, slot, h):
        if self.sib is not None:
            self.put(slot, h, self.sib)

    def got(self, slot, h):
        part = self.piece(slot, h)
        remote(
            part, part, self.send.at[0], self.recv.at[slot, h], {self.axis: self.mate}
        ).wait_recv()

    def own(self):
        for h in range(2):
            for to in (self.mate, self.turn(self.me, 1), self.turn(self.me, 3)):
                self.put(self.me, h, to)
        for h in range(2):
            self.hand(self.me, h)

    def of_mate(self):
        for h in range(2):
            self.got(self.mate, h)
            for k in (1, 3):
                self.put(self.mate, h, self.turn(self.me, k))
            self.hand(self.mate, h)

    def near(self, base):
        for h in range(2):
            for k in (3, 1):
                slot = self.turn(base, k)
                self.got(slot, h)
                if (k == 3) == (h == 0):
                    self.put(slot, h, self.turn(self.me, 4 - k))
                self.hand(slot, h)

    def near_of_me(self):
        self.near(self.me)

    def far_of_me(self):
        slot = self.turn(self.me, 2)
        for h in range(2):
            self.got(slot, h)
            if self.over_mate:
                self.put(slot, h, self.mate)
            self.hand(slot, h)

    def near_of_mate(self):
        if not self.over_mate:
            return self.near(self.mate)
        for h in range(2):
            for k in (3, 1):
                slot = self.turn(self.mate, k)
                self.got(slot, h)
                self.hand(slot, h)

    def far_of_mate(self):
        slot = self.turn(self.mate, 2)
        for h in range(2):
            self.got(slot, h)
            self.hand(slot, h)

    def handed(self, other_mate):
        for h in range(2):
            for slot in (self.sib, other_mate):
                for k in range(4):
                    self.got(self.turn(slot, k), h)

    def sent(self):
        for copy in self.started:
            copy.wait_send()


def dot(a, b):
    return jnp.dot(a, b, preferred_element_type=F32)


def dot_nt(a, b):
    return lax.dot_general(a, b, (((1,), (1,)), ((), ())), preferred_element_type=F32)


def lane_iota(shape):
    return lax.broadcasted_iota(jnp.int32, shape, len(shape) - 1)


def fold(u):
    return jnp.concatenate([u[:, : D // 2], u[:, D // 2 :]], axis=0)


def unfold(u):
    return jnp.concatenate([u[:8], u[8:]], axis=1)


CH = 512
NCH = ROW // CH


def layer_kernel(
    span_ref,
    inv_ref,
    len_ref,
    x_ref,
    cot_ref,
    w_in_ref,
    w_out_ref,
    vectors_ref,
    cos_ref,
    sin_ref,
    out_sum,
    grad_sum,
    win_sum,
    wout_sum,
    square_ref,
    vec_ref,
    xh_all,
    cot_all,
    win_own,
    win_all,
    wout_all,
    swap_all,
    small,
    xs,
    cs,
    wqr,
    wfr,
    wqp,
    wfp,
    woa,
    wof,
    qt,
    qn,
    kt,
    kn,
    vt,
    vn,
    dot_t,
    dot_n,
    ot,
    lse,
    delta,
    act,
    act_t,
    dact,
    mixf,
    mixf_t,
    mixq,
    mixq_t,
    att,
    att_t,
    dqt,
    dkn,
    dvn,
    vg,
    cot_cols,
    gin,
    goa_buf,
    gof_buf,
    po_sib,
    hg_sib,
    po_got,
    hg_got,
    gin_got,
    own_out,
    out_got,
    win_part,
    tile_a,
    tile_b,
    got_a,
    got_b,
    local_sem,
    a_send,
    a_recv,
    x_send,
    x_recv,
    c_send,
    c_recv,
    l_send,
    l_recv,
    o_send,
    o_recv,
    w_send,
    w_recv,
    ps_send,
    ps_recv,
    pg_send,
    pg_recv,
    hs_send,
    hs_recv,
    hgs_send,
    hgs_recv,
    g_send,
    g_recv,
    v_send,
    v_recv,
    go_send,
    go_recv,
    b_send,
    b_recv,
    ta_send,
    ta_recv,
    tb_send,
    tb_recv,
):
    me = lax.axis_index("seq")
    dm = lax.axis_index("dp")
    core = lax.rem(me, 2)
    chip = me // 2
    sib = me + 1 - 2 * core
    mate = me + 2 - 4 * lax.rem(chip, 2)
    sib_mate = mate + 1 - 2 * core
    dp_mate = lax.rem(dm + 4, DP)
    head = head_index(me)
    greet(me, dm)

    row = lax.broadcasted_iota(jnp.int32, (TOK, 1), 0)
    place = jnp.where(row < SPAN, span_ref[2 * me] * SPAN + row, span_ref[2 * me + 1] * SPAN + row - SPAN)
    x_rows = x_ref[...].astype(F32)
    centered = x_rows - jnp.mean(x_rows, axis=-1, keepdims=True)
    inv_std = lax.rsqrt(jnp.mean(centered * centered, axis=-1, keepdims=True) + NORM_EPS)
    xh_all[pl.ds(2 * me, 2)] = (centered * inv_std).astype(BF16).reshape(2, SPAN, D)

    small[...] = jnp.zeros((128, 128), F32)
    small[0:VEC_ROWS, 0:8] = vectors_ref[...]
    vec_t = jnp.transpose(small[...])[0:8, 0:64]
    for s in range(SEQ):
        take = [w_in_ref[:, 64 * int(p) : 64 * int(p) + 64] for p in PIECES[s]]
        qkv = jnp.concatenate(take[:3] + [vec_t], axis=1)
        win_own[s] = jnp.concatenate([jnp.concatenate(take[3:], axis=1), qkv], axis=0).astype(BF16)
    for u in range(5):
        wout_all[5 * dm + u] = fold(w_out_ref[8 * u : 8 * u + 8]).astype(BF16)
    cot_own = jnp.where(place < len_ref[0], cot_ref[...].astype(F32), 0.0)
    cot_all[pl.ds(2 * me, 2)] = cot_own.astype(BF16).reshape(2, SPAN, D)
    cot_sum = jnp.sum(cot_own, axis=0, keepdims=True)
    cot_cols[...] = jnp.transpose(jnp.broadcast_to(cot_sum, (128, D)))
    keep = pltpu.make_async_copy(win_own.at[me], win_all.at[dm, me], local_sem.at[0])
    keep.start()

    def seq_turn(s, k):
        return lax.rem(s + 4 * k, SEQ)

    def dp_turn(d, k):
        return d // 4 * 4 + lax.rem(d + k, 4)

    x_tree = Tree(
        "seq",
        lambda slot, h: xh_all.at[2 * slot + h],
        me,
        seq_turn,
        mate,
        sib,
        x_send,
        x_recv,
        True,
    )
    cot_tree = Tree(
        "seq",
        lambda slot, h: cot_all.at[2 * slot + h],
        me,
        seq_turn,
        mate,
        sib,
        c_send,
        c_recv,
        True,
    )
    in_tree = Tree(
        "dp",
        lambda slot, h: win_all.at[slot, pl.ds(8 * h, 8)],
        dm,
        dp_turn,
        dp_mate,
        None,
        l_send,
        l_recv,
        False,
    )
    out_tree = Tree(
        "dp",
        lambda slot, h: wout_all.at[pl.ds(5 * slot + 2 * h, 2 + h)],
        dm,
        dp_turn,
        dp_mate,
        None,
        o_send,
        o_recv,
        False,
    )

    def a_copy(k, to, frm):
        return remote(
            win_own.at[to], win_all.at[dm, frm], a_send.at[k], a_recv.at[frm], {"seq": to}
        )

    await_greetings()

    @pl.loop(1, SEQ)
    def _(k):
        a_copy(k, lax.rem(me + k, SEQ), me).start()

    x_tree.own()
    out_tree.own()
    keep.wait()

    @pl.loop(1, SEQ)
    def _(k):
        a_copy(k, me, lax.rem(me + k, SEQ)).wait_recv()

    in_tree.own()
    out_tree.of_mate()
    x_tree.of_mate()
    out_tree.near_of_me()
    in_tree.of_mate()
    x_tree.near_of_me()
    out_tree.near_of_mate()
    in_tree.near_of_me()
    x_tree.far_of_me()
    cot_tree.own()
    in_tree.near_of_mate()
    x_tree.near_of_mate()
    x_tree.far_of_mate()
    in_tree.far_of_me()
    in_tree.far_of_mate()
    out_tree.far_of_me()
    out_tree.far_of_mate()

    def swap_few(r):
        return remote(
            wout_all.at[pl.ds(8 + 8 * r, 8)],
            swap_all.at[0],
            w_send.at[r],
            w_recv.at[0],
            {"seq": 4 + 4 * me + r},
        )

    def swap_many():
        return remote(
            wout_all.at[pl.ds(32, 8)],
            swap_all.at[lax.rem(me, 4)],
            w_send.at[0],
            w_recv.at[lax.rem(me, 4)],
            {"seq": (me - 4) // 4},
        )

    @pl.when(me < 3)
    def _():
        for r in range(4):
            swap_few(r).start()

    @pl.when(me > 3)
    def _():
        swap_many().start()

    def unpack(sb, carry):
        cq, cf = carry
        tiles = [win_all[d, sb].astype(F32) for d in range(DP)]
        ff = jnp.concatenate([t[:8] for t in tiles], axis=0)
        qk = jnp.concatenate([t[8:] for t in tiles], axis=0)
        rows = pl.ds(pl.multiple_of(sb * 64, 64), 64)
        gain_a, bias_a, gain_m, bias_m = (qk[:, 192 + i : 193 + i] for i in range(4))
        wfr[rows] = ff.astype(BF16)
        wqr[rows] = qk.astype(BF16)
        wfp[rows] = (ff * gain_m).astype(BF16)
        wqp[rows] = jnp.where(lane_iota(qk.shape) < 192, qk * gain_a, 0.0).astype(BF16)
        return (
            cq + jnp.sum(qk * bias_a, axis=0, keepdims=True),
            cf + jnp.sum(ff * bias_m, axis=0, keepdims=True),
        )

    zero_row = jnp.zeros((1, 256), F32)
    cq, cf = lax.fori_loop(0, SEQ, unpack, (zero_row, zero_row))

    slab = jnp.transpose(wqr[:, 128:256].astype(F32))
    vec_ref[...] = slab[64:80]

    hid = []
    for r in range(4):
        w = hidden_index(me, r)
        rows = pl.ds(pl.multiple_of(lax.rem(w, 16) * 64, 64), 64)
        part = wqr[rows, 128:256].astype(F32)
        lane = 64 + 9 + w // 16
        hid.append(
            jnp.sum(jnp.where(lane_iota(part.shape) == lane, part, 0.0), axis=1, keepdims=True)
        )
    hid = jnp.concatenate(hid, axis=0)
    cf = cf + jnp.transpose(jnp.broadcast_to(hid, (256, 128)))[0:1]

    head_rows = pl.ds(pl.multiple_of(head * 64, 64), 64)
    head_vecs = wqr[head_rows, 128:256].astype(F32)
    bq, bk, bv = (head_vecs[:, 68 + i : 69 + i] for i in range(3))

    x_tree.handed(sib_mate)

    @pl.loop(0, 32)
    def _(i):
        rows = pl.ds(pl.multiple_of(i * SPAN, SPAN), SPAN)
        xs[rows] = xh_all[inv_ref[i]]

    cot_tree.of_mate()

    aug = jnp.where(lax.broadcasted_iota(jnp.int32, (64, CH), 0) == 0, 1.0, 0.0)
    zeros_aug = jnp.zeros((64, CH), F32)

    def rotate_t(u, cosine, sine, sign):
        first, second = u[0:8], u[8:16]
        return jnp.concatenate(
            [
                first * cosine - sign * (second * sine),
                second * cosine + sign * (first * sine),
                u[16:],
            ],
            axis=0,
        )

    @pl.loop(0, NCH)
    def _(i):
        start = pl.multiple_of(i * CH, CH)
        rows = pl.ds(start, CH)
        xh = xs[rows]
        qkv = jnp.transpose(dot(xh, wqp[...]) + cq)
        cosine, sine = cos_ref[:, rows], sin_ref[:, rows]
        q = rotate_t(qkv[0:64] + bq, cosine, sine, 1.0) * 0.125
        k = rotate_t(qkv[64:128] + bk, cosine, sine, 1.0)
        v = qkv[128:192] + bv
        q_full = jnp.concatenate([q, aug], axis=0)
        past = (start + lane_iota((64, CH))) >= len_ref[0]
        k_full = jnp.concatenate([k, jnp.where(past, NEG_FILL, 0.0) * aug], axis=0)
        v_full = jnp.concatenate([v, zeros_aug], axis=0)
        qt[:, rows] = q_full.astype(BF16)
        kt[:, rows] = k.astype(BF16)
        vt[:, rows] = v.astype(BF16)
        qn[rows] = jnp.transpose(q_full).astype(BF16)
        kn[rows] = jnp.transpose(k_full).astype(BF16)
        vn[rows] = jnp.transpose(v_full).astype(BF16)
        pre = dot(xh, wfp[...]) + cf
        cdf = 0.5 * (1.0 + lax.erf(pre * (1.0 / math.sqrt(2.0))))
        pdf = jnp.exp(-0.5 * pre * pre) * (1.0 / math.sqrt(2.0 * math.pi))
        activ = pre * cdf
        act[pl.ds(8 * i, 8)] = activ.astype(BF16).reshape(8, SPAN, 256)
        act_t[:, rows] = jnp.transpose(activ).astype(BF16)
        dact[rows] = cdf + pre * pdf

    cot_tree.near_of_me()
    causal = lax.broadcasted_iota(jnp.int32, (CH, CH), 0) <= lane_iota((CH, CH))

    def scores(kc, qi):
        s = dot(kn[kc * CH : (kc + 1) * CH], qt[:, qi * CH : (qi + 1) * CH])
        if kc == qi:
            s = jnp.where(causal, s, NEG_FILL)
        return s

    for qi in range(NCH):
        lanes = slice(qi * CH, (qi + 1) * CH)
        parts = [scores(kc, qi) for kc in range(qi + 1)]
        top = functools.reduce(jnp.maximum, [jnp.max(s, axis=0, keepdims=True) for s in parts])
        total = jnp.zeros((1, CH), F32)
        out = jnp.zeros((64, CH), F32)
        for kc, s in enumerate(parts):
            p = jnp.exp(s - top)
            total = total + jnp.sum(p, axis=0, keepdims=True)
            out = out + dot(vt[:, kc * CH : (kc + 1) * CH], p.astype(BF16))
        out = out / total
        ot[:, lanes] = out
        lse[:, lanes] = jnp.broadcast_to(top + jnp.log(total), (8, CH))
        att_t[:, lanes] = out.astype(BF16)
        att[8 * qi : 8 * qi + 8] = jnp.transpose(out).astype(BF16).reshape(8, SPAN, HEAD)
        if qi == 2:
            cot_tree.far_of_me()
            cot_tree.near_of_mate()
    cot_tree.far_of_mate()

    def put_units(src, base, dst, count):
        @pl.loop(0, count // 2)
        def _(i):
            pair = [unfold(src[base + 2 * i + j].astype(F32)) for j in range(2)]
            dst[pl.ds(pl.multiple_of(i * 16, 16), 16)] = jnp.concatenate(pair, axis=0).astype(BF16)

    def put_swap(dst, rs):
        for r in range(rs):
            for i in range(4):
                pair = [unfold(swap_all[r, 2 * i + j].astype(F32)) for j in range(2)]
                dst[r * 64 + i * 16 : r * 64 + i * 16 + 16] = jnp.concatenate(pair, axis=0).astype(
                    BF16
                )

    @pl.when(me < 4)
    def _():
        put_units(wout_all, 0, woa, 8)

    @pl.when(me < 3)
    def _():
        for r in range(4):
            remote(
                wout_all.at[pl.ds(32, 8)], swap_all.at[r], w_send.at[r], w_recv.at[r], {"seq": sib}
            ).wait_recv()
            swap_few(r).wait_send()
        put_swap(wof, 4)

    @pl.when(me == 3)
    def _():
        put_units(wout_all, 8, wof, 32)

    @pl.when(me > 3)
    def _():
        swap_many().wait_send()
        remote(
            wout_all.at[pl.ds(32, 8)], swap_all.at[0], w_send.at[0], w_recv.at[0], {"seq": sib}
        ).wait_recv()
        put_swap(woa, 1)
        put_units(wout_all, 0, wof, 32)

    def of_chip(ref, j):
        return jnp.concatenate([ref[span_ref[4 * j + i]] for i in range(4)], axis=0)

    def chip_sums(part, buf, sib_buf, got, s_send, s_recv, c_send, c_recv):
        def to_sib(j):
            return remote(
                buf.at[pl.ds(4 * j + 2 - 2 * core, 2)], sib_buf.at[j], s_send.at[j], s_recv.at[j], {"seq": sib}
            )

        def to_chip(j, frm):
            return remote(
                buf.at[pl.ds(4 * j + 2 * core, 2)],
                got.at[frm],
                c_send.at[j],
                c_recv.at[frm],
                {"seq": 2 * j + core},
            )

        def compute():
            @pl.loop(0, 8)
            def _(k):
                j = lax.rem(chip + 1 + k, 8)
                buf[pl.ds(4 * j, 4)] = part(j).astype(BF16).reshape(4, SPAN, D)
                to_sib(j).start()

        def send():
            @pl.loop(0, 8)
            def _(k):
                j = lax.rem(chip + 1 + k, 8)
                to_sib(j).wait_recv()
                mine = pl.ds(4 * j + 2 * core, 2)
                buf[mine] = (buf[mine].astype(F32) + sib_buf[j].astype(F32)).astype(BF16)

                @pl.when(k < 7)
                def _():
                    to_chip(j, chip).start()

        def finish(total):
            @pl.loop(1, 8)
            def _(k):
                to_chip(chip, lax.rem(chip + k, 8)).wait_recv()

            value = buf[pl.ds(2 * me, 2)].astype(F32)
            for k in range(1, 8):
                value = value + got[lax.rem(chip + k, 8)].astype(F32)
            total[...] = value.reshape(TOK, D)

            @pl.loop(0, 8)
            def _(k):
                j = lax.rem(chip + 1 + k, 8)
                to_sib(j).wait_send()

                @pl.when(k < 7)
                def _():
                    to_chip(j, chip).wait_send()

        return compute, send, finish

    def out_part(j):
        return dot(of_chip(att, j), woa[...]) + dot(of_chip(act, j), wof[...])

    def grad_part(j):
        return dot_nt(of_chip(mixq, j), wqp[...]) + dot_nt(of_chip(mixf, j), wfp[...])

    po_compute, po_send, po_finish = chip_sums(
        out_part, xh_all, po_sib, po_got, ps_send, ps_recv, pg_send, pg_recv
    )
    hg_compute, hg_send, hg_finish = chip_sums(
        grad_part, cot_all, hg_sib, hg_got, hs_send, hs_recv, hgs_send, hgs_recv
    )
    x_tree.sent()
    po_compute()
    cot_tree.handed(sib_mate)

    @pl.loop(0, 32)
    def _(i):
        rows = pl.ds(pl.multiple_of(i * SPAN, SPAN), SPAN)
        cs[rows] = cot_all[inv_ref[i]]

    po_send()

    @pl.loop(0, NCH)
    def _(i):
        rows = pl.ds(pl.multiple_of(i * CH, CH), CH)
        cot = cs[rows]
        ag = dot_nt(cot, woa[...]).astype(BF16).astype(F32)
        ag_t = jnp.transpose(ag)
        dot_n[rows] = ag.astype(BF16)
        dot_t[:, rows] = ag_t.astype(BF16)
        delta[:, rows] = jnp.broadcast_to(
            jnp.sum(ag_t * ot[:, rows], axis=0, keepdims=True), (8, CH)
        )
        pg = dot_nt(cot, wof[...]) * dact[rows]
        mixf[pl.ds(8 * i, 8)] = pg.astype(BF16).reshape(8, SPAN, 256)
        mixf_t[:, rows] = jnp.transpose(pg).astype(BF16)

    goa = dot(att_t[...], cs[...])
    for u in range(8):
        goa_buf[u] = fold(goa[8 * u : 8 * u + 8]).astype(BF16)

    @pl.loop(0, 4)
    def _(i):
        gof = dot(act_t[pl.ds(pl.multiple_of(i * 64, 64), 64)], cs[...])
        for u in range(8):
            gof_buf[8 * i + u] = fold(gof[8 * u : 8 * u + 8]).astype(BF16)

    def back_few(r):
        return remote(
            gof_buf.at[pl.ds(8 * r, 8)],
            own_out.at[pl.ds(32, 8)],
            v_send.at[r],
            v_recv.at[0],
            {"seq": 4 + 4 * me + r},
        )

    def back_many():
        return remote(
            goa_buf,
            own_out.at[pl.ds(8 + 8 * lax.rem(me, 4), 8)],
            v_send.at[0],
            v_recv.at[lax.rem(me, 4)],
            {"seq": (me - 4) // 4},
        )

    keep_a = pltpu.make_async_copy(goa_buf, own_out.at[pl.ds(0, 8)], local_sem.at[0])
    keep_f3 = pltpu.make_async_copy(gof_buf, own_out.at[pl.ds(8, 32)], local_sem.at[1])
    keep_f = pltpu.make_async_copy(gof_buf, own_out.at[pl.ds(0, 32)], local_sem.at[1])

    @pl.when(me < 3)
    def _():
        for r in range(4):
            back_few(r).start()

    @pl.when(me < 4)
    def _():
        keep_a.start()

    @pl.when(me == 3)
    def _():
        keep_f3.start()

    @pl.when(me > 3)
    def _():
        back_many().start()
        keep_f.start()

    for qi in range(NCH):
        lanes = slice(qi * CH, (qi + 1) * CH)
        dq = jnp.zeros((64, CH), F32)
        for kc in range(qi + 1):
            keys = slice(kc * CH, (kc + 1) * CH)
            p = jnp.exp(scores(kc, qi) - lse[0:1, lanes])
            dp = dot(vn[keys, 0:64], dot_t[:, lanes])
            ds = (p * (dp - delta[0:1, lanes])).astype(BF16)
            dv = dot(p.astype(BF16), dot_n[lanes])
            dk = dot(ds, qn[lanes, 0:64])
            dq = dq + dot(kt[:, keys], ds)
            if kc == qi:
                dvn[keys] = dv
                dkn[keys] = dk
            else:
                dvn[keys] += dv
                dkn[keys] += dk
        dqt[:, lanes] = dq * 0.125

    @pl.loop(0, NCH)
    def _(i):
        rows = pl.ds(pl.multiple_of(i * CH, CH), CH)
        cosine, sine = cos_ref[:, rows], sin_ref[:, rows]
        dq = rotate_t(dqt[:, rows], cosine, sine, -1.0)
        dk = rotate_t(jnp.transpose(dkn[rows]), cosine, sine, -1.0)
        dv = jnp.transpose(dvn[rows])
        full = jnp.concatenate([dq, dk, dv, zeros_aug], axis=0)
        mixq_t[:, rows] = full.astype(BF16)
        mixq[pl.ds(8 * i, 8)] = jnp.transpose(full).astype(BF16).reshape(8, SPAN, 256)

    @pl.when(me < 3)
    def _():
        for r in range(4):
            back_few(r).wait_send()
            remote(
                goa_buf, own_out.at[pl.ds(8 + 8 * r, 8)], v_send.at[r], v_recv.at[r], {"seq": sib}
            ).wait_recv()

    @pl.when(me < 4)
    def _():
        keep_a.wait()

    @pl.when(me == 3)
    def _():
        keep_f3.wait()

    @pl.when(me > 3)
    def _():
        back_many().wait_send()
        keep_f.wait()
        remote(
            goa_buf, own_out.at[pl.ds(32, 8)], v_send.at[0], v_recv.at[0], {"seq": sib}
        ).wait_recv()

    def go_copy(k, to, frm):
        return remote(
            own_out.at[pl.ds(5 * to, 5)],
            out_got.at[frm],
            go_send.at[k],
            go_recv.at[frm],
            {"dp": to},
        )

    @pl.loop(1, DP)
    def _(k):
        go_copy(k, lax.rem(dm + k, DP), dm).start()

    cot_tree.sent()
    hg_compute()

    sums_q = jnp.sum(mixq[...].reshape(ROW, 256).astype(F32), axis=0, keepdims=True)
    sums_f = jnp.sum(mixf[...].reshape(ROW, 256).astype(F32), axis=0, keepdims=True)
    cols_q = jnp.sum(mixq_t[...].astype(F32), axis=1, keepdims=True)
    cols_f = jnp.sum(mixf_t[...].astype(F32), axis=1, keepdims=True)
    lanes_d = lane_iota((D, 128))
    vg[...] = jnp.where((lanes_d == 71) | (lanes_d == 72), cot_cols[...], 0.0)
    lanes_h = lane_iota((64, 128))
    for i in range(3):
        vg[head_rows] += jnp.where(lanes_h == 68 + i, cols_q[64 * i : 64 * i + 64], 0.0)
    for r in range(4):
        w = hidden_index(me, r)
        rows = pl.ds(pl.multiple_of(lax.rem(w, 16) * 64, 64), 64)
        vg[rows] += jnp.where(lanes_h == 64 + 9 + w // 16, cols_f[64 * r : 64 * r + 64], 0.0)

    @pl.loop(0, 4)
    def _(i):
        rows = pl.ds(pl.multiple_of(i * 256, 256), 256)
        hq = jnp.transpose(dot(mixq_t[...], xs[:, rows]))
        hf = jnp.transpose(dot(mixf_t[...], xs[:, rows]))
        raw_q = wqr[rows].astype(F32)
        raw_f = wfr[rows].astype(F32)
        gain_a, bias_a, gain_m, bias_m = (raw_q[:, 192 + j : 193 + j] for j in range(4))
        gq = gain_a * hq + bias_a * sums_q
        gf = gain_m * hf + bias_m * sums_f
        extra = vg[rows]
        lanes = lane_iota((256, 128))
        for j, col in enumerate((raw_q * hq, raw_q * sums_q, raw_f * hf, raw_f * sums_f)):
            extra = extra + jnp.where(lanes == 64 + j, jnp.sum(col, axis=1, keepdims=True), 0.0)
        gq = jnp.concatenate([gq[:, :128], gq[:, 128:] + extra], axis=1)
        for j in range(4):
            part_f = gf[64 * j : 64 * j + 64].reshape(8, 8, 256)
            part_q = gq[64 * j : 64 * j + 64].reshape(8, 8, 256)
            gin[:, 4 * i + j] = jnp.concatenate([part_f, part_q], axis=1).astype(BF16)

    def g_copy(k, to, frm):
        return remote(gin.at[to], gin_got.at[frm], g_send.at[k], g_recv.at[frm], {"dp": to})

    @pl.loop(1, DP)
    def _(k):
        g_copy(k, lax.rem(dm + k, DP), dm).start()

    hg_send()

    @pl.loop(1, DP)
    def _(k):
        go_copy(k, dm, lax.rem(dm + k, DP)).wait_recv()

    total = own_out[pl.ds(5 * dm, 5)].astype(F32)
    for k in range(1, DP):
        total = total + out_got[lax.rem(dm + k, DP)].astype(F32)
    wout_sum[...] = total
    squares = jnp.sum(total * total, axis=0)
    squares = jnp.sum(squares, axis=0, keepdims=True)

    po_finish(out_sum)

    @pl.loop(1, DP)
    def _(k):
        g_copy(k, dm, lax.rem(dm + k, DP)).wait_recv()

    @pl.loop(0, SEQ)
    def _(s):
        total = gin[dm, s].astype(F32)
        for k in range(1, DP):
            total = total + gin_got[lax.rem(dm + k, DP), s].astype(F32)
        win_part[s] = total

    def b_copy(k, to, frm):
        return remote(win_part.at[to], win_sum.at[frm], b_send.at[k], b_recv.at[frm], {"seq": to})

    @pl.loop(1, SEQ)
    def _(k):
        b_copy(k, lax.rem(me + k, SEQ), me).start()

    win_sum[me] = win_part[me]

    @pl.loop(1, SEQ)
    def _(k):
        b_copy(k, me, lax.rem(me + k, SEQ)).wait_recv()

    all_in = win_sum[...]
    weights = jnp.where(
        (lax.broadcasted_iota(jnp.int32, all_in.shape, 1) < 8) | (lane_iota(all_in.shape) < 192),
        all_in,
        0.0,
    )
    in_squares = jnp.sum(jnp.sum(weights * weights, axis=0), axis=0, keepdims=True)
    vec_total = jnp.sum(all_in, axis=0)[8:, 128:]
    vec_total = jnp.where(lane_iota(vec_total.shape) >= 64, vec_total, 0.0)
    vec_squares = jnp.sum(vec_total * vec_total, axis=0, keepdims=True)
    row = (
        in_squares[:, :128]
        + in_squares[:, 128:]
        + vec_squares
        + squares[:, :128]
        + squares[:, 128:256]
        + squares[:, 256:384]
        + squares[:, 384:]
    )
    tile_a[...] = jnp.broadcast_to(row, (8, 128))

    def ta_copy(k, to, frm):
        return remote(tile_a, got_a.at[frm], ta_send.at[k], ta_recv.at[frm], {"seq": to})

    def tb_copy(k, to, frm):
        return remote(tile_b, got_b.at[frm], tb_send.at[k], tb_recv.at[frm], {"dp": to})

    @pl.loop(1, SEQ)
    def _(k):
        ta_copy(k, lax.rem(me + k, SEQ), me).start()

    got_a[me] = tile_a[...]

    @pl.loop(1, SEQ)
    def _(k):
        ta_copy(k, me, lax.rem(me + k, SEQ)).wait_recv()

    tile_b[...] = jnp.sum(got_a[...], axis=0)

    @pl.loop(1, DP)
    def _(k):
        tb_copy(k, lax.rem(dm + k, DP), dm).start()

    got_b[dm] = tile_b[...]

    @pl.loop(1, DP)
    def _(k):
        tb_copy(k, dm, lax.rem(dm + k, DP)).wait_recv()

    everything = jnp.sum(got_b[...], axis=0)
    square_ref[...] = jnp.broadcast_to(jnp.sum(everything, axis=1, keepdims=True), (8, 128))

    hg_finish(grad_sum)
    in_tree.sent()
    out_tree.sent()

    @pl.loop(1, DP)
    def _(k):
        to = lax.rem(dm + k, DP)
        g_copy(k, to, dm).wait_send()
        go_copy(k, to, dm).wait_send()
        tb_copy(k, to, dm).wait_send()

    @pl.loop(1, SEQ)
    def _(k):
        to = lax.rem(me + k, SEQ)
        a_copy(k, to, me).wait_send()
        b_copy(k, to, me).wait_send()
        ta_copy(k, to, me).wait_send()


def layer_call(span, inv, length, x, cot, w_in, w_out, vectors):
    freqs = np.float32(THETA_BASE) ** (-2.0 * np.arange(ROT // 2) / ROT)
    angles = np.arange(ROW, dtype=np.float32)[None, :] * freqs.astype(np.float32)[:, None]
    cosine, sine = np.cos(angles).astype(np.float32), np.sin(angles).astype(np.float32)
    smem = pl.BlockSpec(memory_space=pltpu.SMEM)
    vmem = pl.BlockSpec(memory_space=pltpu.VMEM)
    sds = jax.ShapeDtypeStruct
    dma = pltpu.SemaphoreType.DMA

    def buf(shape, dtype=BF16):
        return pltpu.VMEM(shape, dtype)

    return pl.pallas_call(
        layer_kernel,
        out_shape=(
            sds((TOK, D), F32),
            sds((TOK, D), F32),
            sds((SEQ, 16, 256), F32),
            sds((5, 16, 512), F32),
            sds((8, 128), F32),
            sds((16, D), F32),
        ),
        in_specs=[smem] * 3 + [vmem] * 7,
        out_specs=[vmem] * 6,
        scratch_shapes=[
            buf((32, SPAN, D)),
            buf((32, SPAN, D)),
            buf((SEQ, 16, 256)),
            buf((DP, SEQ, 16, 256)),
            buf((40, 16, 512)),
            buf((4, 8, 16, 512)),
            buf((128, 128), F32),
            buf((ROW, D)),
            buf((ROW, D)),
            buf((D, 256)),
            buf((D, 256)),
            buf((D, 256)),
            buf((D, 256)),
            buf((64, D)),
            buf((256, D)),
            buf((128, ROW)),
            buf((ROW, 128)),
            buf((64, ROW)),
            buf((ROW, 128)),
            buf((64, ROW)),
            buf((ROW, 128)),
            buf((64, ROW)),
            buf((ROW, 64)),
            buf((64, ROW), F32),
            buf((8, ROW), F32),
            buf((8, ROW), F32),
            buf((32, SPAN, 256)),
            buf((256, ROW)),
            buf((ROW, 256), F32),
            buf((32, SPAN, 256)),
            buf((256, ROW)),
            buf((32, SPAN, 256)),
            buf((256, ROW)),
            buf((32, SPAN, HEAD)),
            buf((64, ROW)),
            buf((64, ROW), F32),
            buf((ROW, 64), F32),
            buf((ROW, 64), F32),
            buf((D, 128), F32),
            buf((D, 128), F32),
            buf((DP, SEQ, 16, 256)),
            buf((8, 16, 512)),
            buf((32, 16, 512)),
            buf((8, 2, SPAN, D)),
            buf((8, 2, SPAN, D)),
            buf((8, 2, SPAN, D)),
            buf((8, 2, SPAN, D)),
            buf((DP, SEQ, 16, 256)),
            buf((40, 16, 512)),
            buf((DP, 5, 16, 512)),
            buf((SEQ, 16, 256), F32),
            buf((8, 128), F32),
            buf((8, 128), F32),
            buf((SEQ, 8, 128), F32),
            buf((DP, 8, 128), F32),
            dma((2,)),
            dma((SEQ,)),
            dma((SEQ,)),
            dma((32,)),
            dma((SEQ, 2)),
            dma((32,)),
            dma((SEQ, 2)),
            dma((16,)),
            dma((DP, 2)),
            dma((16,)),
            dma((DP, 2)),
            dma((4,)),
            dma((4,)),
            dma((8,)),
            dma((8,)),
            dma((8,)),
            dma((8,)),
            dma((8,)),
            dma((8,)),
            dma((8,)),
            dma((8,)),
            dma((DP,)),
            dma((DP,)),
            dma((4,)),
            dma((4,)),
            dma((DP,)),
            dma((DP,)),
            dma((SEQ,)),
            dma((SEQ,)),
            dma((SEQ,)),
            dma((SEQ,)),
            dma((DP,)),
            dma((DP,)),
        ],
        compiler_params=pltpu.CompilerParams(
            collective_id=0, has_side_effects=True, vmem_limit_bytes=VMEM_LIMIT
        ),
        name="layer_of_one_row",
    )(span, inv, length, x, cot, w_in, w_out, vectors, jnp.asarray(cosine), jnp.asarray(sine))


def adam(weight, grad, first, second, factor, rate, decay):
    clipped = grad * factor
    first_new = BETA_ONE * first + (1.0 - BETA_ONE) * clipped
    second_new = BETA_TWO * second + (1.0 - BETA_TWO) * clipped * clipped
    first_hat = first_new / (1.0 - BETA_ONE**STEP)
    second_hat = second_new / (1.0 - BETA_TWO**STEP)
    weight_new = weight * (1.0 - rate * decay) - rate * first_hat / (
        jnp.sqrt(second_hat) + ADAM_EPS
    )
    return (weight_new, first_new, second_new)


def update_kernel(
    span_ref,
    len_ref,
    x_ref,
    cot_ref,
    out_sum,
    grad_sum,
    vec_ref,
    win_sum,
    wout_sum,
    square_ref,
    w_in,
    w_out,
    vectors,
    in_first,
    out_first,
    vec_first,
    in_second,
    out_second,
    vec_second,
    block_out,
    input_grad,
    norm_ref,
    new_in,
    new_out,
    new_vec,
    new_in_first,
    new_out_first,
    new_vec_first,
    new_in_second,
    new_out_second,
    new_vec_second,
    low_in,
    low_out,
    low_vec,
    grad_in,
    small,
):
    me = lax.axis_index("seq")
    x_rows = x_ref[...].astype(F32)
    block_out[...] = (x_rows + out_sum[...] + (vec_ref[7:8] + vec_ref[8:9])).astype(BF16)
    centered = x_rows - jnp.mean(x_rows, axis=-1, keepdims=True)
    inv_std = lax.rsqrt(jnp.mean(centered * centered, axis=-1, keepdims=True) + NORM_EPS)
    x_hat = centered * inv_std
    row = lax.broadcasted_iota(jnp.int32, (TOK, 1), 0)
    place = jnp.where(row < SPAN, span_ref[2 * me] * SPAN + row, span_ref[2 * me + 1] * SPAN + row - SPAN)
    cot = jnp.where(place < len_ref[0], cot_ref[...].astype(F32), 0.0)
    grad = grad_sum[...]
    back = (
        grad
        - jnp.mean(grad, axis=-1, keepdims=True)
        - x_hat * jnp.mean(grad * x_hat, axis=-1, keepdims=True)
    )
    input_grad[...] = (cot + inv_std * back).astype(BF16)

    norm = jnp.sqrt(square_ref[...])
    norm_ref[...] = norm
    factor = jnp.minimum(1.0, CLIP_NORM / norm)[0:1, 0:1]

    for s in range(SEQ):
        for j, p in enumerate(PIECES[s]):
            p = int(p)
            if j < 3:
                piece = win_sum[s, 8:16, 64 * j : 64 * j + 64]
            else:
                piece = win_sum[s, 0:8, 64 * (j - 3) : 64 * (j - 3) + 64]
            grad_in[:, 64 * p : 64 * p + 64] = piece
    new, first, second = adam(
        w_in[...], grad_in[...], in_first[...], in_second[...], factor, RATE_MATRIX, DECAY_RATE
    )
    new_in[...] = new
    new_in_first[...] = first
    new_in_second[...] = second
    low_in[...] = new.astype(BF16)

    grad_out = jnp.concatenate([unfold(wout_sum[u]) for u in range(5)], axis=0)
    new, first, second = adam(
        w_out[...], grad_out, out_first[...], out_second[...], factor, RATE_MATRIX, DECAY_RATE
    )
    new_out[...] = new
    new_out_first[...] = first
    new_out_second[...] = second
    low_out[...] = new.astype(BF16)

    small[...] = jnp.zeros((128, 128), F32)
    small[0:8, :] = jnp.sum(win_sum[:, 8:16, 128:256], axis=0)
    grad_vec = jnp.transpose(small[...])[64 : 64 + VEC_ROWS, 0:8]
    new, first, second = adam(
        vectors[...], grad_vec, vec_first[...], vec_second[...], factor, RATE_VECTOR, 0.0
    )
    new_vec[...] = new
    new_vec_first[...] = first
    new_vec_second[...] = second
    low_vec[...] = new.astype(BF16)


def update_call(*args):
    smem = pl.BlockSpec(memory_space=pltpu.SMEM)
    vmem = pl.BlockSpec(memory_space=pltpu.VMEM)
    sds = jax.ShapeDtypeStruct
    matrices = ((8, 7 * D), (40, D), (VEC_ROWS, 8))
    return pl.pallas_call(
        update_kernel,
        out_shape=(sds((TOK, D), BF16), sds((TOK, D), BF16), sds((8, 128), F32))
        + tuple(sds(m, F32) for m in matrices * 3)
        + tuple(sds(m, BF16) for m in matrices),
        in_specs=[smem] * 2 + [vmem] * (len(args) - 2),
        out_specs=[vmem] * 15,
        scratch_shapes=[pltpu.VMEM((8, 7 * D), F32), pltpu.VMEM((128, 128), F32)],
        compiler_params=pltpu.CompilerParams(vmem_limit_bytes=32 * 1024 * 1024),
        name="clipped_update",
    )(*args)


def body(
    hidden_in,
    out_cot,
    in_weight,
    out_weight,
    vectors,
    in_first,
    in_second,
    out_first,
    out_second,
    vec_first,
    vec_second,
    lengths,
    span_of,
):
    span = span_of.reshape(32)
    blocks = jnp.arange(32, dtype=jnp.int32)
    inv = jnp.sum(jnp.where(span[None, :] == blocks[:, None], blocks[None, :], 0), axis=1)
    out_sum, grad_sum, win_sum, wout_sum, squares, vec_full = layer_call(
        span, inv, lengths, hidden_in[0], out_cot[0], in_weight, out_weight, vectors
    )
    outs = update_call(
        span,
        lengths,
        hidden_in[0],
        out_cot[0],
        out_sum,
        grad_sum,
        vec_full,
        win_sum,
        wout_sum,
        squares,
        in_weight,
        out_weight,
        vectors,
        in_first,
        out_first,
        vec_first,
        in_second,
        out_second,
        vec_second,
    )
    return (outs[0][None], outs[1][None], outs[2][0, 0]) + tuple(outs[3:])


def solution(mesh):
    tokens = P("dp", "seq", None)
    matrix = P(("seq", "dp"), None)
    vector = P(None, ("seq", "dp"))
    return jax.shard_map(
        body,
        mesh=mesh,
        in_specs=(
            tokens,
            tokens,
            matrix,
            matrix,
            vector,
            matrix,
            matrix,
            matrix,
            matrix,
            vector,
            vector,
            P("dp"),
            P(),
        ),
        out_specs=(tokens, tokens, P()) + (matrix, matrix, vector) * 4,
        check_vma=False,
    )
```

time: 378 us -> 180 us (0.48)
  local copies, waits for them, and re-layouts: 112 us -> 15 us
  Pallas kernels: 239 us -> 163 us
  other arithmetic: 21.6 us -> 0.63 us
    another operation x116 -> x0, local copies, waits for them, and re-layouts: 105 us -> none  [the longest x113 105 us: unpack_in(): jnp.stack([pieces[where[p][0], :, where[p][1]] for p in range(112)], axis=1)]
    pallas_call x3 -> x2, Pallas kernels: 239 us -> 163 us  [the longest x1 160 us: layer_call(): pl.pallas_call(layer_kernel, out_shape=(sds((TOK, D), F32), sds((TOK, D),...]
    unnamed x20 -> x50, local copies, waits for them, and re-layouts: 0.82 us -> 14.4 us
    convert_element_type x7 -> x0, other arithmetic: 8.33 us -> none  [the longest x1 2.13 us: body(): new_in.astype(BF16)]
    reduce_sum x5 -> x1, other arithmetic: 5.06 us -> 0.63 us  [body(): jnp.sum(jnp.where(span[None, :] == blocks[:, None], blocks[None, :], 0),...]
    slice x18 -> x1, local copies, waits for them, and re-layouts: 4.45 us -> 0.51 us  [body(): return (outs[0][None], outs[1][None], outs[2][0, 0]) + tuple(outs[3:])]
where the time goes in v2:
time: 180 us
  Pallas kernels  163 us (91%)
  local copies, waits for them, and re-layouts  15 us (8%)
    pallas_call x1, Pallas kernels, layer_call(): pl.pallas_call(layer_kernel, out_shape=(sds((TOK, D), F32), sds((TOK, D),...  160 us
    unnamed x50, local copies, waits for them, and re-layouts  14.4 us

profile of v2, /device:TPU:1, one launch (start us, length us, event | category | flops | bytes accessed | tf_op | source)
XLA Modules:
  0.0 179.8 jit_solution(4209405418548543730)
XLA Ops:
  0.6 0.0 copy-start.17
  1.3 0.0 copy-done.17
  1.3 0.0 copy-start.18
  1.3 0.7 copy.49.vectors_ref.vectors
  2.0 0.0 copy-done.18
  2.0 0.0 copy-start.19
  2.0 0.1 copy.51.vec_first
  2.1 0.6 copy-done.19
  2.7 0.0 copy-start.20
  2.7 0.1 copy.52.vec_second
  2.8 0.6 copy-done.20
  3.4 0.0 copy-start.9
  3.4 0.1 copy.48
  3.5 0.1 reshape.34.span_ref
  3.6 0.0 copy-start.14
  3.6 0.6 select_reduce_fusion.inv_ref
  4.2 0.0 copy-done.14
  4.2 0.0 copy-start
  4.2 0.0 copy-start.1
  4.2 0.0 copy-start.2
  4.2 0.0 copy-start.3
  4.2 160.4 %layer_of_one_row.1 = (f32[128,1024]{1,0:T(8,128)}, f32[128,1024]{1,0:T(8,128)}, f32[16,16,256]{2,1,0:T(8,128)}, f32[5,16,512]{2,1,0:T(8,128)}, f32[8,128]{1,0:T(8,128)}, /*index=5*/f32[16,1024]{1,0:T(8,128)}) custom-call(s32[32]{0:T(128)} %copy-done.14, s32[32]{0:T(128)} %select_reduce_fusion.inv_ref, s32[1]{0:T(128)S(6)} %copy.57.len_ref, ...), custom_call_target="tpu_custom_call" | custom-call | tf_op jit(solution)/shard_map/layer_of_one_row/pallas_call | solution.py:1012
  164.7 0.0 copy-start.12
  164.7 0.0 copy-done.9
  164.7 0.0 copy-done
  164.7 0.0 copy-done.1
  164.7 0.0 copy-done.2
  164.7 0.0 copy-done.3
  164.7 0.6 copy-done.12
  165.4 0.0 copy-start.4
  165.4 1.0 copy-done.4
  166.4 0.0 copy-start.5
  166.4 1.0 copy-done.5
  167.5 0.0 copy-start.6
  167.5 0.9 copy-done.6
  168.4 0.9 copy-done.7
  169.4 0.9 copy-done.8
  170.3 0.9 copy-done.10
  171.2 0.9 copy-done.11
  172.1 0.8 copy-done.13
  173.0 0.7 copy-done.15
  173.6 0.7 copy-done.16
  174.3 2.4 %clipped_update.1 = (bf16[128,1024]{1,0:T(8,128)(2,1)}, bf16[128,1024]{1,0:T(8,128)(2,1)}, f32[8,128]{1,0:T(8,128)S(1)}, f32[8,7168]{1,0:T(8,128)}, f32[40,1024]...) custom-call(s32[32]{0:T(128)S(1)} %copy-done.15, ...), custom_call_target="tpu_custom_call" | custom-call | tf_op jit(solution)/shard_map/clipped_update/pallas_call | solution.py:1234
  176.7 0.5 slice.3
  177.2 0.7 copy.56
  177.8 0.7 copy.53
  178.5 0.7 copy.54
  179.2 0.7 copy.55
  (7 shorter events, 0.0 us)
Async XLA Ops:
  0.6 0.7 copy-start.17
  1.3 0.7 copy-start.18
  2.0 0.7 copy-start.19
  2.7 0.7 copy-start.20
  3.4 161.3 %copy-start.9 = (f32[40,1024]{1,0:T(8,128)S(1)}, f32[40,1024]{1,0:T(8,128)}, u32[]{:S(2)}) copy-start(f32[40,1024]{1,0:T(8,128)} %out_first.1) | copy-start | bytes 491524
  3.6 0.6 copy-start.14
  4.2 160.5 %copy-start = (bf16[1,128,1024]{2,1,0:T(8,128)(2,1)S(1)}, bf16[1,128,1024]{2,1,0:T(8,128)(2,1)}, u32[]{:S(2)}) copy-start(bf16[1,128,1024]{2,1,0:T(8,128)(2,1)} %param.15) | copy-start | bytes 786436
  4.2 160.5 %copy-start.1 = (bf16[1,128,1024]{2,1,0:T(8,128)(2,1)S(1)}, bf16[1,128,1024]{2,1,0:T(8,128)(2,1)}, u32[]{:S(2)}) copy-start(bf16[1,128,1024]{2,1,0:T(8,128)(2,1)} %param.16) | copy-start | bytes 786436
  4.2 160.5 %copy-start.2 = (f32[8,7168]{1,0:T(8,128)S(1)}, f32[8,7168]{1,0:T(8,128)}, u32[]{:S(2)}) copy-start(f32[8,7168]{1,0:T(8,128)} %w_in.1) | copy-start | bytes 688132
  4.2 160.5 %copy-start.3 = (f32[40,1024]{1,0:T(8,128)S(1)}, f32[40,1024]{1,0:T(8,128)}, u32[]{:S(2)}) copy-start(f32[40,1024]{1,0:T(8,128)} %w_out.1) | copy-start | bytes 491524
  164.7 0.7 copy-start.12
  165.4 1.0 copy-start.4
  166.4 1.0 copy-start.5
  167.5 0.9 copy-start.6
  168.4 0.9 copy-start.7
  169.4 0.9 copy-start.8
  170.3 0.9 copy-start.10
  171.2 0.9 copy-start.11
  172.1 0.8 copy-start.13
  173.0 0.7 copy-start.15
  173.6 0.7 copy-start.16

commit v3 on v2

v3 whole, which is shorter than its diff:
```python
import functools
import math

import jax
import jax.numpy as jnp
import numpy as np
from jax import lax
from jax.experimental import pallas as pl
from jax.experimental.pallas import tpu as pltpu
from jax.sharding import PartitionSpec as P

D = 1024
FF = 4096
HEADS = 16
HEAD = 64
ROT = 16
STEP = 5
SEQ = 16
DP = 8
TOK = 128
ROW = 2048
SPAN = 64
VEC_ROWS = 13

NORM_EPS = 1e-05
NEG_FILL = -1e30
CLIP_NORM = 1.0
RATE_MATRIX = 0.02
RATE_VECTOR = 0.2
BETA_ONE = 0.5
BETA_TWO = 0.5
DECAY_RATE = 0.1
ADAM_EPS = 1e-08
THETA_BASE = 10000.0

F32 = jnp.float32
BF16 = jnp.bfloat16
MESH = pl.DeviceIdType.MESH
VMEM_LIMIT = 60 * 1024 * 1024
UPDATE_LIMIT = 60 * 1024 * 1024


def head_of(s):
    if s < 4:
        return 5 * s
    return 5 * ((s - 4) // 4) + 1 + (s - 4) % 4


def hidden_pieces(s):
    if s < 3:
        return [20 * s + 5 * r + 8 for r in range(4)]
    if s == 3:
        return [0, 1, 2, 3]
    return [5 * s - 16 + r for r in range(4)]


def column_pieces():
    rows = []
    for s in range(SEQ):
        h = head_of(s)
        rows.append([h, 16 + h, 32 + h] + [48 + w for w in hidden_pieces(s)])
    return np.array(rows, np.int32)


PIECES = column_pieces()


def head_index(s):
    late = (s + 12) // 16
    return (1 - late) * (5 * s) + late * (5 * ((s - 4) // 4) + 1 + lax.rem(s, 4))


def hidden_index(s, r):
    late, not_few = (s + 12) // 16, (s + 13) // 16
    return (
        (1 - not_few) * (20 * s + 5 * r + 8) + (not_few - late) * r + late * (5 * s - 16 + r)
    )


def remote(src, dst, send, recv, where):
    return pltpu.make_async_remote_copy(
        src_ref=src, dst_ref=dst, send_sem=send, recv_sem=recv, device_id=where, device_id_type=MESH
    )


def greet(me, dm):
    barrier = pltpu.get_barrier_semaphore()

    @pl.loop(1, SEQ)
    def _(k):
        pl.semaphore_signal(
            barrier, inc=1, device_id={"seq": lax.rem(me + k, SEQ)}, device_id_type=MESH
        )

    @pl.loop(1, DP)
    def _(k):
        pl.semaphore_signal(
            barrier, inc=1, device_id={"dp": lax.rem(dm + k, DP)}, device_id_type=MESH
        )


def await_greetings():
    pl.semaphore_wait(pltpu.get_barrier_semaphore(), SEQ + DP - 2)


class Tree:
    def __init__(self, axis, piece, me, turn, mate, sib, send, recv, over_mate):
        self.axis, self.piece, self.me, self.turn, self.mate, self.sib = (
            axis,
            piece,
            me,
            turn,
            mate,
            sib,
        )
        self.send, self.recv, self.over_mate = send, recv, over_mate
        self.started = []

    def put(self, slot, h, to):
        part = self.piece(slot, h)
        copy = remote(
            part, part, self.send.at[len(self.started)], self.recv.at[slot, h], {self.axis: to}
        )
        copy.start()
        self.started.append(copy)

    def hand(self, slot, h):
        if self.sib is not None:
            self.put(slot, h, self.sib)

    def got(self, slot, h):
        part = self.piece(slot, h)
        remote(
            part, part, self.send.at[0], self.recv.at[slot, h], {self.axis: self.mate}
        ).wait_recv()

    def own_to_ring(self):
        for h in range(2):
            for k in (1, 3):
                self.put(self.me, h, self.turn(self.me, k))

    def own_to_mate(self):
        for h in range(2):
            self.put(self.me, h, self.mate)
        for h in range(2):
            self.hand(self.me, h)

    def of_mate(self):
        for h in range(2):
            self.got(self.mate, h)
            for k in (1, 3):
                self.put(self.mate, h, self.turn(self.me, k))
            self.hand(self.mate, h)

    def near(self, base):
        for h in range(2):
            for k in (3, 1):
                slot = self.turn(base, k)
                self.got(slot, h)
                if (k == 3) == (h == 0):
                    self.put(slot, h, self.turn(self.me, 4 - k))
                self.hand(slot, h)

    def near_of_me(self):
        self.near(self.me)

    def far_of_me(self):
        slot = self.turn(self.me, 2)
        for h in range(2):
            self.got(slot, h)
            if self.over_mate:
                self.put(slot, h, self.mate)
            self.hand(slot, h)

    def near_of_mate(self):
        if not self.over_mate:
            return self.near(self.mate)
        for h in range(2):
            for k in (3, 1):
                slot = self.turn(self.mate, k)
                self.got(slot, h)
                self.hand(slot, h)

    def far_of_mate(self):
        slot = self.turn(self.mate, 2)
        for h in range(2):
            self.got(slot, h)
            self.hand(slot, h)

    def handed(self, other_mate):
        for h in range(2):
            for slot in (self.sib, other_mate):
                for k in range(4):
                    self.got(self.turn(slot, k), h)

    def sent(self):
        for copy in self.started:
            copy.wait_send()


class SumTree:
    def __init__(self, axis, piece, land, me, turn, mate, send, recv):
        self.axis, self.piece, self.land, self.me, self.turn, self.mate = (
            axis,
            piece,
            land,
            me,
            turn,
            mate,
        )
        self.send, self.recv = send, recv
        self.started = []

    def put(self, slot, kind, h, to):
        copy = remote(
            self.piece(slot, h),
            self.land(kind, h),
            self.send.at[len(self.started)],
            self.recv.at[kind, h],
            {self.axis: to},
        )
        copy.start()
        self.started.append(copy)

    def got(self, kind, h):
        part = self.land(kind, h)
        remote(
            part, part, self.send.at[0], self.recv.at[kind, h], {self.axis: self.mate}
        ).wait_recv()
        return part[...].astype(F32)

    def add(self, slot, h, *kinds):
        part = self.piece(slot, h)
        total = part[...].astype(F32)
        for kind in kinds:
            total = total + self.got(kind, h)
        part[...] = total.astype(BF16)

    def far_of_mate(self):
        for h in range(2):
            self.put(self.turn(self.mate, 2), 0, h, self.mate)

    def near_of_mate(self, k):
        for h in range(2):
            self.put(self.turn(self.mate, k), 2 if k == 1 else 1, h, self.turn(self.me, k))

    def near_early(self, k):
        h = 0 if k == 1 else 1
        self.put(self.turn(self.me, k), 5 if k == 1 else 4, h, self.turn(self.me, k))

    def far_of_me(self):
        slot = self.turn(self.me, 2)
        for h in range(2):
            self.add(slot, h, 0)
            self.put(slot, 3, h, self.turn(self.me, 3 - 2 * h))

    def near_late(self):
        for h in range(2):
            k = 3 - 2 * h
            slot = self.turn(self.me, k)
            self.add(slot, h, 3)
            self.put(slot, 4 + h, h, self.turn(self.me, k))

    def of_mate(self):
        for h in range(2):
            self.add(self.mate, h, 1, 2)
            self.put(self.mate, 6, h, self.mate)

    def begin(self):
        self.far_of_mate()
        for k in (1, 3):
            self.near_of_mate(k)
        for k in (1, 3):
            self.near_early(k)

    def total(self, h):
        value = self.piece(self.me, h)[...].astype(F32)
        for kind in (4, 5, 6):
            value = value + self.got(kind, h)
        return value

    def sent(self):
        for copy in self.started:
            copy.wait_send()


def dot(a, b):
    return jnp.dot(a, b, preferred_element_type=F32)


def dot_nt(a, b):
    return lax.dot_general(a, b, (((1,), (1,)), ((), ())), preferred_element_type=F32)


def lane_iota(shape):
    return lax.broadcasted_iota(jnp.int32, shape, len(shape) - 1)


def fold(u):
    return jnp.concatenate([u[:, : D // 2], u[:, D // 2 :]], axis=0)


def unfold(u):
    return jnp.concatenate([u[:8], u[8:]], axis=1)


CH = 512
NCH = ROW // CH


def layer_kernel(
    span_ref,
    len_ref,
    x_ref,
    cot_ref,
    w_in_ref,
    w_out_ref,
    vectors_ref,
    cos_ref,
    sin_ref,
    out_sum,
    grad_sum,
    f_sum,
    q_sum,
    wout_sum,
    square_ref,
    vec_ref,
    vec_grad,
    inv_ref,
    xh_all,
    cot_all,
    win_own,
    win_all,
    wout_all,
    swap_all,
    small,
    xs,
    cs,
    wr,
    wp,
    wo,
    qt,
    qn,
    kt,
    kn,
    vt,
    vn,
    dot_t,
    dot_n,
    ot,
    lse,
    delta,
    joined,
    joined_t,
    dact,
    mixed,
    mixed_t,
    dqt,
    dkn,
    dvn,
    vg,
    goa_buf,
    gof_buf,
    own_out,
    gf,
    gq,
    po_sib,
    hg_sib,
    po_land,
    hg_land,
    gf_land,
    gq_got,
    vt_part,
    vt_seq,
    vt_own,
    vt_dp,
    go_land,
    f_part,
    q_part,
    tile_b,
    got_b,
    local_sem,
    a_send,
    a_recv,
    x_send,
    x_recv,
    c_send,
    c_recv,
    l_send,
    l_recv,
    o_send,
    o_recv,
    w_send,
    w_recv,
    ps_send,
    ps_recv,
    p_send,
    p_recv,
    hs_send,
    hs_recv,
    h_send,
    h_recv,
    gf_send,
    gf_recv,
    gq_send,
    gq_recv,
    go_send,
    go_recv,
    v_send,
    v_recv,
    bf_send,
    bf_recv,
    bq_send,
    bq_recv,
    vs_send,
    vs_recv,
    vd_send,
    vd_recv,
    tb_send,
    tb_recv,
):
    me = lax.axis_index("seq")
    dm = lax.axis_index("dp")
    core = lax.rem(me, 2)
    chip = me // 2
    sib = me + 1 - 2 * core
    mate = me + 2 - 4 * lax.rem(chip, 2)
    sib_mate = mate + 1 - 2 * core
    dp_mate = lax.rem(dm + 4, DP)
    head = head_index(me)
    greet(me, dm)

    row = lax.broadcasted_iota(jnp.int32, (TOK, 1), 0)
    place = jnp.where(row < SPAN, span_ref[0, me] * SPAN + row, span_ref[1, me] * SPAN + row - SPAN)
    x_rows = x_ref[...].astype(F32)
    centered = x_rows - jnp.mean(x_rows, axis=-1, keepdims=True)
    inv_std = lax.rsqrt(jnp.mean(centered * centered, axis=-1, keepdims=True) + NORM_EPS)
    xh_all[pl.ds(2 * me, 2)] = (centered * inv_std).astype(BF16).reshape(2, SPAN, D)

    small[...] = jnp.zeros((128, 128), F32)
    small[0:8, 0:VEC_ROWS] = vectors_ref[...]
    vec_t = small[0:8, 0:64]
    for s in range(SEQ):
        take = [w_in_ref[:, 64 * int(p) : 64 * int(p) + 64] for p in PIECES[s]]
        qkv = jnp.concatenate(take[:3] + [vec_t], axis=1)
        win_own[s] = jnp.concatenate([jnp.concatenate(take[3:], axis=1), qkv], axis=0).astype(BF16)
    for u in range(5):
        wout_all[5 * dm + u] = fold(w_out_ref[8 * u : 8 * u + 8]).astype(BF16)
    cot_own = jnp.where(place < len_ref[0], cot_ref[...].astype(F32), 0.0)
    cot_all[pl.ds(2 * me, 2)] = cot_own.astype(BF16).reshape(2, SPAN, D)
    cot_sum = jnp.sum(cot_own, axis=0, keepdims=True)
    vg[...] = jnp.transpose(jnp.broadcast_to(cot_sum, (128, D)))
    keep = pltpu.make_async_copy(win_own.at[me], win_all.at[dm, me], local_sem.at[0])
    keep.start()

    @pl.loop(0, 32)
    def _(i):
        slot = jnp.int32(0)
        for s in range(SEQ):
            for j in range(2):
                slot = jnp.maximum(slot, jnp.where(span_ref[j, s] == i, 2 * s + j, 0))
        inv_ref[i] = slot

    def seq_turn(s, k):
        return lax.rem(s + 4 * k, SEQ)

    def dp_turn(d, k):
        return d // 4 * 4 + lax.rem(d + k, 4)

    x_tree = Tree(
        "seq",
        lambda slot, h: xh_all.at[2 * slot + h],
        me,
        seq_turn,
        mate,
        sib,
        x_send,
        x_recv,
        True,
    )
    cot_tree = Tree(
        "seq",
        lambda slot, h: cot_all.at[2 * slot + h],
        me,
        seq_turn,
        mate,
        sib,
        c_send,
        c_recv,
        True,
    )
    in_tree = Tree(
        "dp",
        lambda slot, h: win_all.at[slot, pl.ds(8 * h, 8)],
        dm,
        dp_turn,
        dp_mate,
        None,
        l_send,
        l_recv,
        False,
    )
    out_tree = Tree(
        "dp",
        lambda slot, h: wout_all.at[pl.ds(5 * slot + 2 * h, 2 + h)],
        dm,
        dp_turn,
        dp_mate,
        None,
        o_send,
        o_recv,
        False,
    )

    def a_copy(k, to, frm):
        return remote(
            win_own.at[to], win_all.at[dm, frm], a_send.at[k], a_recv.at[frm], {"seq": to}
        )

    await_greetings()

    @pl.loop(1, SEQ)
    def _(k):
        a_copy(k, lax.rem(me + k, SEQ), me).start()

    x_tree.own_to_mate()
    x_tree.own_to_ring()
    out_tree.own_to_mate()
    out_tree.own_to_ring()
    keep.wait()

    @pl.loop(1, SEQ)
    def _(k):
        a_copy(k, me, lax.rem(me + k, SEQ)).wait_recv()

    in_tree.own_to_mate()
    in_tree.own_to_ring()
    x_tree.near_of_me()
    x_tree.of_mate()
    out_tree.of_mate()
    out_tree.near_of_me()
    x_tree.far_of_me()
    cot_tree.own_to_ring()
    cot_tree.own_to_mate()
    in_tree.of_mate()
    in_tree.near_of_me()
    out_tree.near_of_mate()
    in_tree.near_of_mate()
    x_tree.near_of_mate()
    in_tree.far_of_me()
    in_tree.far_of_mate()
    out_tree.far_of_me()
    out_tree.far_of_mate()

    def swap_few(r):
        return remote(
            wout_all.at[pl.ds(8 + 8 * r, 8)],
            swap_all.at[0],
            w_send.at[r],
            w_recv.at[0],
            {"seq": 4 + 4 * me + r},
        )

    def swap_many():
        return remote(
            wout_all.at[pl.ds(32, 8)],
            swap_all.at[lax.rem(me, 4)],
            w_send.at[0],
            w_recv.at[lax.rem(me, 4)],
            {"seq": (me - 4) // 4},
        )

    @pl.when(me < 3)
    def _():
        for r in range(4):
            swap_few(r).start()

    @pl.when(me > 3)
    def _():
        swap_many().start()

    def unpack(sb, carry):
        cq, cf = carry
        tiles = [win_all[d, sb].astype(F32) for d in range(DP)]
        ff = jnp.concatenate([t[:8] for t in tiles], axis=0)
        qk = jnp.concatenate([t[8:] for t in tiles], axis=0)
        rows = pl.ds(pl.multiple_of(sb * 64, 64), 64)
        gain_a, bias_a, gain_m, bias_m = (qk[:, 192 + i : 193 + i] for i in range(4))
        wr[rows] = jnp.concatenate([ff, qk], axis=1).astype(BF16)
        folded = jnp.where(lane_iota(qk.shape) < 192, qk * gain_a, 0.0)
        wp[rows] = jnp.concatenate([ff * gain_m, folded], axis=1).astype(BF16)
        return (
            cq + jnp.sum(qk * bias_a, axis=0, keepdims=True),
            cf + jnp.sum(ff * bias_m, axis=0, keepdims=True),
        )

    zero_row = jnp.zeros((1, 256), F32)
    cq, cf = lax.fori_loop(0, SEQ, unpack, (zero_row, zero_row))

    slab = jnp.transpose(wr[:, 384:512].astype(F32))
    vec_ref[...] = slab[64:80]

    hid = []
    for r in range(4):
        w = hidden_index(me, r)
        rows = pl.ds(pl.multiple_of(lax.rem(w, 16) * 64, 64), 64)
        part = wr[rows, 384:512].astype(F32)
        lane = 64 + 9 + w // 16
        hid.append(
            jnp.sum(jnp.where(lane_iota(part.shape) == lane, part, 0.0), axis=1, keepdims=True)
        )
    hid = jnp.concatenate(hid, axis=0)
    cf = cf + jnp.transpose(jnp.broadcast_to(hid, (256, 128)))[0:1]

    head_rows = pl.ds(pl.multiple_of(head * 64, 64), 64)
    head_vecs = wr[head_rows, 384:512].astype(F32)
    bq, bk, bv = (head_vecs[:, 68 + i : 69 + i] for i in range(3))

    x_tree.far_of_mate()
    x_tree.handed(sib_mate)

    @pl.loop(0, 32)
    def _(i):
        rows = pl.ds(pl.multiple_of(i * SPAN, SPAN), SPAN)
        xs[rows] = xh_all[inv_ref[i]]

    cot_tree.of_mate()

    aug = jnp.where(lax.broadcasted_iota(jnp.int32, (64, CH), 0) == 0, 1.0, 0.0)
    zeros_aug = jnp.zeros((64, CH), F32)

    def rotate_t(u, cosine, sine, sign):
        first, second = u[0:8], u[8:16]
        return jnp.concatenate(
            [
                first * cosine - sign * (second * sine),
                second * cosine + sign * (first * sine),
                u[16:],
            ],
            axis=0,
        )

    @pl.loop(0, NCH)
    def _(i):
        start = pl.multiple_of(i * CH, CH)
        rows = pl.ds(start, CH)
        xh = xs[rows]
        first = dot(xh, wp[...])
        qkv = jnp.transpose(first[:, 256:] + cq)
        cosine, sine = cos_ref[:, rows], sin_ref[:, rows]
        q = rotate_t(qkv[0:64] + bq, cosine, sine, 1.0) * 0.125
        k = rotate_t(qkv[64:128] + bk, cosine, sine, 1.0)
        v = qkv[128:192] + bv
        q_full = jnp.concatenate([q, aug], axis=0)
        past = (start + lane_iota((64, CH))) >= len_ref[0]
        k_full = jnp.concatenate([k, jnp.where(past, NEG_FILL, 0.0) * aug], axis=0)
        v_full = jnp.concatenate([v, zeros_aug], axis=0)
        qt[:, rows] = q_full.astype(BF16)
        kt[:, rows] = k.astype(BF16)
        vt[:, rows] = v.astype(BF16)
        qn[rows] = jnp.transpose(q_full).astype(BF16)
        kn[rows] = jnp.transpose(k_full).astype(BF16)
        vn[rows] = jnp.transpose(v_full).astype(BF16)
        pre = first[:, :256] + cf
        cdf = 0.5 * (1.0 + lax.erf(pre * (1.0 / math.sqrt(2.0))))
        pdf = jnp.exp(-0.5 * pre * pre) * (1.0 / math.sqrt(2.0 * math.pi))
        activ = pre * cdf
        joined[pl.ds(8 * i, 8), :, 0:256] = activ.astype(BF16).reshape(8, SPAN, 256)
        joined_t[0:256, rows] = jnp.transpose(activ).astype(BF16)
        dact[rows] = cdf + pre * pdf

    cot_tree.near_of_me()
    causal = lax.broadcasted_iota(jnp.int32, (CH, CH), 0) <= lane_iota((CH, CH))

    def scores(kc, qi):
        s = dot(kn[kc * CH : (kc + 1) * CH], qt[:, qi * CH : (qi + 1) * CH])
        if kc == qi:
            s = jnp.where(causal, s, NEG_FILL)
        return s

    for qi in range(NCH):
        lanes = slice(qi * CH, (qi + 1) * CH)
        parts = [scores(kc, qi) for kc in range(qi + 1)]
        top = functools.reduce(jnp.maximum, [jnp.max(s, axis=0, keepdims=True) for s in parts])
        total = jnp.zeros((1, CH), F32)
        out = jnp.zeros((64, CH), F32)
        for kc, s in enumerate(parts):
            p = jnp.exp(s - top)
            total = total + jnp.sum(p, axis=0, keepdims=True)
            out = out + dot(vt[:, kc * CH : (kc + 1) * CH], p.astype(BF16))
        out = out / total
        ot[:, lanes] = out
        lse[:, lanes] = jnp.broadcast_to(top + jnp.log(total), (8, CH))
        joined_t[256:320, lanes] = out.astype(BF16)
        joined[8 * qi : 8 * qi + 8, :, 256:320] = jnp.transpose(out).astype(BF16).reshape(8, SPAN, HEAD)
        if qi == 2:
            cot_tree.far_of_me()
            cot_tree.near_of_mate()
    def put_units(base, at, count):
        @pl.loop(0, count // 2)
        def _(i):
            pair = [unfold(wout_all[base + 2 * i + j].astype(F32)) for j in range(2)]
            rows = pl.ds(pl.multiple_of(at + i * 16, 16), 16)
            wo[rows] = jnp.concatenate(pair, axis=0).astype(BF16)

    def put_swap(base, rs):
        for r in range(rs):
            for i in range(4):
                pair = [unfold(swap_all[r, 2 * i + j].astype(F32)) for j in range(2)]
                at = base + r * 64 + i * 16
                wo[at : at + 16] = jnp.concatenate(pair, axis=0).astype(BF16)

    @pl.when(me < 4)
    def _():
        put_units(0, 256, 8)

    @pl.when(me < 3)
    def _():
        for r in range(4):
            remote(
                wout_all.at[pl.ds(32, 8)], swap_all.at[r], w_send.at[r], w_recv.at[r], {"seq": sib}
            ).wait_recv()
            swap_few(r).wait_send()
        put_swap(0, 4)

    @pl.when(me == 3)
    def _():
        put_units(8, 0, 32)

    @pl.when(me > 3)
    def _():
        swap_many().wait_send()
        remote(
            wout_all.at[pl.ds(32, 8)], swap_all.at[0], w_send.at[0], w_recv.at[0], {"seq": sib}
        ).wait_recv()
        put_swap(256, 1)
        put_units(0, 0, 32)

    def of_chip(ref, j):
        return jnp.concatenate([ref[span_ref[i % 2, 2 * j + i // 2]] for i in range(4)], axis=0)

    order = [(mate, 2), (mate, 1), (mate, 3), (me, 2), (me, 3), (me, 1), (mate, 0), (me, 0)]

    class ChipSums:
        def __init__(self, part, buf, sib_buf, land, s_send, s_recv, send, recv):
            self.part, self.buf, self.sib_buf = part, buf, sib_buf
            self.s_send, self.s_recv = s_send, s_recv
            self.tree = SumTree(
                "seq",
                lambda slot, h: buf.at[2 * slot + h],
                lambda kind, h: land.at[kind, h],
                me,
                seq_turn,
                mate,
                send,
                recv,
            )

        def to_sib(self, j):
            return remote(
                self.buf.at[pl.ds(4 * j + 2 - 2 * core, 2)],
                self.sib_buf.at[j],
                self.s_send.at[j],
                self.s_recv.at[j],
                {"seq": sib},
            )

        def compute(self, n):
            j = seq_turn(*order[n]) // 2
            self.buf[pl.ds(4 * j, 4)] = self.part(j).astype(BF16).reshape(4, SPAN, D)
            self.to_sib(j).start()

        def pair(self, n):
            j = seq_turn(*order[n]) // 2
            self.to_sib(j).wait_recv()
            mine = pl.ds(4 * j + 2 * core, 2)
            self.buf[mine] = (self.buf[mine].astype(F32) + self.sib_buf[j].astype(F32)).astype(BF16)
            if n == 0:
                self.tree.far_of_mate()
            elif n < 3:
                self.tree.near_of_mate(order[n][1])
            elif n in (4, 5):
                self.tree.near_early(order[n][1])

        def begin(self):
            for n in range(8):
                self.compute(n)
                if n > 2:
                    self.pair(n - 3)
            for n in range(5, 8):
                self.pair(n)

        def finish(self, total):
            for h in range(2):
                total[SPAN * h : SPAN * (h + 1)] = self.tree.total(h)
            self.tree.sent()
            for n in range(8):
                self.to_sib(seq_turn(*order[n]) // 2).wait_send()

    po = ChipSums(
        lambda j: dot(of_chip(joined, j), wo[...]),
        xh_all,
        po_sib,
        po_land,
        ps_send,
        ps_recv,
        p_send,
        p_recv,
    )
    hg = ChipSums(
        lambda j: dot_nt(of_chip(mixed, j), wp[...]),
        cot_all,
        hg_sib,
        hg_land,
        hs_send,
        hs_recv,
        h_send,
        h_recv,
    )
    x_tree.sent()
    po.begin()
    cot_tree.far_of_mate()
    cot_tree.handed(sib_mate)

    @pl.loop(0, 32)
    def _(i):
        rows = pl.ds(pl.multiple_of(i * SPAN, SPAN), SPAN)
        cs[rows] = cot_all[inv_ref[i]]

    @pl.loop(0, NCH)
    def _(i):
        rows = pl.ds(pl.multiple_of(i * CH, CH), CH)
        cot = cs[rows]
        back = dot_nt(cot, wo[...])
        ag = back[:, 256:].astype(BF16).astype(F32)
        ag_t = jnp.transpose(ag)
        dot_n[rows] = ag.astype(BF16)
        dot_t[:, rows] = ag_t.astype(BF16)
        delta[:, rows] = jnp.broadcast_to(
            jnp.sum(ag_t * ot[:, rows], axis=0, keepdims=True), (8, CH)
        )
        pg = back[:, :256] * dact[rows]
        mixed[pl.ds(8 * i, 8), :, 0:256] = pg.astype(BF16).reshape(8, SPAN, 256)
        mixed_t[0:256, rows] = jnp.transpose(pg).astype(BF16)

    @pl.loop(0, 2)
    def _(i):
        left = dot(joined_t[...], cs[:, pl.ds(pl.multiple_of(i * 256, 256), 256)])
        right = dot(joined_t[...], cs[:, pl.ds(pl.multiple_of(i * 256 + 512, 256), 256)])
        units = jnp.concatenate([left.reshape(40, 8, 256), right.reshape(40, 8, 256)], axis=1)
        lanes = pl.ds(pl.multiple_of(i * 256, 256), 256)
        gof_buf[:, :, lanes] = units[:32].astype(BF16)
        goa_buf[:, :, lanes] = units[32:].astype(BF16)

    def back_few(r):
        return remote(
            gof_buf.at[pl.ds(8 * r, 8)],
            own_out.at[pl.ds(32, 8)],
            v_send.at[r],
            v_recv.at[0],
            {"seq": 4 + 4 * me + r},
        )

    def back_many():
        return remote(
            goa_buf,
            own_out.at[pl.ds(8 + 8 * lax.rem(me, 4), 8)],
            v_send.at[0],
            v_recv.at[lax.rem(me, 4)],
            {"seq": (me - 4) // 4},
        )

    keep_a = pltpu.make_async_copy(goa_buf, own_out.at[pl.ds(0, 8)], local_sem.at[0])
    keep_f3 = pltpu.make_async_copy(gof_buf, own_out.at[pl.ds(8, 32)], local_sem.at[1])
    keep_f = pltpu.make_async_copy(gof_buf, own_out.at[pl.ds(0, 32)], local_sem.at[1])

    @pl.when(me < 3)
    def _():
        for r in range(4):
            back_few(r).start()

    @pl.when(me < 4)
    def _():
        keep_a.start()

    @pl.when(me == 3)
    def _():
        keep_f3.start()

    @pl.when(me > 3)
    def _():
        back_many().start()
        keep_f.start()

    def grads_by_owner(dst, base, columns):
        sums = jnp.sum(
            mixed[:, :, base : base + 256].reshape(ROW, 256).astype(F32), axis=0, keepdims=True
        )

        @pl.loop(0, 4)
        def _(i):
            rows = pl.ds(pl.multiple_of(i * 256, 256), 256)
            h = jnp.transpose(dot(mixed_t[base : base + 256], xs[:, rows]))
            raw = wr[rows, base : base + 256].astype(F32)
            vecs = wr[rows, 384:512].astype(F32)
            gain, bias = (vecs[:, columns + 64 + j : columns + 65 + j] for j in range(2))
            grad = gain * h + bias * sums
            lanes = lane_iota((256, 128))
            extra = vg[rows]
            for j, col in enumerate((raw * h, raw * sums)):
                extra = extra + jnp.where(
                    lanes == 64 + columns + j, jnp.sum(col, axis=1, keepdims=True), 0.0
                )
            vg[rows] = extra
            for j in range(2):
                pair = [
                    grad[128 * j + 64 * t : 128 * j + 64 * t + 64].reshape(8, 8, 256)
                    for t in range(2)
                ]
                dst[:, 2 * i + j] = jnp.concatenate(pair, axis=1).astype(BF16)

    def owner_tree(dst, land, send, recv):
        return SumTree(
            "dp",
            lambda slot, h: dst.at[slot, pl.ds(4 * h, 4)],
            lambda kind, h: land.at[kind, pl.ds(4 * h, 4)],
            dm,
            dp_turn,
            dp_mate,
            send,
            recv,
        )

    gf_tree = owner_tree(gf, gf_land, gf_send, gf_recv)
    go_tree = SumTree(
        "dp",
        lambda slot, h: own_out.at[pl.ds(5 * slot + 2 * h, 2 + h)],
        lambda kind, h: go_land.at[kind, pl.ds(2 * h, 2 + h)],
        dm,
        dp_turn,
        dp_mate,
        go_send,
        go_recv,
    )
    lanes_d = lane_iota((D, 128))
    vg[...] = jnp.where((lanes_d == 71) | (lanes_d == 72), vg[...], 0.0)
    lanes_h = lane_iota((64, 128))
    cols_f = jnp.sum(mixed_t[0:256].astype(F32), axis=1, keepdims=True)
    for r in range(4):
        w = hidden_index(me, r)
        rows = pl.ds(pl.multiple_of(lax.rem(w, 16) * 64, 64), 64)
        vg[rows] += jnp.where(lanes_h == 64 + 9 + w // 16, cols_f[64 * r : 64 * r + 64], 0.0)
    grads_by_owner(gf, 0, 2)
    gf_tree.begin()
    po.tree.far_of_me()
    po.tree.of_mate()

    def back_arrived():
        @pl.when(me < 3)
        def _():
            for r in range(4):
                back_few(r).wait_send()
                remote(
                    goa_buf,
                    own_out.at[pl.ds(8 + 8 * r, 8)],
                    v_send.at[r],
                    v_recv.at[r],
                    {"seq": sib},
                ).wait_recv()

        @pl.when(me < 4)
        def _():
            keep_a.wait()

        @pl.when(me == 3)
        def _():
            keep_f3.wait()

        @pl.when(me > 3)
        def _():
            back_many().wait_send()
            keep_f.wait()
            remote(
                goa_buf, own_out.at[pl.ds(32, 8)], v_send.at[0], v_recv.at[0], {"seq": sib}
            ).wait_recv()

    for qi in reversed(range(NCH)):
        lanes = slice(qi * CH, (qi + 1) * CH)
        dq = jnp.zeros((64, CH), F32)
        for kc in range(qi + 1):
            keys = slice(kc * CH, (kc + 1) * CH)
            p = jnp.exp(scores(kc, qi) - lse[0:1, lanes])
            dp = dot(vn[keys, 0:64], dot_t[:, lanes])
            ds = (p * (dp - delta[0:1, lanes])).astype(BF16)
            dv = dot(p.astype(BF16), dot_n[lanes])
            dk = dot(ds, qn[lanes, 0:64])
            dq = dq + dot(kt[:, keys], ds)
            if qi == NCH - 1:
                dvn[keys] = dv
                dkn[keys] = dk
            else:
                dvn[keys] += dv
                dkn[keys] += dk
        dqt[:, lanes] = dq * 0.125
        if qi == 2:
            back_arrived()
            go_tree.begin()

    @pl.loop(0, NCH)
    def _(i):
        rows = pl.ds(pl.multiple_of(i * CH, CH), CH)
        cosine, sine = cos_ref[:, rows], sin_ref[:, rows]
        dq = rotate_t(dqt[:, rows], cosine, sine, -1.0)
        dk = rotate_t(jnp.transpose(dkn[rows]), cosine, sine, -1.0)
        dv = jnp.transpose(dvn[rows])
        full = jnp.concatenate([dq, dk, dv, zeros_aug], axis=0)
        mixed_t[256:512, rows] = full.astype(BF16)
        mixed[pl.ds(8 * i, 8), :, 256:512] = jnp.transpose(full).astype(BF16).reshape(8, SPAN, 256)

    cols_q = jnp.sum(mixed_t[256:448].astype(F32), axis=1, keepdims=True)
    for i in range(3):
        vg[head_rows] += jnp.where(lanes_h == 68 + i, cols_q[64 * i : 64 * i + 64], 0.0)
    po.tree.near_late()
    gf_tree.far_of_me()
    gf_tree.of_mate()
    grads_by_owner(gq, 256, 0)

    def gq_copy(k, to, frm):
        return remote(gq.at[to], gq_got.at[frm], gq_send.at[k], gq_recv.at[frm], {"dp": to})

    @pl.loop(1, DP)
    def _(k):
        gq_copy(k, lax.rem(dm + k, DP), dm).start()

    slab = jnp.transpose(vg[...])
    for p in range(8):
        vt_part[p] = slab[64:80, 128 * p : 128 * p + 128]

    def vs_copy(k, to, frm):
        return remote(
            vt_part.at[to // 2], vt_seq.at[frm], vs_send.at[k], vs_recv.at[frm], {"seq": to}
        )

    def vd_copy(k, to, frm):
        return remote(vt_own, vt_dp.at[frm], vd_send.at[k], vd_recv.at[frm], {"dp": to})

    @pl.loop(1, SEQ)
    def _(k):
        vs_copy(k, lax.rem(me + k, SEQ), me).start()

    vt_seq[me] = vt_part[chip]
    gf_tree.near_late()
    cot_tree.sent()
    hg.begin()
    go_tree.far_of_me()
    go_tree.of_mate()
    hg.tree.far_of_me()
    hg.tree.of_mate()

    @pl.loop(1, SEQ)
    def _(k):
        vs_copy(k, me, lax.rem(me + k, SEQ)).wait_recv()

    vt_own[...] = jnp.sum(vt_seq[...], axis=0)

    @pl.loop(1, DP)
    def _(k):
        vd_copy(k, lax.rem(dm + k, DP), dm).start()

    vt_dp[dm] = vt_own[...]
    go_tree.near_late()

    def to_owner(part, total, send, recv, k, to, frm):
        return remote(part.at[to], total.at[frm], send.at[k], recv.at[frm], {"seq": to})

    def own_sums(part, total, send, recv):
        @pl.loop(1, SEQ)
        def _(k):
            to_owner(part, total, send, recv, k, lax.rem(me + k, SEQ), me).start()

        total[me] = part[me]

    def own_arrived(part, total, send, recv):
        @pl.loop(1, SEQ)
        def _(k):
            to_owner(part, total, send, recv, k, me, lax.rem(me + k, SEQ)).wait_recv()

    def squares_of(value):
        return jnp.sum(jnp.sum(value * value, axis=0), axis=0, keepdims=True)

    for h in range(2):
        f_part[8 * h : 8 * h + 8] = gf_tree.total(h).reshape(8, 8, 256)
    own_sums(f_part, f_sum, bf_send, bf_recv)
    squares = squares_of(f_part[...])

    @pl.loop(1, DP)
    def _(k):
        gq_copy(k, dm, lax.rem(dm + k, DP)).wait_recv()

    total = gq[dm].astype(F32)
    for k in range(1, DP):
        total = total + gq_got[lax.rem(dm + k, DP)].astype(F32)
    total = total.reshape(SEQ, 8, 256)
    squares = squares + squares_of(total)
    for h in range(2):
        out_total = go_tree.total(h)
        wout_sum[2 * h : 2 * h + 2 + h] = out_total
        out_squares = squares_of(out_total)
        squares = squares + out_squares[:, :256] + out_squares[:, 256:]

    @pl.loop(1, DP)
    def _(k):
        vd_copy(k, dm, lax.rem(dm + k, DP)).wait_recv()

    vec_total = jnp.sum(vt_dp[...], axis=0)
    first = lax.rem(me, 2) * 64 + dm * 8
    lanes = lane_iota(vec_total.shape)
    vec_mine = jnp.where((lanes >= first) & (lanes < first + 8), vec_total, 0.0)
    vec_squares = jnp.sum(vec_mine * vec_mine, axis=0, keepdims=True)
    small[...] = jnp.zeros((128, 128), F32)
    small[0:16] = vec_total
    small[...] = jnp.transpose(small[...])
    vec_grad[...] = small[pl.ds(pl.multiple_of(first, 8), 8)]
    row = squares[:, :128] + squares[:, 128:] + vec_squares
    mine = jnp.sum(row, axis=1, keepdims=True)
    q_part[...] = jnp.where(lane_iota(total.shape) < 192, total, mine[None])
    own_sums(q_part, q_sum, bq_send, bq_recv)
    hg.tree.near_late()
    po.finish(out_sum)
    own_arrived(q_part, q_sum, bq_send, bq_recv)
    tile_b[...] = jnp.sum(q_sum[:, :, 128:256], axis=0)

    def tb_copy(k, to, frm):
        return remote(tile_b, got_b.at[frm], tb_send.at[k], tb_recv.at[frm], {"dp": to})

    @pl.loop(1, DP)
    def _(k):
        tb_copy(k, lax.rem(dm + k, DP), dm).start()

    got_b[dm] = tile_b[...]

    @pl.loop(1, DP)
    def _(k):
        tb_copy(k, dm, lax.rem(dm + k, DP)).wait_recv()

    everything = jnp.sum(got_b[...], axis=0)
    square_ref[...] = jnp.broadcast_to(everything[:, 127:128], (8, 128))
    own_arrived(f_part, f_sum, bf_send, bf_recv)

    hg.finish(grad_sum)
    for tree in (in_tree, out_tree, gf_tree, go_tree):
        tree.sent()

    @pl.loop(1, DP)
    def _(k):
        to = lax.rem(dm + k, DP)
        tb_copy(k, to, dm).wait_send()
        gq_copy(k, to, dm).wait_send()
        vd_copy(k, to, dm).wait_send()

    @pl.loop(1, SEQ)
    def _(k):
        to = lax.rem(me + k, SEQ)
        a_copy(k, to, me).wait_send()
        vs_copy(k, to, me).wait_send()
        to_owner(f_part, f_sum, bf_send, bf_recv, k, to, me).wait_send()
        to_owner(q_part, q_sum, bq_send, bq_recv, k, to, me).wait_send()


def layer_call(span, length, x, cot, w_in, w_out, vectors):
    freqs = np.float32(THETA_BASE) ** (-2.0 * np.arange(ROT // 2) / ROT)
    angles = np.arange(ROW, dtype=np.float32)[None, :] * freqs.astype(np.float32)[:, None]
    cosine, sine = np.cos(angles).astype(np.float32), np.sin(angles).astype(np.float32)
    smem = pl.BlockSpec(memory_space=pltpu.SMEM)
    vmem = pl.BlockSpec(memory_space=pltpu.VMEM)
    sds = jax.ShapeDtypeStruct
    dma = pltpu.SemaphoreType.DMA

    def buf(shape, dtype=BF16):
        return pltpu.VMEM(shape, dtype)

    return pl.pallas_call(
        layer_kernel,
        out_shape=(
            sds((TOK, D), F32),
            sds((TOK, D), F32),
            sds((SEQ, 8, 256), F32),
            sds((SEQ, 8, 256), F32),
            sds((5, 16, 512), F32),
            sds((8, 128), F32),
            sds((16, D), F32),
            sds((8, 128), F32),
        ),
        in_specs=[smem] * 2 + [vmem] * 7,
        out_specs=[vmem] * 8,
        scratch_shapes=[
            pltpu.SMEM((32,), jnp.int32),
            buf((32, SPAN, D)),
            buf((32, SPAN, D)),
            buf((SEQ, 16, 256)),
            buf((DP, SEQ, 16, 256)),
            buf((40, 16, 512)),
            buf((4, 8, 16, 512)),
            buf((128, 128), F32),
            buf((ROW, D)),
            buf((ROW, D)),
            buf((D, 512)),
            buf((D, 512)),
            buf((320, D)),
            buf((128, ROW)),
            buf((ROW, 128)),
            buf((64, ROW)),
            buf((ROW, 128)),
            buf((64, ROW)),
            buf((ROW, 128)),
            buf((64, ROW)),
            buf((ROW, 64)),
            buf((64, ROW), F32),
            buf((8, ROW), F32),
            buf((8, ROW), F32),
            buf((32, SPAN, 320)),
            buf((320, ROW)),
            buf((ROW, 256), F32),
            buf((32, SPAN, 512)),
            buf((512, ROW)),
            buf((64, ROW), F32),
            buf((ROW, 64), F32),
            buf((ROW, 64), F32),
            buf((D, 128), F32),
            buf((8, 16, 512)),
            buf((32, 16, 512)),
            buf((40, 16, 512)),
            buf((DP, 8, 16, 256)),
            buf((DP, 8, 16, 256)),
            buf((8, 2, SPAN, D)),
            buf((8, 2, SPAN, D)),
            buf((7, 2, SPAN, D)),
            buf((7, 2, SPAN, D)),
            buf((7, 8, 16, 256)),
            buf((DP, 8, 16, 256)),
            buf((8, 16, 128), F32),
            buf((SEQ, 16, 128), F32),
            buf((16, 128), F32),
            buf((DP, 16, 128), F32),
            buf((7, 5, 16, 512)),
            buf((SEQ, 8, 256), F32),
            buf((SEQ, 8, 256), F32),
            buf((8, 128), F32),
            buf((DP, 8, 128), F32),
            dma((2,)),
            dma((SEQ,)),
            dma((SEQ,)),
            dma((32,)),
            dma((SEQ, 2)),
            dma((32,)),
            dma((SEQ, 2)),
            dma((16,)),
            dma((DP, 2)),
            dma((16,)),
            dma((DP, 2)),
            dma((4,)),
            dma((4,)),
            dma((8,)),
            dma((8,)),
            dma((16,)),
            dma((7, 2)),
            dma((8,)),
            dma((8,)),
            dma((16,)),
            dma((7, 2)),
            dma((16,)),
            dma((7, 2)),
            dma((DP,)),
            dma((DP,)),
            dma((16,)),
            dma((7, 2)),
            dma((4,)),
            dma((4,)),
            dma((SEQ,)),
            dma((SEQ,)),
            dma((SEQ,)),
            dma((SEQ,)),
            dma((SEQ,)),
            dma((SEQ,)),
            dma((DP,)),
            dma((DP,)),
            dma((DP,)),
            dma((DP,)),
        ],
        compiler_params=pltpu.CompilerParams(
            collective_id=0, has_side_effects=True, vmem_limit_bytes=VMEM_LIMIT
        ),
        name="layer_of_one_row",
    )(span, length, x, cot, w_in, w_out, vectors, jnp.asarray(cosine), jnp.asarray(sine))


def adam(weight, grad, first, second, factor, rate, decay):
    clipped = grad * factor
    first_new = BETA_ONE * first + (1.0 - BETA_ONE) * clipped
    second_new = BETA_TWO * second + (1.0 - BETA_TWO) * clipped * clipped
    first_hat = first_new / (1.0 - BETA_ONE**STEP)
    second_hat = second_new / (1.0 - BETA_TWO**STEP)
    weight_new = weight * (1.0 - rate * decay) - rate * first_hat / (
        jnp.sqrt(second_hat) + ADAM_EPS
    )
    return (weight_new, first_new, second_new, weight_new.astype(BF16))


UPDATE_IN = (
    ("square", (8, 128), F32),
    ("f_sum", (SEQ, 8, 256), F32),
    ("q_sum", (SEQ, 8, 256), F32),
    ("w_in", (8, 7 * D), F32),
    ("in_first", (8, 7 * D), F32),
    ("in_second", (8, 7 * D), F32),
    ("wout_sum", (5, 16, 512), F32),
    ("w_out", (40, D), F32),
    ("out_first", (40, D), F32),
    ("out_second", (40, D), F32),
    ("vectors", (8, VEC_ROWS), F32),
    ("vec_first", (8, VEC_ROWS), F32),
    ("vec_second", (8, VEC_ROWS), F32),
    ("x", (TOK, D), BF16),
    ("cot", (TOK, D), BF16),
    ("grad_sum", (TOK, D), F32),
    ("out_sum", (TOK, D), F32),
    ("vec", (16, D), F32),
    ("vec_grad", (8, 128), F32),
)
UPDATE_OUT = (
    ((TOK, D), BF16),
    ((TOK, D), BF16),
    ((8, 128), F32),
    ((8, 7 * D), F32),
    ((40, D), F32),
    ((8, VEC_ROWS), F32),
    ((8, 7 * D), F32),
    ((40, D), F32),
    ((8, VEC_ROWS), F32),
    ((8, 7 * D), F32),
    ((40, D), F32),
    ((8, VEC_ROWS), F32),
    ((8, 7 * D), BF16),
    ((40, D), BF16),
    ((8, VEC_ROWS), BF16),
)


def update_kernel(span_ref, len_ref, *refs):
    ins, refs = refs[: len(UPDATE_IN)], refs[len(UPDATE_IN) :]
    outs, refs = refs[: len(UPDATE_OUT)], refs[len(UPDATE_OUT) :]
    in_bufs, refs = refs[: len(UPDATE_IN)], refs[len(UPDATE_IN) :]
    out_bufs, (in_sem, out_sem, grad_in) = refs[: len(UPDATE_OUT)], refs[len(UPDATE_OUT) :]
    me = lax.axis_index("seq")
    loads = [
        pltpu.make_async_copy(a, b, in_sem.at[i]) for i, (a, b) in enumerate(zip(ins, in_bufs))
    ]
    stores = [
        pltpu.make_async_copy(b, a, out_sem.at[i]) for i, (a, b) in enumerate(zip(outs, out_bufs))
    ]
    for load in loads:
        load.start()
    names = [name for name, _, _ in UPDATE_IN]

    def take(name):
        i = names.index(name)
        loads[i].wait()
        return in_bufs[i]

    def give(i, value):
        out_bufs[i][...] = value
        stores[i].start()

    norm = jnp.sqrt(take("square")[...])
    give(2, norm)
    factor = jnp.minimum(1.0, CLIP_NORM / norm)[0:1, 0:1]

    f_sum, q_sum = take("f_sum"), take("q_sum")
    for s in range(SEQ):
        for j, p in enumerate(PIECES[s]):
            p = int(p)
            piece = (
                q_sum[s, :, 64 * j : 64 * j + 64]
                if j < 3
                else f_sum[s, :, 64 * (j - 3) : 64 * (j - 3) + 64]
            )
            grad_in[:, 64 * p : 64 * p + 64] = piece

    def matrix(at, grad, weight, first, second, rate, decay):
        values = adam(
            take(weight)[...], grad, take(first)[...], take(second)[...], factor, rate, decay
        )
        for k, value in enumerate(values):
            give(at + 3 * k, value)

    matrix(3, grad_in[...], "w_in", "in_first", "in_second", RATE_MATRIX, DECAY_RATE)
    sums = take("wout_sum")
    grad_out = jnp.concatenate([unfold(sums[u]) for u in range(5)], axis=0)
    matrix(4, grad_out, "w_out", "out_first", "out_second", RATE_MATRIX, DECAY_RATE)
    grad_vec = take("vec_grad")[:, 0:VEC_ROWS]
    matrix(5, grad_vec, "vectors", "vec_first", "vec_second", RATE_VECTOR, 0.0)

    x_rows = take("x")[...].astype(F32)
    centered = x_rows - jnp.mean(x_rows, axis=-1, keepdims=True)
    inv_std = lax.rsqrt(jnp.mean(centered * centered, axis=-1, keepdims=True) + NORM_EPS)
    x_hat = centered * inv_std
    row = lax.broadcasted_iota(jnp.int32, (TOK, 1), 0)
    place = jnp.where(row < SPAN, span_ref[0, me] * SPAN + row, span_ref[1, me] * SPAN + row - SPAN)
    cot = jnp.where(place < len_ref[0], take("cot")[...].astype(F32), 0.0)
    grad = take("grad_sum")[...]
    back = (
        grad
        - jnp.mean(grad, axis=-1, keepdims=True)
        - x_hat * jnp.mean(grad * x_hat, axis=-1, keepdims=True)
    )
    give(1, (cot + inv_std * back).astype(BF16))
    out, vec = take("out_sum")[...], take("vec")
    give(0, (x_rows + out + (vec[7:8] + vec[8:9])).astype(BF16))
    for store in stores:
        store.wait()


def update_call(span, length, *args):
    smem = pl.BlockSpec(memory_space=pltpu.SMEM)
    anywhere = pl.BlockSpec(memory_space=pl.ANY)
    dma = pltpu.SemaphoreType.DMA
    return pl.pallas_call(
        update_kernel,
        out_shape=tuple(jax.ShapeDtypeStruct(shape, kind) for shape, kind in UPDATE_OUT),
        in_specs=[smem] * 2 + [anywhere] * len(UPDATE_IN),
        out_specs=[anywhere] * len(UPDATE_OUT),
        scratch_shapes=[pltpu.VMEM(shape, kind) for _, shape, kind in UPDATE_IN]
        + [pltpu.VMEM(shape, kind) for shape, kind in UPDATE_OUT]
        + [dma((len(UPDATE_IN),)), dma((len(UPDATE_OUT),)), pltpu.VMEM((8, 7 * D), F32)],
        compiler_params=pltpu.CompilerParams(vmem_limit_bytes=UPDATE_LIMIT),
        name="clipped_update",
    )(span, length, *args)


def body(
    hidden_in,
    out_cot,
    in_weight,
    out_weight,
    vectors,
    in_first,
    in_second,
    out_first,
    out_second,
    vec_first,
    vec_second,
    lengths,
    span_of,
):
    span = span_of.T
    out_sum, grad_sum, f_sum, q_sum, wout_sum, squares, vec_full, vec_grad = layer_call(
        span, lengths, hidden_in[0], out_cot[0], in_weight, out_weight, vectors.T
    )
    outs = update_call(
        span,
        lengths,
        squares,
        f_sum,
        q_sum,
        in_weight,
        in_first,
        in_second,
        wout_sum,
        out_weight,
        out_first,
        out_second,
        vectors.T,
        vec_first.T,
        vec_second.T,
        hidden_in[0],
        out_cot[0],
        grad_sum,
        out_sum,
        vec_full,
        vec_grad,
    )
    block_out, input_grad, norm = outs[:3]
    rest = [out.T if i % 3 == 2 else out for i, out in enumerate(outs[3:])]
    return (block_out[None], input_grad[None], norm[0, 0], *rest)


def solution(mesh):
    tokens = P("dp", "seq", None)
    matrix = P(("seq", "dp"), None)
    vector = P(None, ("seq", "dp"))
    return jax.shard_map(
        body,
        mesh=mesh,
        in_specs=(
            tokens,
            tokens,
            matrix,
            matrix,
            vector,
            matrix,
            matrix,
            matrix,
            matrix,
            vector,
            vector,
            P("dp"),
            P(),
        ),
        out_specs=(tokens, tokens, P()) + (matrix, matrix, vector) * 4,
        check_vma=False,
    )
```

time: 180 us -> 125 us (0.69)
  Pallas kernels: 163 us -> 122 us
  local copies, waits for them, and re-layouts: 15 us -> 1.18 us
    pallas_call x1, Pallas kernels: 160 us -> 118 us  [layer_call(): pl.pallas_call(layer_kernel, out_shape=(sds((TOK, D), F32), sds((TOK, D),...]
    unnamed x50 -> x0, local copies, waits for them, and re-layouts: 14.4 us -> none
    pallas_call x1, Pallas kernels: 2.37 us -> 4.22 us  [update_call(): pl.pallas_call(update_kernel, out_shape=tuple((jax.ShapeDtypeStruct(shape...]
where the time goes in v3:
time: 125 us
  Pallas kernels  122 us (98%)
  between operations  1.31 us (1%)
    pallas_call x1, Pallas kernels, layer_call(): pl.pallas_call(layer_kernel, out_shape=(sds((TOK, D), F32), sds((TOK, D),...  118 us
    pallas_call x1, Pallas kernels, update_call(): pl.pallas_call(update_kernel, out_shape=tuple((jax.ShapeDtypeStruct(shape...  4.22 us

profile of v3, /device:TPU:1, one launch (start us, length us, event | category | flops | bytes accessed | tf_op | source)
XLA Modules:
  0.0 124.5 jit_solution(4693457517734230426)
XLA Ops:
  1.3 117.8 %layer_of_one_row.1 = (f32[128,1024]{1,0:T(8,128)}, f32[128,1024]{1,0:T(8,128)}, f32[16,8,256]{2,1,0:T(8,128)}, f32[16,8,256]{2,1,0:T(8,128)}, f32[5,16,512]{2,1...) custom-call(s32[2,16]{1,0:T(2,128)} %bitcast.19, s32[1]{0:T(128)S(6)} %copy.30.len_ref, ...), custom_call_target="tpu_custom_call" | custom-call | tf_op jit(solution)/shard_map/layer_of_one_row/pallas_call | solution.py:1182
  119.1 4.2 %clipped_update.1 = (bf16[128,1024]{1,0:T(8,128)(2,1)}, bf16[128,1024]{1,0:T(8,128)(2,1)}, f32[8,128]{1,0:T(8,128)}, f32[8,7168]{1,0:T(8,128)}, f32[40,1024]{1,0...) custom-call(s32[2,16]{1,0:T(2,128)} %bitcast.20, ...), custom_call_target="tpu_custom_call" | custom-call | tf_op jit(solution)/shard_map/clipped_update/pallas_call | solution.py:1427
  123.3 1.2 slice.3

commit v4 on v3

--- a/solution.py
+++ b/solution.py
@@ -99,39 +99,62 @@
         )
 
 
-def await_greetings():
-    pl.semaphore_wait(pltpu.get_barrier_semaphore(), SEQ + DP - 2)
+def await_greetings(me, dm):
+    barrier = pltpu.get_barrier_semaphore()
+
+    def wait_if(condition, more):
+        @pl.when(condition)
+        def _():
+            pl.semaphore_wait(barrier, SEQ + DP - 2 + more)
+
+    @pl.when(me < 3)
+    def _():
+        wait_if(dm == 0, 0)
+        wait_if(dm == 1, 2)
+        wait_if(dm > 1, 5)
+
+    @pl.when(me == 3)
+    def _():
+        pl.semaphore_wait(barrier, SEQ + DP - 2)
+
+    @pl.when(me > 3)
+    def _():
+        wait_if(dm < 6, 0)
+        wait_if(dm == 6, 3)
+        wait_if(dm == 7, 5)
+
+
+def all_sent(ref, sem):
+    remote(ref, ref, sem, sem, {"seq": 0}).wait_send()
+
+
+def all_here(ref, sem):
+    pltpu.make_async_copy(ref, ref, sem).wait()
 
 
 class Tree:
-    def __init__(self, axis, piece, me, turn, mate, sib, send, recv, over_mate):
-        self.axis, self.piece, self.me, self.turn, self.mate, self.sib = (
-            axis,
-            piece,
-            me,
-            turn,
-            mate,
-            sib,
-        )
+    def __init__(self, axis, piece, me, turn, mate, send, recv, over_mate, sib=None, given=None):
+        self.axis, self.piece, self.me, self.turn, self.mate = (axis, piece, me, turn, mate)
         self.send, self.recv, self.over_mate = send, recv, over_mate
-        self.started = []
+        self.sib, self.given = sib, given
+        self.per = 1 if sib is None else 2
 
     def put(self, slot, h, to):
         part = self.piece(slot, h)
-        copy = remote(
-            part, part, self.send.at[len(self.started)], self.recv.at[slot, h], {self.axis: to}
-        )
-        copy.start()
-        self.started.append(copy)
+        remote(part, part, self.send, self.arrival(slot, h), {self.axis: to}).start()
 
     def hand(self, slot, h):
         if self.sib is not None:
-            self.put(slot, h, self.sib)
+            part = self.piece(slot, h)
+            remote(part, part, self.send, self.given, {self.axis: self.sib}).start()
+
+    def arrival(self, slot, h):
+        return self.recv.at[slot // self.per, h]
 
     def got(self, slot, h):
         part = self.piece(slot, h)
         remote(
-            part, part, self.send.at[0], self.recv.at[slot, h], {self.axis: self.mate}
+            part, part, self.send, self.arrival(slot, h), {self.axis: self.mate}
         ).wait_recv()
 
     def own_to_ring(self):
@@ -186,16 +209,6 @@
         for h in range(2):
             self.got(slot, h)
             self.hand(slot, h)
-
-    def handed(self, other_mate):
-        for h in range(2):
-            for slot in (self.sib, other_mate):
-                for k in range(4):
-                    self.got(self.turn(slot, k), h)
-
-    def sent(self):
-        for copy in self.started:
-            copy.wait_send()
 
 
 class SumTree:
@@ -209,24 +222,20 @@
             mate,
         )
         self.send, self.recv = send, recv
-        self.started = []
 
     def put(self, slot, kind, h, to):
         copy = remote(
             self.piece(slot, h),
             self.land(kind, h),
-            self.send.at[len(self.started)],
+            self.send,
             self.recv.at[kind, h],
             {self.axis: to},
         )
         copy.start()
-        self.started.append(copy)
 
     def got(self, kind, h):
         part = self.land(kind, h)
-        remote(
-            part, part, self.send.at[0], self.recv.at[kind, h], {self.axis: self.mate}
-        ).wait_recv()
+        remote(part, part, self.send, self.recv.at[kind, h], {self.axis: self.mate}).wait_recv()
         return part[...].astype(F32)
 
     def add(self, slot, h, *kinds):
@@ -279,9 +288,56 @@
             value = value + self.got(kind, h)
         return value
 
+
+class ColumnSums:
+    def __init__(self, axis, piece, landing, me, turn, mate, send, recv):
+        self.axis, self.piece, self.me, self.turn, self.mate = (axis, piece, me, turn, mate)
+        self.land = lambda i: landing.at[i]
+        self.lands = lambda i, n: landing.at[pl.ds(i, n)]
+        self.send, self.recv = send, recv
+
+    def copy(self, k, of_mate):
+        to = self.turn(self.me, k)
+        return remote(
+            self.piece(self.turn(self.mate, k) if of_mate else to),
+            self.land(4 * of_mate + 4 - k),
+            self.send,
+            self.recv.at[1 + of_mate],
+            {self.axis: to},
+        )
+
+    def last(self):
+        return remote(
+            self.piece(self.mate),
+            self.land(0),
+            self.send,
+            self.recv.at[0],
+            {self.axis: self.mate},
+        )
+
+    def start(self):
+        for of_mate in (1, 0):
+            for k in (1, 3, 2):
+                self.copy(k, of_mate).start()
+
+    def summed(self, slot, of_mate):
+        total = self.piece(slot)[...].astype(F32)
+        all_here(self.lands(4 * of_mate + 1, 3), self.recv.at[1 + of_mate])
+        for k in (1, 3, 2):
+            total = total + self.land(4 * of_mate + 4 - k)[...].astype(F32)
+        return total
+
+    def middle(self):
+        self.piece(self.mate)[...] = self.summed(self.mate, 1).astype(BF16)
+        self.last().start()
+
+    def total(self):
+        value = self.summed(self.me, 0)
+        self.last().wait_recv()
+        return value + self.land(0)[...].astype(F32)
+
     def sent(self):
-        for copy in self.started:
-            copy.wait_send()
+        all_sent(self.lands(0, 7), self.send)
 
 
 def dot(a, b):
@@ -311,6 +367,20 @@
 def layer_kernel(
     span_ref,
     len_ref,
+    x_any,
+    cot_any,
+    w_in_any,
+    w_out_any,
+    vectors_any,
+    cos_any,
+    sin_any,
+    block_out_any,
+    input_grad_any,
+    f_sum_any,
+    q_sum_any,
+    wout_sum_any,
+    square_any,
+    vec_grad_any,
     x_ref,
     cot_ref,
     w_in_ref,
@@ -318,22 +388,24 @@
     vectors_ref,
     cos_ref,
     sin_ref,
-    out_sum,
-    grad_sum,
+    block_out,
+    input_grad,
     f_sum,
     q_sum,
     wout_sum,
     square_ref,
-    vec_ref,
     vec_grad,
+    load_sem,
+    store_sem,
     inv_ref,
     xh_all,
     cot_all,
     win_own,
     win_all,
     wout_all,
-    swap_all,
+    wout_own,
     small,
+    vec_ref,
     xs,
     cs,
     wr,
@@ -359,9 +431,8 @@
     dkn,
     dvn,
     vg,
-    goa_buf,
-    gof_buf,
-    own_out,
+    go_buf,
+    out_part,
     gf,
     gq,
     po_sib,
@@ -369,7 +440,7 @@
     po_land,
     hg_land,
     gf_land,
-    gq_got,
+    gq_land,
     vt_part,
     vt_seq,
     vt_own,
@@ -377,15 +448,19 @@
     go_land,
     f_part,
     q_part,
+    tile_a,
     tile_b,
+    got_a,
     got_b,
     local_sem,
     a_send,
     a_recv,
     x_send,
     x_recv,
+    x_given,
     c_send,
     c_recv,
+    c_given,
     l_send,
     l_recv,
     o_send,
@@ -412,6 +487,8 @@
     bf_recv,
     bq_send,
     bq_recv,
+    ta_send,
+    ta_recv,
     vs_send,
     vs_recv,
     vd_send,
@@ -425,18 +502,100 @@
     chip = me // 2
     sib = me + 1 - 2 * core
     mate = me + 2 - 4 * lax.rem(chip, 2)
-    sib_mate = mate + 1 - 2 * core
     dp_mate = lax.rem(dm + 4, DP)
     head = head_index(me)
+    loads = [
+        pltpu.make_async_copy(a, b, load_sem.at[i])
+        for i, (a, b) in enumerate(
+            (
+                (x_any, x_ref),
+                (w_in_any, w_in_ref),
+                (vectors_any, vectors_ref),
+                (cot_any, cot_ref),
+                (w_out_any, w_out_ref),
+                (cos_any, cos_ref),
+                (sin_any, sin_ref),
+            )
+        )
+    ]
+    block_store, grad_store, f_store, q_store, wout_store, square_store, vec_store = stores = [
+        pltpu.make_async_copy(a, b, store_sem.at[i])
+        for i, (a, b) in enumerate(
+            (
+                (block_out, block_out_any),
+                (input_grad, input_grad_any),
+                (f_sum, f_sum_any),
+                (q_sum, q_sum_any),
+                (wout_sum, wout_sum_any),
+                (square_ref, square_any),
+                (vec_grad, vec_grad_any),
+            )
+        )
+    ]
+    def trades(step):
+        for u in range(5):
+            i = 5 * dm + u
+
+            @pl.when(me < 3)
+            def _(u=u, i=i):
+                @pl.when(i >= 8)
+                def _():
+                    k = lax.rem(i, 8)
+                    step(u, 4 * me + 3 + i // 8, (32 + k) // 5, 32 + k)
+
+            @pl.when(me > 3)
+            def _(u=u, i=i):
+                @pl.when(i >= 32)
+                def _():
+                    slot = 8 + 8 * lax.rem(me, 4) + i - 32
+                    step(u, (me - 4) // 4, slot // 5, slot)
+
+    def kept(step):
+        for u in range(5):
+            i = 5 * dm + u
+
+            @pl.when(me < 3)
+            def _(u=u, i=i):
+                @pl.when(i < 8)
+                def _():
+                    step(u)
+
+            @pl.when(me == 3)
+            def _(u=u):
+                step(u)
+
+            @pl.when(me > 3)
+            def _(u=u, i=i):
+                @pl.when(i < 32)
+                def _():
+                    step(u)
+
+    barrier = pltpu.get_barrier_semaphore()
+    trades(
+        lambda u, s, d, slot: pl.semaphore_signal(
+            barrier, inc=1, device_id={"seq": s, "dp": d}, device_id_type=MESH
+        )
+    )
     greet(me, dm)
+    for load in loads:
+        load.start()
 
     row = lax.broadcasted_iota(jnp.int32, (TOK, 1), 0)
     place = jnp.where(row < SPAN, span_ref[0, me] * SPAN + row, span_ref[1, me] * SPAN + row - SPAN)
-    x_rows = x_ref[...].astype(F32)
-    centered = x_rows - jnp.mean(x_rows, axis=-1, keepdims=True)
-    inv_std = lax.rsqrt(jnp.mean(centered * centered, axis=-1, keepdims=True) + NORM_EPS)
-    xh_all[pl.ds(2 * me, 2)] = (centered * inv_std).astype(BF16).reshape(2, SPAN, D)
-
+    def own_rows():
+        x_rows = x_ref[...].astype(F32)
+        centered = x_rows - jnp.mean(x_rows, axis=-1, keepdims=True)
+        inv_std = lax.rsqrt(jnp.mean(centered * centered, axis=-1, keepdims=True) + NORM_EPS)
+        return x_rows, centered * inv_std, inv_std
+
+    def own_cot():
+        return jnp.where(place < len_ref[0], cot_ref[...].astype(F32), 0.0)
+
+    loads[0].wait()
+    xh_all[pl.ds(2 * me, 2)] = own_rows()[1].astype(BF16).reshape(2, SPAN, D)
+
+    loads[1].wait()
+    loads[2].wait()
     small[...] = jnp.zeros((128, 128), F32)
     small[0:8, 0:VEC_ROWS] = vectors_ref[...]
     vec_t = small[0:8, 0:64]
@@ -444,9 +603,16 @@
         take = [w_in_ref[:, 64 * int(p) : 64 * int(p) + 64] for p in PIECES[s]]
         qkv = jnp.concatenate(take[:3] + [vec_t], axis=1)
         win_own[s] = jnp.concatenate([jnp.concatenate(take[3:], axis=1), qkv], axis=0).astype(BF16)
+    loads[4].wait()
     for u in range(5):
-        wout_all[5 * dm + u] = fold(w_out_ref[8 * u : 8 * u + 8]).astype(BF16)
-    cot_own = jnp.where(place < len_ref[0], cot_ref[...].astype(F32), 0.0)
+        wout_own[u] = fold(w_out_ref[8 * u : 8 * u + 8]).astype(BF16)
+
+    def keep_unit(u):
+        wout_all[5 * dm + u] = wout_own[u]
+
+    kept(keep_unit)
+    loads[3].wait()
+    cot_own = own_cot()
     cot_all[pl.ds(2 * me, 2)] = cot_own.astype(BF16).reshape(2, SPAN, D)
     cot_sum = jnp.sum(cot_own, axis=0, keepdims=True)
     vg[...] = jnp.transpose(jnp.broadcast_to(cot_sum, (128, D)))
@@ -473,10 +639,11 @@
         me,
         seq_turn,
         mate,
-        sib,
-        x_send,
+        x_send.at[0],
         x_recv,
         True,
+        sib,
+        x_given.at[0],
     )
     cot_tree = Tree(
         "seq",
@@ -484,10 +651,11 @@
         me,
         seq_turn,
         mate,
-        sib,
-        c_send,
+        c_send.at[0],
         c_recv,
         True,
+        sib,
+        c_given.at[0],
     )
     in_tree = Tree(
         "dp",
@@ -495,8 +663,7 @@
         dm,
         dp_turn,
         dp_mate,
-        None,
-        l_send,
+        l_send.at[0],
         l_recv,
         False,
     )
@@ -506,99 +673,89 @@
         dm,
         dp_turn,
         dp_mate,
-        None,
-        o_send,
+        o_send.at[0],
         o_recv,
         False,
     )
 
     def a_copy(k, to, frm):
         return remote(
-            win_own.at[to], win_all.at[dm, frm], a_send.at[k], a_recv.at[frm], {"seq": to}
-        )
-
-    await_greetings()
+            win_own.at[to], win_all.at[dm, frm], a_send.at[0], a_recv.at[0], {"seq": to}
+        )
+
+    await_greetings(me, dm)
 
     @pl.loop(1, SEQ)
     def _(k):
         a_copy(k, lax.rem(me + k, SEQ), me).start()
 
+    def trade_out(u, s, d, slot):
+        return remote(
+            wout_own.at[u],
+            wout_all.at[slot],
+            w_send.at[u],
+            w_recv.at[lax.rem(slot, 5)],
+            {"seq": s, "dp": d},
+        )
+
+    def trade_in(u):
+        return remote(
+            wout_own.at[u], wout_all.at[5 * dm + u], w_send.at[u], w_recv.at[u], {"seq": sib}
+        )
+
+    trades(lambda u, s, d, slot: trade_out(u, s, d, slot).start())
     x_tree.own_to_mate()
     x_tree.own_to_ring()
+    keep.wait()
+
+    all_here(win_own.at[pl.ds(0, SEQ - 1)], a_recv.at[0])
+
+    in_tree.own_to_mate()
+    in_tree.own_to_ring()
+    trades(lambda u, s, d, slot: trade_in(u).wait_recv())
     out_tree.own_to_mate()
     out_tree.own_to_ring()
-    keep.wait()
-
-    @pl.loop(1, SEQ)
-    def _(k):
-        a_copy(k, me, lax.rem(me + k, SEQ)).wait_recv()
-
-    in_tree.own_to_mate()
-    in_tree.own_to_ring()
     x_tree.near_of_me()
     x_tree.of_mate()
+    in_tree.near_of_me()
+    in_tree.of_mate()
+    out_tree.near_of_me()
     out_tree.of_mate()
-    out_tree.near_of_me()
     x_tree.far_of_me()
+    in_tree.far_of_me()
     cot_tree.own_to_ring()
+
+    def unpack(column):
+        def step(sb, carry):
+            cq, cf = carry
+            tiles = [win_all[4 * column + y, sb].astype(F32) for y in range(4)]
+            ff = jnp.concatenate([t[:8] for t in tiles], axis=0)
+            qk = jnp.concatenate([t[8:] for t in tiles], axis=0)
+            rows = pl.ds(pl.multiple_of(sb * 64 + 32 * column, 32), 32)
+            gain_a, bias_a, gain_m, bias_m = (qk[:, 192 + i : 193 + i] for i in range(4))
+            wr[rows] = jnp.concatenate([ff, qk], axis=1).astype(BF16)
+            folded = jnp.where(lane_iota(qk.shape) < 192, qk * gain_a, 0.0)
+            wp[rows] = jnp.concatenate([ff * gain_m, folded], axis=1).astype(BF16)
+            return (
+                cq + jnp.sum(qk * bias_a, axis=0, keepdims=True),
+                cf + jnp.sum(ff * bias_m, axis=0, keepdims=True),
+            )
+
+        return step
+
+    zero_row = jnp.zeros((1, 256), F32)
+    sums = lax.fori_loop(0, SEQ, unpack(dm // 4), (zero_row, zero_row))
+    x_tree.near_of_mate()
     cot_tree.own_to_mate()
-    in_tree.of_mate()
-    in_tree.near_of_me()
-    out_tree.near_of_mate()
     in_tree.near_of_mate()
-    x_tree.near_of_mate()
-    in_tree.far_of_me()
     in_tree.far_of_mate()
-    out_tree.far_of_me()
-    out_tree.far_of_mate()
-
-    def swap_few(r):
-        return remote(
-            wout_all.at[pl.ds(8 + 8 * r, 8)],
-            swap_all.at[0],
-            w_send.at[r],
-            w_recv.at[0],
-            {"seq": 4 + 4 * me + r},
-        )
-
-    def swap_many():
-        return remote(
-            wout_all.at[pl.ds(32, 8)],
-            swap_all.at[lax.rem(me, 4)],
-            w_send.at[0],
-            w_recv.at[lax.rem(me, 4)],
-            {"seq": (me - 4) // 4},
-        )
-
-    @pl.when(me < 3)
-    def _():
-        for r in range(4):
-            swap_few(r).start()
-
-    @pl.when(me > 3)
-    def _():
-        swap_many().start()
-
-    def unpack(sb, carry):
-        cq, cf = carry
-        tiles = [win_all[d, sb].astype(F32) for d in range(DP)]
-        ff = jnp.concatenate([t[:8] for t in tiles], axis=0)
-        qk = jnp.concatenate([t[8:] for t in tiles], axis=0)
-        rows = pl.ds(pl.multiple_of(sb * 64, 64), 64)
-        gain_a, bias_a, gain_m, bias_m = (qk[:, 192 + i : 193 + i] for i in range(4))
-        wr[rows] = jnp.concatenate([ff, qk], axis=1).astype(BF16)
-        folded = jnp.where(lane_iota(qk.shape) < 192, qk * gain_a, 0.0)
-        wp[rows] = jnp.concatenate([ff * gain_m, folded], axis=1).astype(BF16)
-        return (
-            cq + jnp.sum(qk * bias_a, axis=0, keepdims=True),
-            cf + jnp.sum(ff * bias_m, axis=0, keepdims=True),
-        )
-
-    zero_row = jnp.zeros((1, 256), F32)
-    cq, cf = lax.fori_loop(0, SEQ, unpack, (zero_row, zero_row))
+    cot_tree.near_of_me()
+    cq, cf = lax.fori_loop(0, SEQ, unpack(dp_mate // 4), sums)
 
     slab = jnp.transpose(wr[:, 384:512].astype(F32))
     vec_ref[...] = slab[64:80]
+    loads[5].wait()
+    loads[6].wait()
 
     hid = []
     for r in range(4):
@@ -617,14 +774,15 @@
     bq, bk, bv = (head_vecs[:, 68 + i : 69 + i] for i in range(3))
 
     x_tree.far_of_mate()
-    x_tree.handed(sib_mate)
+    all_here(xh_all.at[pl.ds(0, 16)], x_given.at[0])
 
     @pl.loop(0, 32)
     def _(i):
         rows = pl.ds(pl.multiple_of(i * SPAN, SPAN), SPAN)
         xs[rows] = xh_all[inv_ref[i]]
 
-    cot_tree.of_mate()
+    out_tree.near_of_mate()
+    out_tree.far_of_me()
 
     aug = jnp.where(lax.broadcasted_iota(jnp.int32, (64, CH), 0) == 0, 1.0, 0.0)
     zeros_aug = jnp.zeros((64, CH), F32)
@@ -640,8 +798,7 @@
             axis=0,
         )
 
-    @pl.loop(0, NCH)
-    def _(i):
+    def project(i):
         start = pl.multiple_of(i * CH, CH)
         rows = pl.ds(start, CH)
         xh = xs[rows]
@@ -669,7 +826,11 @@
         joined_t[0:256, rows] = jnp.transpose(activ).astype(BF16)
         dact[rows] = cdf + pre * pdf
 
-    cot_tree.near_of_me()
+    pl.loop(0, 2)(project)
+    cot_tree.of_mate()
+    cot_tree.far_of_me()
+    pl.loop(2, NCH)(project)
+    out_tree.far_of_mate()
     causal = lax.broadcasted_iota(jnp.int32, (CH, CH), 0) <= lane_iota((CH, CH))
 
     def scores(kc, qi):
@@ -693,9 +854,6 @@
         lse[:, lanes] = jnp.broadcast_to(top + jnp.log(total), (8, CH))
         joined_t[256:320, lanes] = out.astype(BF16)
         joined[8 * qi : 8 * qi + 8, :, 256:320] = jnp.transpose(out).astype(BF16).reshape(8, SPAN, HEAD)
-        if qi == 2:
-            cot_tree.far_of_me()
-            cot_tree.near_of_mate()
     def put_units(base, at, count):
         @pl.loop(0, count // 2)
         def _(i):
@@ -703,38 +861,9 @@
             rows = pl.ds(pl.multiple_of(at + i * 16, 16), 16)
             wo[rows] = jnp.concatenate(pair, axis=0).astype(BF16)
 
-    def put_swap(base, rs):
-        for r in range(rs):
-            for i in range(4):
-                pair = [unfold(swap_all[r, 2 * i + j].astype(F32)) for j in range(2)]
-                at = base + r * 64 + i * 16
-                wo[at : at + 16] = jnp.concatenate(pair, axis=0).astype(BF16)
-
-    @pl.when(me < 4)
-    def _():
-        put_units(0, 256, 8)
-
-    @pl.when(me < 3)
-    def _():
-        for r in range(4):
-            remote(
-                wout_all.at[pl.ds(32, 8)], swap_all.at[r], w_send.at[r], w_recv.at[r], {"seq": sib}
-            ).wait_recv()
-            swap_few(r).wait_send()
-        put_swap(0, 4)
-
-    @pl.when(me == 3)
-    def _():
-        put_units(8, 0, 32)
-
-    @pl.when(me > 3)
-    def _():
-        swap_many().wait_send()
-        remote(
-            wout_all.at[pl.ds(32, 8)], swap_all.at[0], w_send.at[0], w_recv.at[0], {"seq": sib}
-        ).wait_recv()
-        put_swap(256, 1)
-        put_units(0, 0, 32)
+    late = (me + 12) // 16
+    put_units(8 * (1 - late), 0, 32)
+    put_units(32 * late, 256, 8)
 
     def of_chip(ref, j):
         return jnp.concatenate([ref[span_ref[i % 2, 2 * j + i // 2]] for i in range(4)], axis=0)
@@ -743,7 +872,7 @@
 
     class ChipSums:
         def __init__(self, part, buf, sib_buf, land, s_send, s_recv, send, recv):
-            self.part, self.buf, self.sib_buf = part, buf, sib_buf
+            self.part, self.buf, self.sib_buf, self.land = part, buf, sib_buf, land
             self.s_send, self.s_recv = s_send, s_recv
             self.tree = SumTree(
                 "seq",
@@ -760,7 +889,7 @@
             return remote(
                 self.buf.at[pl.ds(4 * j + 2 - 2 * core, 2)],
                 self.sib_buf.at[j],
-                self.s_send.at[j],
+                self.s_send,
                 self.s_recv.at[j],
                 {"seq": sib},
             )
@@ -782,29 +911,32 @@
             elif n in (4, 5):
                 self.tree.near_early(order[n][1])
 
-        def begin(self):
+        def begin(self, between=()):
             for n in range(8):
                 self.compute(n)
+                for at, step in between:
+                    if at == n:
+                        step()
                 if n > 2:
                     self.pair(n - 3)
             for n in range(5, 8):
                 self.pair(n)
 
-        def finish(self, total):
-            for h in range(2):
-                total[SPAN * h : SPAN * (h + 1)] = self.tree.total(h)
-            self.tree.sent()
-            for n in range(8):
-                self.to_sib(seq_turn(*order[n]) // 2).wait_send()
+        def total(self):
+            return jnp.concatenate([self.tree.total(h) for h in range(2)], axis=0)
+
+        def sent(self):
+            all_sent(self.land, self.tree.send)
+            all_sent(self.sib_buf, self.s_send)
 
     po = ChipSums(
         lambda j: dot(of_chip(joined, j), wo[...]),
         xh_all,
         po_sib,
         po_land,
-        ps_send,
+        ps_send.at[0],
         ps_recv,
-        p_send,
+        p_send.at[0],
         p_recv,
     )
     hg = ChipSums(
@@ -812,15 +944,16 @@
         cot_all,
         hg_sib,
         hg_land,
-        hs_send,
+        hs_send.at[0],
         hs_recv,
-        h_send,
+        h_send.at[0],
         h_recv,
     )
-    x_tree.sent()
+    all_sent(xh_all.at[pl.ds(0, 30)], x_send.at[0])
     po.begin()
+    cot_tree.near_of_mate()
     cot_tree.far_of_mate()
-    cot_tree.handed(sib_mate)
+    all_here(cot_all.at[pl.ds(0, 16)], c_given.at[0])
 
     @pl.loop(0, 32)
     def _(i):
@@ -849,48 +982,8 @@
         right = dot(joined_t[...], cs[:, pl.ds(pl.multiple_of(i * 256 + 512, 256), 256)])
         units = jnp.concatenate([left.reshape(40, 8, 256), right.reshape(40, 8, 256)], axis=1)
         lanes = pl.ds(pl.multiple_of(i * 256, 256), 256)
-        gof_buf[:, :, lanes] = units[:32].astype(BF16)
-        goa_buf[:, :, lanes] = units[32:].astype(BF16)
-
-    def back_few(r):
-        return remote(
-            gof_buf.at[pl.ds(8 * r, 8)],
-            own_out.at[pl.ds(32, 8)],
-            v_send.at[r],
-            v_recv.at[0],
-            {"seq": 4 + 4 * me + r},
-        )
-
-    def back_many():
-        return remote(
-            goa_buf,
-            own_out.at[pl.ds(8 + 8 * lax.rem(me, 4), 8)],
-            v_send.at[0],
-            v_recv.at[lax.rem(me, 4)],
-            {"seq": (me - 4) // 4},
-        )
-
-    keep_a = pltpu.make_async_copy(goa_buf, own_out.at[pl.ds(0, 8)], local_sem.at[0])
-    keep_f3 = pltpu.make_async_copy(gof_buf, own_out.at[pl.ds(8, 32)], local_sem.at[1])
-    keep_f = pltpu.make_async_copy(gof_buf, own_out.at[pl.ds(0, 32)], local_sem.at[1])
-
-    @pl.when(me < 3)
-    def _():
-        for r in range(4):
-            back_few(r).start()
-
-    @pl.when(me < 4)
-    def _():
-        keep_a.start()
-
-    @pl.when(me == 3)
-    def _():
-        keep_f3.start()
-
-    @pl.when(me > 3)
-    def _():
-        back_many().start()
-        keep_f.start()
+        go_buf[pl.ds(8 * (1 - late), 32), :, lanes] = units[:32].astype(BF16)
+        go_buf[pl.ds(32 * late, 8), :, lanes] = units[32:].astype(BF16)
 
     def grads_by_owner(dst, base, columns):
         sums = jnp.sum(
@@ -919,27 +1012,28 @@
                 ]
                 dst[:, 2 * i + j] = jnp.concatenate(pair, axis=1).astype(BF16)
 
-    def owner_tree(dst, land, send, recv):
-        return SumTree(
+    def owner_sums(dst, land, send, recv):
+        return ColumnSums(
             "dp",
-            lambda slot, h: dst.at[slot, pl.ds(4 * h, 4)],
-            lambda kind, h: land.at[kind, pl.ds(4 * h, 4)],
+            lambda slot: dst.at[slot],
+            land,
             dm,
             dp_turn,
             dp_mate,
-            send,
+            send.at[0],
             recv,
         )
 
-    gf_tree = owner_tree(gf, gf_land, gf_send, gf_recv)
-    go_tree = SumTree(
+    gf_sums = owner_sums(gf, gf_land, gf_send, gf_recv)
+    gq_sums = owner_sums(gq, gq_land, gq_send, gq_recv)
+    go_sums = ColumnSums(
         "dp",
-        lambda slot, h: own_out.at[pl.ds(5 * slot + 2 * h, 2 + h)],
-        lambda kind, h: go_land.at[kind, pl.ds(2 * h, 2 + h)],
+        lambda slot: go_buf.at[pl.ds(5 * slot, 5)],
+        go_land,
         dm,
         dp_turn,
         dp_mate,
-        go_send,
+        go_send.at[0],
         go_recv,
     )
     lanes_d = lane_iota((D, 128))
@@ -951,38 +1045,11 @@
         rows = pl.ds(pl.multiple_of(lax.rem(w, 16) * 64, 64), 64)
         vg[rows] += jnp.where(lanes_h == 64 + 9 + w // 16, cols_f[64 * r : 64 * r + 64], 0.0)
     grads_by_owner(gf, 0, 2)
-    gf_tree.begin()
+    gf_sums.start()
     po.tree.far_of_me()
     po.tree.of_mate()
 
-    def back_arrived():
-        @pl.when(me < 3)
-        def _():
-            for r in range(4):
-                back_few(r).wait_send()
-                remote(
-                    goa_buf,
-                    own_out.at[pl.ds(8 + 8 * r, 8)],
-                    v_send.at[r],
-                    v_recv.at[r],
-                    {"seq": sib},
-                ).wait_recv()
-
-        @pl.when(me < 4)
-        def _():
-            keep_a.wait()
-
-        @pl.when(me == 3)
-        def _():
-            keep_f3.wait()
-
-        @pl.when(me > 3)
-        def _():
-            back_many().wait_send()
-            keep_f.wait()
-            remote(
-                goa_buf, own_out.at[pl.ds(32, 8)], v_send.at[0], v_recv.at[0], {"seq": sib}
-            ).wait_recv()
+    go_sums.start()
 
     for qi in reversed(range(NCH)):
         lanes = slice(qi * CH, (qi + 1) * CH)
@@ -1002,9 +1069,6 @@
                 dvn[keys] += dv
                 dkn[keys] += dk
         dqt[:, lanes] = dq * 0.125
-        if qi == 2:
-            back_arrived()
-            go_tree.begin()
 
     @pl.loop(0, NCH)
     def _(i):
@@ -1021,16 +1085,9 @@
     for i in range(3):
         vg[head_rows] += jnp.where(lanes_h == 68 + i, cols_q[64 * i : 64 * i + 64], 0.0)
     po.tree.near_late()
-    gf_tree.far_of_me()
-    gf_tree.of_mate()
+    gf_sums.middle()
     grads_by_owner(gq, 256, 0)
-
-    def gq_copy(k, to, frm):
-        return remote(gq.at[to], gq_got.at[frm], gq_send.at[k], gq_recv.at[frm], {"dp": to})
-
-    @pl.loop(1, DP)
-    def _(k):
-        gq_copy(k, lax.rem(dm + k, DP), dm).start()
+    gq_sums.start()
 
     slab = jnp.transpose(vg[...])
     for p in range(8):
@@ -1038,40 +1095,31 @@
 
     def vs_copy(k, to, frm):
         return remote(
-            vt_part.at[to // 2], vt_seq.at[frm], vs_send.at[k], vs_recv.at[frm], {"seq": to}
+            vt_part.at[to // 2], vt_seq.at[frm], vs_send.at[0], vs_recv.at[0], {"seq": to}
         )
 
     def vd_copy(k, to, frm):
-        return remote(vt_own, vt_dp.at[frm], vd_send.at[k], vd_recv.at[frm], {"dp": to})
+        return remote(vt_own, vt_dp.at[frm], vd_send.at[0], vd_recv.at[0], {"dp": to})
 
     @pl.loop(1, SEQ)
     def _(k):
         vs_copy(k, lax.rem(me + k, SEQ), me).start()
 
     vt_seq[me] = vt_part[chip]
-    gf_tree.near_late()
-    cot_tree.sent()
-    hg.begin()
-    go_tree.far_of_me()
-    go_tree.of_mate()
-    hg.tree.far_of_me()
-    hg.tree.of_mate()
-
-    @pl.loop(1, SEQ)
-    def _(k):
-        vs_copy(k, me, lax.rem(me + k, SEQ)).wait_recv()
-
-    vt_own[...] = jnp.sum(vt_seq[...], axis=0)
-
-    @pl.loop(1, DP)
-    def _(k):
-        vd_copy(k, lax.rem(dm + k, DP), dm).start()
-
-    vt_dp[dm] = vt_own[...]
-    go_tree.near_late()
+    all_sent(cot_all.at[pl.ds(0, 30)], c_send.at[0])
+
+    def vectors_on():
+        all_here(vt_seq.at[pl.ds(0, SEQ - 1)], vs_recv.at[0])
+        vt_own[...] = jnp.sum(vt_seq[...], axis=0)
+
+        @pl.loop(1, DP)
+        def _(k):
+            vd_copy(k, lax.rem(dm + k, DP), dm).start()
+
+        vt_dp[dm] = vt_own[...]
 
     def to_owner(part, total, send, recv, k, to, frm):
-        return remote(part.at[to], total.at[frm], send.at[k], recv.at[frm], {"seq": to})
+        return remote(part.at[to], total.at[frm], send.at[0], recv.at[0], {"seq": to})
 
     def own_sums(part, total, send, recv):
         @pl.loop(1, SEQ)
@@ -1081,37 +1129,39 @@
         total[me] = part[me]
 
     def own_arrived(part, total, send, recv):
-        @pl.loop(1, SEQ)
-        def _(k):
-            to_owner(part, total, send, recv, k, me, lax.rem(me + k, SEQ)).wait_recv()
+        all_here(total.at[pl.ds(0, SEQ - 1)], recv.at[0])
 
     def squares_of(value):
         return jnp.sum(jnp.sum(value * value, axis=0), axis=0, keepdims=True)
 
-    for h in range(2):
-        f_part[8 * h : 8 * h + 8] = gf_tree.total(h).reshape(8, 8, 256)
-    own_sums(f_part, f_sum, bf_send, bf_recv)
-    squares = squares_of(f_part[...])
-
-    @pl.loop(1, DP)
-    def _(k):
-        gq_copy(k, dm, lax.rem(dm + k, DP)).wait_recv()
-
-    total = gq[dm].astype(F32)
-    for k in range(1, DP):
-        total = total + gq_got[lax.rem(dm + k, DP)].astype(F32)
-    total = total.reshape(SEQ, 8, 256)
-    squares = squares + squares_of(total)
-    for h in range(2):
-        out_total = go_tree.total(h)
-        wout_sum[2 * h : 2 * h + 2 + h] = out_total
-        out_squares = squares_of(out_total)
-        squares = squares + out_squares[:, :256] + out_squares[:, 256:]
-
-    @pl.loop(1, DP)
-    def _(k):
-        vd_copy(k, dm, lax.rem(dm + k, DP)).wait_recv()
-
+    def hidden_on():
+        f_part[...] = gf_sums.total().reshape(SEQ, 8, 256)
+        own_sums(f_part, f_sum, bf_send, bf_recv)
+
+    hg.begin(((5, hidden_on), (6, go_sums.middle), (7, vectors_on)))
+    gq_sums.middle()
+    hg.tree.far_of_me()
+    out_total = go_sums.total()
+    out_part[...] = out_total
+
+    def back_out(u, s, d, slot):
+        at = lax.rem(slot, 5)
+        return remote(
+            out_part.at[u], wout_sum.at[at], v_send.at[u], v_recv.at[at], {"seq": s, "dp": d}
+        )
+
+    def back_in(u):
+        return remote(out_part.at[u], wout_sum.at[u], v_send.at[u], v_recv.at[u], {"seq": sib})
+
+    def keep_total(u):
+        wout_sum[u] = out_part[u]
+
+    trades(lambda u, s, d, slot: back_out(u, s, d, slot).start())
+    kept(keep_total)
+    out_squares = squares_of(out_total)
+    squares = squares_of(f_part[...]) + out_squares[:, :256] + out_squares[:, 256:]
+
+    all_here(vt_dp.at[pl.ds(0, DP - 1)], vd_recv.at[0])
     vec_total = jnp.sum(vt_dp[...], axis=0)
     first = lax.rem(me, 2) * 64 + dm * 8
     lanes = lane_iota(vec_total.shape)
@@ -1121,50 +1171,76 @@
     small[0:16] = vec_total
     small[...] = jnp.transpose(small[...])
     vec_grad[...] = small[pl.ds(pl.multiple_of(first, 8), 8)]
+    vec_store.start()
+    total = gq_sums.total().reshape(SEQ, 8, 256)
+    squares = squares + squares_of(total)
     row = squares[:, :128] + squares[:, 128:] + vec_squares
     mine = jnp.sum(row, axis=1, keepdims=True)
-    q_part[...] = jnp.where(lane_iota(total.shape) < 192, total, mine[None])
+    tile_a[...] = jnp.broadcast_to(mine, (8, 128))
+
+    def ta_copy(k, to, frm):
+        return remote(tile_a, got_a.at[frm], ta_send.at[0], ta_recv.at[0], {"seq": to})
+
+    @pl.loop(1, SEQ)
+    def _(k):
+        ta_copy(k, lax.rem(me + k, SEQ), me).start()
+
+    got_a[me] = tile_a[...]
+    q_part[...] = total
     own_sums(q_part, q_sum, bq_send, bq_recv)
+    hg.tree.of_mate()
     hg.tree.near_late()
-    po.finish(out_sum)
-    own_arrived(q_part, q_sum, bq_send, bq_recv)
-    tile_b[...] = jnp.sum(q_sum[:, :, 128:256], axis=0)
+    all_here(got_a.at[pl.ds(0, SEQ - 1)], ta_recv.at[0])
+    tile_b[...] = jnp.sum(got_a[...], axis=0)
 
     def tb_copy(k, to, frm):
-        return remote(tile_b, got_b.at[frm], tb_send.at[k], tb_recv.at[frm], {"dp": to})
+        return remote(tile_b, got_b.at[frm], tb_send.at[0], tb_recv.at[0], {"dp": to})
 
     @pl.loop(1, DP)
     def _(k):
         tb_copy(k, lax.rem(dm + k, DP), dm).start()
 
     got_b[dm] = tile_b[...]
-
-    @pl.loop(1, DP)
-    def _(k):
-        tb_copy(k, dm, lax.rem(dm + k, DP)).wait_recv()
-
+    own_arrived(f_part, f_sum, bf_send, bf_recv)
+    f_store.start()
+    x_rows, x_hat, inv_std = own_rows()
+    cot_own = own_cot()
+    block_out[...] = (x_rows + po.total() + (vec_ref[7:8] + vec_ref[8:9])).astype(BF16)
+    block_store.start()
+    own_arrived(q_part, q_sum, bq_send, bq_recv)
+    q_store.start()
+    trades(lambda u, s, d, slot: back_in(u).wait_recv())
+    wout_store.start()
+
+    all_here(got_b.at[pl.ds(0, DP - 1)], tb_recv.at[0])
     everything = jnp.sum(got_b[...], axis=0)
-    square_ref[...] = jnp.broadcast_to(everything[:, 127:128], (8, 128))
-    own_arrived(f_part, f_sum, bf_send, bf_recv)
-
-    hg.finish(grad_sum)
-    for tree in (in_tree, out_tree, gf_tree, go_tree):
-        tree.sent()
-
-    @pl.loop(1, DP)
-    def _(k):
-        to = lax.rem(dm + k, DP)
-        tb_copy(k, to, dm).wait_send()
-        gq_copy(k, to, dm).wait_send()
-        vd_copy(k, to, dm).wait_send()
-
-    @pl.loop(1, SEQ)
-    def _(k):
-        to = lax.rem(me + k, SEQ)
-        a_copy(k, to, me).wait_send()
-        vs_copy(k, to, me).wait_send()
-        to_owner(f_part, f_sum, bf_send, bf_recv, k, to, me).wait_send()
-        to_owner(q_part, q_sum, bq_send, bq_recv, k, to, me).wait_send()
+    square_ref[...] = jnp.broadcast_to(everything[:, 0:1], (8, 128))
+    square_store.start()
+    grad = hg.total()
+    back = (
+        grad
+        - jnp.mean(grad, axis=-1, keepdims=True)
+        - x_hat * jnp.mean(grad * x_hat, axis=-1, keepdims=True)
+    )
+    input_grad[...] = (cot_own + inv_std * back).astype(BF16)
+    grad_store.start()
+    po.sent()
+    hg.sent()
+    trades(lambda u, s, d, slot: trade_out(u, s, d, slot).wait_send())
+    trades(lambda u, s, d, slot: back_out(u, s, d, slot).wait_send())
+    for sums in (gf_sums, gq_sums, go_sums):
+        sums.sent()
+    all_sent(win_all.at[pl.ds(0, 7)], l_send.at[0])
+    all_sent(wout_all.at[pl.ds(0, 35)], o_send.at[0])
+    all_sent(win_own.at[pl.ds(0, SEQ - 1)], a_send.at[0])
+    all_sent(vt_seq.at[pl.ds(0, SEQ - 1)], vs_send.at[0])
+    all_sent(vt_dp.at[pl.ds(0, DP - 1)], vd_send.at[0])
+    all_sent(got_a.at[pl.ds(0, SEQ - 1)], ta_send.at[0])
+    all_sent(got_b.at[pl.ds(0, DP - 1)], tb_send.at[0])
+    all_sent(f_part.at[pl.ds(0, SEQ - 1)], bf_send.at[0])
+    all_sent(q_part.at[pl.ds(0, SEQ - 1)], bq_send.at[0])
+    for store in stores:
+        store.wait()
 
 
 def layer_call(span, length, x, cot, w_in, w_out, vectors):
@@ -1172,7 +1248,7 @@
     angles = np.arange(ROW, dtype=np.float32)[None, :] * freqs.astype(np.float32)[:, None]
     cosine, sine = np.cos(angles).astype(np.float32), np.sin(angles).astype(np.float32)
     smem = pl.BlockSpec(memory_space=pltpu.SMEM)
-    vmem = pl.BlockSpec(memory_space=pltpu.VMEM)
+    anywhere = pl.BlockSpec(memory_space=pl.ANY)
     sds = jax.ShapeDtypeStruct
     dma = pltpu.SemaphoreType.DMA
 
@@ -1182,26 +1258,42 @@
     return pl.pallas_call(
         layer_kernel,
         out_shape=(
-            sds((TOK, D), F32),
-            sds((TOK, D), F32),
+            sds((TOK, D), BF16),
+            sds((TOK, D), BF16),
             sds((SEQ, 8, 256), F32),
             sds((SEQ, 8, 256), F32),
             sds((5, 16, 512), F32),
             sds((8, 128), F32),
-            sds((16, D), F32),
             sds((8, 128), F32),
         ),
-        in_specs=[smem] * 2 + [vmem] * 7,
-        out_specs=[vmem] * 8,
+        in_specs=[smem] * 2 + [anywhere] * 7,
+        out_specs=[anywhere] * 7,
         scratch_shapes=[
+            buf((TOK, D)),
+            buf((TOK, D)),
+            buf((8, 7 * D), F32),
+            buf((40, D), F32),
+            buf((8, VEC_ROWS), F32),
+            buf((8, ROW), F32),
+            buf((8, ROW), F32),
+            buf((TOK, D)),
+            buf((TOK, D)),
+            buf((SEQ, 8, 256), F32),
+            buf((SEQ, 8, 256), F32),
+            buf((5, 16, 512), F32),
+            buf((8, 128), F32),
+            buf((8, 128), F32),
+            dma((7,)),
+            dma((7,)),
             pltpu.SMEM((32,), jnp.int32),
             buf((32, SPAN, D)),
             buf((32, SPAN, D)),
             buf((SEQ, 16, 256)),
             buf((DP, SEQ, 16, 256)),
             buf((40, 16, 512)),
-            buf((4, 8, 16, 512)),
+            buf((5, 16, 512)),
             buf((128, 128), F32),
+            buf((16, D), F32),
             buf((ROW, D)),
             buf((ROW, D)),
             buf((D, 512)),
@@ -1227,65 +1319,70 @@
             buf((ROW, 64), F32),
             buf((ROW, 64), F32),
             buf((D, 128), F32),
-            buf((8, 16, 512)),
-            buf((32, 16, 512)),
             buf((40, 16, 512)),
+            buf((5, 16, 512), F32),
             buf((DP, 8, 16, 256)),
             buf((DP, 8, 16, 256)),
             buf((8, 2, SPAN, D)),
             buf((8, 2, SPAN, D)),
             buf((7, 2, SPAN, D)),
             buf((7, 2, SPAN, D)),
-            buf((7, 8, 16, 256)),
-            buf((DP, 8, 16, 256)),
+            buf((8, 8, 16, 256)),
+            buf((8, 8, 16, 256)),
             buf((8, 16, 128), F32),
             buf((SEQ, 16, 128), F32),
             buf((16, 128), F32),
             buf((DP, 16, 128), F32),
-            buf((7, 5, 16, 512)),
+            buf((8, 5, 16, 512)),
             buf((SEQ, 8, 256), F32),
             buf((SEQ, 8, 256), F32),
             buf((8, 128), F32),
+            buf((8, 128), F32),
+            buf((SEQ, 8, 128), F32),
             buf((DP, 8, 128), F32),
-            dma((2,)),
-            dma((SEQ,)),
-            dma((SEQ,)),
-            dma((32,)),
-            dma((SEQ, 2)),
-            dma((32,)),
-            dma((SEQ, 2)),
-            dma((16,)),
+            dma((1,)),
+            dma((1,)),
+            dma((1,)),
+            dma((1,)),
+            dma((8, 2)),
+            dma((1,)),
+            dma((1,)),
+            dma((8, 2)),
+            dma((1,)),
+            dma((1,)),
             dma((DP, 2)),
-            dma((16,)),
+            dma((1,)),
             dma((DP, 2)),
-            dma((4,)),
-            dma((4,)),
+            dma((5,)),
+            dma((5,)),
+            dma((1,)),
             dma((8,)),
+            dma((1,)),
+            dma((7, 2)),
+            dma((1,)),
             dma((8,)),
-            dma((16,)),
+            dma((1,)),
             dma((7, 2)),
-            dma((8,)),
-            dma((8,)),
-            dma((16,)),
-            dma((7, 2)),
-            dma((16,)),
-            dma((7, 2)),
-            dma((DP,)),
-            dma((DP,)),
-            dma((16,)),
-            dma((7, 2)),
-            dma((4,)),
-            dma((4,)),
-            dma((SEQ,)),
-            dma((SEQ,)),
-            dma((SEQ,)),
-            dma((SEQ,)),
-            dma((SEQ,)),
-            dma((SEQ,)),
-            dma((DP,)),
-            dma((DP,)),
-            dma((DP,)),
-            dma((DP,)),
+            dma((1,)),
+            dma((3,)),
+            dma((1,)),
+            dma((3,)),
+            dma((1,)),
+            dma((3,)),
+            dma((5,)),
+            dma((5,)),
+            dma((1,)),
+            dma((1,)),
+            dma((1,)),
+            dma((1,)),
+            dma((1,)),
+            dma((1,)),
+            dma((1,)),
+            dma((1,)),
+            dma((1,)),
+            dma((1,)),
+            dma((1,)),
+            dma((1,)),
         ],
         compiler_params=pltpu.CompilerParams(
             collective_id=0, has_side_effects=True, vmem_limit_bytes=VMEM_LIMIT
@@ -1307,6 +1404,8 @@
 
 
 UPDATE_IN = (
+    ("block_out", (TOK, D), BF16),
+    ("input_grad", (TOK, D), BF16),
     ("square", (8, 128), F32),
     ("f_sum", (SEQ, 8, 256), F32),
     ("q_sum", (SEQ, 8, 256), F32),
@@ -1320,17 +1419,11 @@
     ("vectors", (8, VEC_ROWS), F32),
     ("vec_first", (8, VEC_ROWS), F32),
     ("vec_second", (8, VEC_ROWS), F32),
-    ("x", (TOK, D), BF16),
-    ("cot", (TOK, D), BF16),
-    ("grad_sum", (TOK, D), F32),
-    ("out_sum", (TOK, D), F32),
-    ("vec", (16, D), F32),
     ("vec_grad", (8, 128), F32),
 )
 UPDATE_OUT = (
     ((TOK, D), BF16),
     ((TOK, D), BF16),
-    ((8, 128), F32),
     ((8, 7 * D), F32),
     ((40, D), F32),
     ((8, VEC_ROWS), F32),
@@ -1346,20 +1439,22 @@
 )
 
 
-def update_kernel(span_ref, len_ref, *refs):
+def update_kernel(*refs):
     ins, refs = refs[: len(UPDATE_IN)], refs[len(UPDATE_IN) :]
+    norm_ref, refs = refs[0], refs[1:]
     outs, refs = refs[: len(UPDATE_OUT)], refs[len(UPDATE_OUT) :]
     in_bufs, refs = refs[: len(UPDATE_IN)], refs[len(UPDATE_IN) :]
     out_bufs, (in_sem, out_sem, grad_in) = refs[: len(UPDATE_OUT)], refs[len(UPDATE_OUT) :]
-    me = lax.axis_index("seq")
     loads = [
         pltpu.make_async_copy(a, b, in_sem.at[i]) for i, (a, b) in enumerate(zip(ins, in_bufs))
     ]
     stores = [
-        pltpu.make_async_copy(b, a, out_sem.at[i]) for i, (a, b) in enumerate(zip(outs, out_bufs))
+        pltpu.make_async_copy(in_bufs[i] if i < 2 else b, a, out_sem.at[i])
+        for i, (a, b) in enumerate(zip(outs, out_bufs))
     ]
-    for load in loads:
-        load.start()
+    order = list(range(2, len(loads))) + [0, 1]
+    for i in order:
+        loads[i].start()
     names = [name for name, _, _ in UPDATE_IN]
 
     def take(name):
@@ -1372,9 +1467,12 @@
         stores[i].start()
 
     norm = jnp.sqrt(take("square")[...])
-    give(2, norm)
+    norm_ref[0, 0] = norm[0, 0]
     factor = jnp.minimum(1.0, CLIP_NORM / norm)[0:1, 0:1]
 
+    for i in range(2):
+        loads[i].wait()
+        stores[i].start()
     f_sum, q_sum = take("f_sum"), take("q_sum")
     for s in range(SEQ):
         for j, p in enumerate(PIECES[s]):
@@ -1393,48 +1491,32 @@
         for k, value in enumerate(values):
             give(at + 3 * k, value)
 
-    matrix(3, grad_in[...], "w_in", "in_first", "in_second", RATE_MATRIX, DECAY_RATE)
+    matrix(2, grad_in[...], "w_in", "in_first", "in_second", RATE_MATRIX, DECAY_RATE)
     sums = take("wout_sum")
     grad_out = jnp.concatenate([unfold(sums[u]) for u in range(5)], axis=0)
-    matrix(4, grad_out, "w_out", "out_first", "out_second", RATE_MATRIX, DECAY_RATE)
+    matrix(3, grad_out, "w_out", "out_first", "out_second", RATE_MATRIX, DECAY_RATE)
     grad_vec = take("vec_grad")[:, 0:VEC_ROWS]
-    matrix(5, grad_vec, "vectors", "vec_first", "vec_second", RATE_VECTOR, 0.0)
-
-    x_rows = take("x")[...].astype(F32)
-    centered = x_rows - jnp.mean(x_rows, axis=-1, keepdims=True)
-    inv_std = lax.rsqrt(jnp.mean(centered * centered, axis=-1, keepdims=True) + NORM_EPS)
-    x_hat = centered * inv_std
-    row = lax.broadcasted_iota(jnp.int32, (TOK, 1), 0)
-    place = jnp.where(row < SPAN, span_ref[0, me] * SPAN + row, span_ref[1, me] * SPAN + row - SPAN)
-    cot = jnp.where(place < len_ref[0], take("cot")[...].astype(F32), 0.0)
-    grad = take("grad_sum")[...]
-    back = (
-        grad
-        - jnp.mean(grad, axis=-1, keepdims=True)
-        - x_hat * jnp.mean(grad * x_hat, axis=-1, keepdims=True)
-    )
-    give(1, (cot + inv_std * back).astype(BF16))
-    out, vec = take("out_sum")[...], take("vec")
-    give(0, (x_rows + out + (vec[7:8] + vec[8:9])).astype(BF16))
+    matrix(4, grad_vec, "vectors", "vec_first", "vec_second", RATE_VECTOR, 0.0)
+
     for store in stores:
         store.wait()
 
 
-def update_call(span, length, *args):
-    smem = pl.BlockSpec(memory_space=pltpu.SMEM)
+def update_call(*args):
     anywhere = pl.BlockSpec(memory_space=pl.ANY)
     dma = pltpu.SemaphoreType.DMA
+    sds = jax.ShapeDtypeStruct
     return pl.pallas_call(
         update_kernel,
-        out_shape=tuple(jax.ShapeDtypeStruct(shape, kind) for shape, kind in UPDATE_OUT),
-        in_specs=[smem] * 2 + [anywhere] * len(UPDATE_IN),
-        out_specs=[anywhere] * len(UPDATE_OUT),
+        out_shape=(sds((1, 1), F32),) + tuple(sds(shape, kind) for shape, kind in UPDATE_OUT),
+        in_specs=[anywhere] * len(UPDATE_IN),
+        out_specs=[pl.BlockSpec(memory_space=pltpu.SMEM)] + [anywhere] * len(UPDATE_OUT),
         scratch_shapes=[pltpu.VMEM(shape, kind) for _, shape, kind in UPDATE_IN]
         + [pltpu.VMEM(shape, kind) for shape, kind in UPDATE_OUT]
         + [dma((len(UPDATE_IN),)), dma((len(UPDATE_OUT),)), pltpu.VMEM((8, 7 * D), F32)],
         compiler_params=pltpu.CompilerParams(vmem_limit_bytes=UPDATE_LIMIT),
         name="clipped_update",
-    )(span, length, *args)
+    )(*args)
 
 
 def body(
@@ -1452,13 +1534,12 @@
     lengths,
     span_of,
 ):
-    span = span_of.T
-    out_sum, grad_sum, f_sum, q_sum, wout_sum, squares, vec_full, vec_grad = layer_call(
-        span, lengths, hidden_in[0], out_cot[0], in_weight, out_weight, vectors.T
+    block_out, input_grad, f_sum, q_sum, wout_sum, squares, vec_grad = layer_call(
+        span_of.T, lengths, hidden_in[0], out_cot[0], in_weight, out_weight, vectors.T
     )
-    outs = update_call(
-        span,
-        lengths,
+    norm, block_out, input_grad, *rest = update_call(
+        block_out,
+        input_grad,
         squares,
         f_sum,
         q_sum,
@@ -1472,16 +1553,10 @@
         vectors.T,
         vec_first.T,
         vec_second.T,
-        hidden_in[0],
-        out_cot[0],
-        grad_sum,
-        out_sum,
-        vec_full,
         vec_grad,
     )
-    block_out, input_grad, norm = outs[:3]
-    rest = [out.T if i % 3 == 2 else out for i, out in enumerate(outs[3:])]
-    return (block_out[None], input_grad[None], norm[0, 0], *rest)
+    rest = [out.T if i % 3 == 2 else out for i, out in enumerate(rest)]
+    return (block_out[None], input_grad[None], norm.reshape(()), *rest)
 
 
 def solution(mesh):

time: 125 us -> 116 us (0.928)
  Pallas kernels: 122 us -> 115 us
    pallas_call x2, Pallas kernels: 122 us -> 115 us  [the longest x1 111 us: layer_call(): pl.pallas_call(layer_kernel, out_shape=(sds((TOK, D), BF16), sds((TOK, D)...]
where the time goes in v4:
time: 116 us
  Pallas kernels  115 us (99%)
  between operations  1.46 us (1%)
    pallas_call x1, Pallas kernels, layer_call(): pl.pallas_call(layer_kernel, out_shape=(sds((TOK, D), BF16), sds((TOK, D)...  111 us
    pallas_call x1, Pallas kernels, update_call(): pl.pallas_call(update_kernel, out_shape=(sds((1, 1), F32),) + tuple((sds(...  4.06 us

profile of v4, /device:TPU:1, one launch (start us, length us, event | category | flops | bytes accessed | tf_op | source)
XLA Modules:
  0.0 116.0 jit_solution(12658927489842288501)
XLA Ops:
  1.3 110.5 %layer_of_one_row.1 = (bf16[128,1024]{1,0:T(8,128)(2,1)}, bf16[128,1024]{1,0:T(8,128)(2,1)}, f32[16,8,256]{2,1,0:T(8,128)}, f32[16,8,256]{2,1,0:T(8,128)}, f32[5...) custom-call(s32[2,16]{1,0:T(2,128)} %bitcast.19, s32[1]{0:T(128)S(6)} %copy.30.len_ref, ...), custom_call_target="tpu_custom_call" | custom-call | tf_op jit(solution)/shard_map/layer_of_one_row/pallas_call | solution.py:1258
  111.8 4.1 %clipped_update.1 = (f32[1,1]{1,0:T(1,128)}, bf16[128,1024]{1,0:T(8,128)(2,1)}, bf16[128,1024]{1,0:T(8,128)(2,1)}, f32[8,7168]{1,0:T(8,128)}, f32[40,1024]{1,0:T...) custom-call(bf16[128,1024]{1,0:T(8,128)(2,1)} %get-tuple-element.37., ...), custom_call_target="tpu_custom_call" | custom-call | tf_op jit(solution)/shard_map/clipped_update/pallas_call | solution.py:1509

commit v5 on v4

--- a/solution.py
+++ b/solution.py
@@ -99,29 +99,8 @@
         )
 
 
-def await_greetings(me, dm):
-    barrier = pltpu.get_barrier_semaphore()
-
-    def wait_if(condition, more):
-        @pl.when(condition)
-        def _():
-            pl.semaphore_wait(barrier, SEQ + DP - 2 + more)
-
-    @pl.when(me < 3)
-    def _():
-        wait_if(dm == 0, 0)
-        wait_if(dm == 1, 2)
-        wait_if(dm > 1, 5)
-
-    @pl.when(me == 3)
-    def _():
-        pl.semaphore_wait(barrier, SEQ + DP - 2)
-
-    @pl.when(me > 3)
-    def _():
-        wait_if(dm < 6, 0)
-        wait_if(dm == 6, 3)
-        wait_if(dm == 7, 5)
+def await_greetings():
+    pl.semaphore_wait(pltpu.get_barrier_semaphore(), SEQ + DP - 2)
 
 
 def all_sent(ref, sem):
@@ -404,6 +383,8 @@
     win_all,
     wout_all,
     wout_own,
+    w_relay,
+    v_relay,
     small,
     vec_ref,
     xs,
@@ -441,10 +422,6 @@
     hg_land,
     gf_land,
     gq_land,
-    vt_part,
-    vt_seq,
-    vt_own,
-    vt_dp,
     go_land,
     f_part,
     q_part,
@@ -489,10 +466,6 @@
     bq_recv,
     ta_send,
     ta_recv,
-    vs_send,
-    vs_recv,
-    vd_send,
-    vd_recv,
     tb_send,
     tb_recv,
 ):
@@ -532,7 +505,7 @@
             )
         )
     ]
-    def trades(step):
+    def units_of(step):
         for u in range(5):
             i = 5 * dm + u
 
@@ -540,15 +513,148 @@
             def _(u=u, i=i):
                 @pl.when(i >= 8)
                 def _():
-                    k = lax.rem(i, 8)
-                    step(u, 4 * me + 3 + i // 8, (32 + k) // 5, 32 + k)
+                    step.few(u, i)
 
             @pl.when(me > 3)
             def _(u=u, i=i):
+                r = lax.rem(me, 4)
+
                 @pl.when(i >= 32)
                 def _():
-                    slot = 8 + 8 * lax.rem(me, 4) + i - 32
-                    step(u, (me - 4) // 4, slot // 5, slot)
+                    @pl.when(r < 3)
+                    def _():
+                        step.many(u, i, 8 + 8 * r + i - 32)
+
+                    @pl.when(r == 3)
+                    def _():
+                        step.straight(u, i)
+
+                @pl.when((i >= 8 + 8 * r) & (i < 16 + 8 * r) & (r < 3))
+                def _():
+                    step.between(u, i, 32 + lax.rem(i, 8))
+
+    class Trade:
+        def __init__(self, src, dst, relay, base, send, recv):
+            self.src, self.dst, self.relay, self.base = src, dst, relay, base
+            self.send, self.recv = send, recv
+
+        def place(self, u):
+            return self.dst.at[self.base + u]
+
+        def few_out(self, u, i):
+            to = 4 * me + 3 + i // 8
+            last = i >= 32
+
+            @pl.when(last)
+            def _():
+                remote(
+                    self.src.at[u], self.place(u), self.send.at[0, u], self.recv.at[0, u], {"seq": to}
+                ).start()
+
+            @pl.when(jnp.logical_not(last))
+            def _():
+                remote(
+                    self.src.at[u],
+                    self.relay.at[0, u],
+                    self.send.at[0, u],
+                    self.recv.at[1, u],
+                    {"seq": to},
+                ).start()
+
+        def many_out(self, u, i, far):
+            at = lax.rem(far, 5)
+            return remote(
+                self.src.at[u],
+                self.relay.at[1, at],
+                self.send.at[0, u],
+                self.recv.at[2, at],
+                {"dp": far // 5},
+            )
+
+        def straight_out(self, u):
+            return remote(
+                self.src.at[u],
+                self.place(u),
+                self.send.at[0, u],
+                self.recv.at[0, u],
+                {"seq": (me - 4) // 4},
+            )
+
+        def on_to_few(self, u):
+            return remote(
+                self.relay.at[1, u],
+                self.place(u),
+                self.send.at[1, u],
+                self.recv.at[0, u],
+                {"seq": (me - 4) // 4},
+            )
+
+        def on_to_many(self, u, far):
+            at = lax.rem(far, 5)
+            base = self.base - 5 * dm + far - at if self.whole else self.base
+            return remote(
+                self.relay.at[0, u],
+                self.dst.at[base + at],
+                self.send.at[2, u],
+                self.recv.at[0, at],
+                {"dp": far // 5},
+            )
+
+        def arrived(self, ref, sem):
+            remote(ref, ref, self.send.at[0, 0], sem, {"seq": sib}).wait_recv()
+
+        def begin(self):
+            class Step:
+                few = staticmethod(self.few_out)
+                many = staticmethod(lambda u, i, far: self.many_out(u, i, far).start())
+                straight = staticmethod(lambda u, i: self.straight_out(u).start())
+                between = staticmethod(lambda u, i, far: None)
+
+            units_of(Step)
+
+        def relay_on(self):
+            def between(u, i, far):
+                self.arrived(self.relay.at[0, u], self.recv.at[1, u])
+                self.on_to_many(u, far).start()
+                self.arrived(self.relay.at[1, u], self.recv.at[2, u])
+                self.on_to_few(u).start()
+
+            class Step:
+                few = staticmethod(lambda u, i: None)
+                many = staticmethod(lambda u, i, far: None)
+                straight = staticmethod(lambda u, i: None)
+
+            Step.between = staticmethod(between)
+            units_of(Step)
+
+        def end(self):
+            class Step:
+                few = staticmethod(lambda u, i: self.arrived(self.place(u), self.recv.at[0, u]))
+                many = staticmethod(
+                    lambda u, i, far: self.arrived(self.place(u), self.recv.at[0, u])
+                )
+                straight = staticmethod(lambda u, i: self.arrived(self.place(u), self.recv.at[0, u]))
+                between = staticmethod(lambda u, i, far: None)
+
+            units_of(Step)
+
+        def sent(self):
+            def done(k, u):
+                remote(
+                    self.src.at[u], self.src.at[u], self.send.at[k, u], self.recv.at[0, u], {"seq": sib}
+                ).wait_send()
+
+            def between(u, i, far):
+                done(1, u)
+                done(2, u)
+
+            class Step:
+                few = staticmethod(lambda u, i: done(0, u))
+                many = staticmethod(lambda u, i, far: done(0, u))
+                straight = staticmethod(lambda u, i: done(0, u))
+
+            Step.between = staticmethod(between)
+            units_of(Step)
 
     def kept(step):
         for u in range(5):
@@ -570,12 +676,6 @@
                 def _():
                     step(u)
 
-    barrier = pltpu.get_barrier_semaphore()
-    trades(
-        lambda u, s, d, slot: pl.semaphore_signal(
-            barrier, inc=1, device_id={"seq": s, "dp": d}, device_id_type=MESH
-        )
-    )
     greet(me, dm)
     for load in loads:
         load.start()
@@ -683,27 +783,14 @@
             win_own.at[to], win_all.at[dm, frm], a_send.at[0], a_recv.at[0], {"seq": to}
         )
 
-    await_greetings(me, dm)
+    await_greetings()
 
     @pl.loop(1, SEQ)
     def _(k):
         a_copy(k, lax.rem(me + k, SEQ), me).start()
 
-    def trade_out(u, s, d, slot):
-        return remote(
-            wout_own.at[u],
-            wout_all.at[slot],
-            w_send.at[u],
-            w_recv.at[lax.rem(slot, 5)],
-            {"seq": s, "dp": d},
-        )
-
-    def trade_in(u):
-        return remote(
-            wout_own.at[u], wout_all.at[5 * dm + u], w_send.at[u], w_recv.at[u], {"seq": sib}
-        )
-
-    trades(lambda u, s, d, slot: trade_out(u, s, d, slot).start())
+    out_trade = Trade(wout_own, wout_all, w_relay, 5 * dm, w_send, w_recv)
+    out_trade.whole = True
     x_tree.own_to_mate()
     x_tree.own_to_ring()
     keep.wait()
@@ -712,16 +799,13 @@
 
     in_tree.own_to_mate()
     in_tree.own_to_ring()
-    trades(lambda u, s, d, slot: trade_in(u).wait_recv())
-    out_tree.own_to_mate()
-    out_tree.own_to_ring()
+    out_trade.begin()
     x_tree.near_of_me()
     x_tree.of_mate()
     in_tree.near_of_me()
     in_tree.of_mate()
-    out_tree.near_of_me()
-    out_tree.of_mate()
     x_tree.far_of_me()
+    out_trade.relay_on()
     in_tree.far_of_me()
     cot_tree.own_to_ring()
 
@@ -745,11 +829,14 @@
 
     zero_row = jnp.zeros((1, 256), F32)
     sums = lax.fori_loop(0, SEQ, unpack(dm // 4), (zero_row, zero_row))
+    in_tree.near_of_mate()
     x_tree.near_of_mate()
+    out_trade.end()
+    out_tree.own_to_mate()
+    out_tree.own_to_ring()
     cot_tree.own_to_mate()
-    in_tree.near_of_mate()
     in_tree.far_of_mate()
-    cot_tree.near_of_me()
+    x_tree.far_of_mate()
     cq, cf = lax.fori_loop(0, SEQ, unpack(dp_mate // 4), sums)
 
     slab = jnp.transpose(wr[:, 384:512].astype(F32))
@@ -773,7 +860,6 @@
     head_vecs = wr[head_rows, 384:512].astype(F32)
     bq, bk, bv = (head_vecs[:, 68 + i : 69 + i] for i in range(3))
 
-    x_tree.far_of_mate()
     all_here(xh_all.at[pl.ds(0, 16)], x_given.at[0])
 
     @pl.loop(0, 32)
@@ -781,8 +867,6 @@
         rows = pl.ds(pl.multiple_of(i * SPAN, SPAN), SPAN)
         xs[rows] = xh_all[inv_ref[i]]
 
-    out_tree.near_of_mate()
-    out_tree.far_of_me()
 
     aug = jnp.where(lax.broadcasted_iota(jnp.int32, (64, CH), 0) == 0, 1.0, 0.0)
     zeros_aug = jnp.zeros((64, CH), F32)
@@ -826,11 +910,17 @@
         joined_t[0:256, rows] = jnp.transpose(activ).astype(BF16)
         dact[rows] = cdf + pre * pdf
 
-    pl.loop(0, 2)(project)
+    project(0)
+    cot_tree.near_of_me()
+    out_tree.near_of_me()
+    out_tree.of_mate()
+    project(1)
+    project(2)
     cot_tree.of_mate()
+    project(3)
     cot_tree.far_of_me()
-    pl.loop(2, NCH)(project)
-    out_tree.far_of_mate()
+    out_tree.near_of_mate()
+    out_tree.far_of_me()
     causal = lax.broadcasted_iota(jnp.int32, (CH, CH), 0) <= lane_iota((CH, CH))
 
     def scores(kc, qi):
@@ -854,6 +944,8 @@
         lse[:, lanes] = jnp.broadcast_to(top + jnp.log(total), (8, CH))
         joined_t[256:320, lanes] = out.astype(BF16)
         joined[8 * qi : 8 * qi + 8, :, 256:320] = jnp.transpose(out).astype(BF16).reshape(8, SPAN, HEAD)
+    out_tree.far_of_mate()
+
     def put_units(base, at, count):
         @pl.loop(0, count // 2)
         def _(i):
@@ -865,8 +957,10 @@
     put_units(8 * (1 - late), 0, 32)
     put_units(32 * late, 256, 8)
 
-    def of_chip(ref, j):
-        return jnp.concatenate([ref[span_ref[i % 2, 2 * j + i // 2]] for i in range(4)], axis=0)
+    def of_chips(ref, chips):
+        return jnp.concatenate(
+            [ref[span_ref[i % 2, 2 * j + i // 2]] for j in chips for i in range(4)], axis=0
+        )
 
     order = [(mate, 2), (mate, 1), (mate, 3), (me, 2), (me, 3), (me, 1), (mate, 0), (me, 0)]
 
@@ -895,9 +989,11 @@
             )
 
         def compute(self, n):
-            j = seq_turn(*order[n]) // 2
-            self.buf[pl.ds(4 * j, 4)] = self.part(j).astype(BF16).reshape(4, SPAN, D)
-            self.to_sib(j).start()
+            chips = [seq_turn(*order[m]) // 2 for m in (n, n + 1)]
+            value = self.part(chips).astype(BF16).reshape(8, SPAN, D)
+            for m, j in enumerate(chips):
+                self.buf[pl.ds(4 * j, 4)] = value[4 * m : 4 * m + 4]
+                self.to_sib(j).start()
 
         def pair(self, n):
             j = seq_turn(*order[n]) // 2
@@ -913,14 +1009,19 @@
 
         def begin(self, between=()):
             for n in range(8):
-                self.compute(n)
+                if n % 2 == 0:
+                    self.compute(n)
                 for at, step in between:
                     if at == n:
                         step()
                 if n > 2:
                     self.pair(n - 3)
-            for n in range(5, 8):
-                self.pair(n)
+            self.pair(5)
+
+        def of_mate(self):
+            self.pair(6)
+            self.tree.of_mate()
+            self.pair(7)
 
         def total(self):
             return jnp.concatenate([self.tree.total(h) for h in range(2)], axis=0)
@@ -930,7 +1031,7 @@
             all_sent(self.sib_buf, self.s_send)
 
     po = ChipSums(
-        lambda j: dot(of_chip(joined, j), wo[...]),
+        lambda chips: dot(of_chips(joined, chips), wo[...]),
         xh_all,
         po_sib,
         po_land,
@@ -940,7 +1041,7 @@
         p_recv,
     )
     hg = ChipSums(
-        lambda j: dot_nt(of_chip(mixed, j), wp[...]),
+        lambda chips: dot_nt(of_chips(mixed, chips), wp[...]),
         cot_all,
         hg_sib,
         hg_land,
@@ -950,9 +1051,7 @@
         h_recv,
     )
     all_sent(xh_all.at[pl.ds(0, 30)], x_send.at[0])
-    po.begin()
-    cot_tree.near_of_mate()
-    cot_tree.far_of_mate()
+    po.begin(((4, cot_tree.near_of_mate), (5, cot_tree.far_of_mate)))
     all_here(cot_all.at[pl.ds(0, 16)], c_given.at[0])
 
     @pl.loop(0, 32)
@@ -960,7 +1059,7 @@
         rows = pl.ds(pl.multiple_of(i * SPAN, SPAN), SPAN)
         cs[rows] = cot_all[inv_ref[i]]
 
-    @pl.loop(0, NCH)
+    @pl.loop(0, NCH, unroll=True)
     def _(i):
         rows = pl.ds(pl.multiple_of(i * CH, CH), CH)
         cot = cs[rows]
@@ -976,7 +1075,9 @@
         mixed[pl.ds(8 * i, 8), :, 0:256] = pg.astype(BF16).reshape(8, SPAN, 256)
         mixed_t[0:256, rows] = jnp.transpose(pg).astype(BF16)
 
-    @pl.loop(0, 2)
+    po.tree.far_of_me()
+
+    @pl.loop(0, 2, unroll=True)
     def _(i):
         left = dot(joined_t[...], cs[:, pl.ds(pl.multiple_of(i * 256, 256), 256)])
         right = dot(joined_t[...], cs[:, pl.ds(pl.multiple_of(i * 256 + 512, 256), 256)])
@@ -990,7 +1091,7 @@
             mixed[:, :, base : base + 256].reshape(ROW, 256).astype(F32), axis=0, keepdims=True
         )
 
-        @pl.loop(0, 4)
+        @pl.loop(0, 4, unroll=True)
         def _(i):
             rows = pl.ds(pl.multiple_of(i * 256, 256), 256)
             h = jnp.transpose(dot(mixed_t[base : base + 256], xs[:, rows]))
@@ -1004,7 +1105,10 @@
                 extra = extra + jnp.where(
                     lanes == 64 + columns + j, jnp.sum(col, axis=1, keepdims=True), 0.0
                 )
-            vg[rows] = extra
+            if base:
+                grad = jnp.concatenate([grad[:, :128], grad[:, 128:] + extra], axis=1)
+            else:
+                vg[rows] = extra
             for j in range(2):
                 pair = [
                     grad[128 * j + 64 * t : 128 * j + 64 * t + 64].reshape(8, 8, 256)
@@ -1046,8 +1150,7 @@
         vg[rows] += jnp.where(lanes_h == 64 + 9 + w // 16, cols_f[64 * r : 64 * r + 64], 0.0)
     grads_by_owner(gf, 0, 2)
     gf_sums.start()
-    po.tree.far_of_me()
-    po.tree.of_mate()
+    po.of_mate()
 
     go_sums.start()
 
@@ -1069,8 +1172,12 @@
                 dvn[keys] += dv
                 dkn[keys] += dk
         dqt[:, lanes] = dq * 0.125
-
-    @pl.loop(0, NCH)
+        if qi == 2:
+            po.tree.near_late()
+        if qi == 1:
+            gf_sums.middle()
+
+    @pl.loop(0, NCH, unroll=True)
     def _(i):
         rows = pl.ds(pl.multiple_of(i * CH, CH), CH)
         cosine, sine = cos_ref[:, rows], sin_ref[:, rows]
@@ -1084,39 +1191,10 @@
     cols_q = jnp.sum(mixed_t[256:448].astype(F32), axis=1, keepdims=True)
     for i in range(3):
         vg[head_rows] += jnp.where(lanes_h == 68 + i, cols_q[64 * i : 64 * i + 64], 0.0)
-    po.tree.near_late()
-    gf_sums.middle()
     grads_by_owner(gq, 256, 0)
     gq_sums.start()
 
-    slab = jnp.transpose(vg[...])
-    for p in range(8):
-        vt_part[p] = slab[64:80, 128 * p : 128 * p + 128]
-
-    def vs_copy(k, to, frm):
-        return remote(
-            vt_part.at[to // 2], vt_seq.at[frm], vs_send.at[0], vs_recv.at[0], {"seq": to}
-        )
-
-    def vd_copy(k, to, frm):
-        return remote(vt_own, vt_dp.at[frm], vd_send.at[0], vd_recv.at[0], {"dp": to})
-
-    @pl.loop(1, SEQ)
-    def _(k):
-        vs_copy(k, lax.rem(me + k, SEQ), me).start()
-
-    vt_seq[me] = vt_part[chip]
     all_sent(cot_all.at[pl.ds(0, 30)], c_send.at[0])
-
-    def vectors_on():
-        all_here(vt_seq.at[pl.ds(0, SEQ - 1)], vs_recv.at[0])
-        vt_own[...] = jnp.sum(vt_seq[...], axis=0)
-
-        @pl.loop(1, DP)
-        def _(k):
-            vd_copy(k, lax.rem(dm + k, DP), dm).start()
-
-        vt_dp[dm] = vt_own[...]
 
     def to_owner(part, total, send, recv, k, to, frm):
         return remote(part.at[to], total.at[frm], send.at[0], recv.at[0], {"seq": to})
@@ -1138,69 +1216,61 @@
         f_part[...] = gf_sums.total().reshape(SEQ, 8, 256)
         own_sums(f_part, f_sum, bf_send, bf_recv)
 
-    hg.begin(((5, hidden_on), (6, go_sums.middle), (7, vectors_on)))
+    hg.begin(((1, hidden_on), (2, go_sums.middle)))
     gq_sums.middle()
-    hg.tree.far_of_me()
     out_total = go_sums.total()
     out_part[...] = out_total
 
-    def back_out(u, s, d, slot):
-        at = lax.rem(slot, 5)
-        return remote(
-            out_part.at[u], wout_sum.at[at], v_send.at[u], v_recv.at[at], {"seq": s, "dp": d}
-        )
-
-    def back_in(u):
-        return remote(out_part.at[u], wout_sum.at[u], v_send.at[u], v_recv.at[u], {"seq": sib})
+    out_back = Trade(out_part, wout_sum, v_relay, 0, v_send, v_recv)
+    out_back.whole = False
 
     def keep_total(u):
         wout_sum[u] = out_part[u]
 
-    trades(lambda u, s, d, slot: back_out(u, s, d, slot).start())
+    out_back.begin()
     kept(keep_total)
     out_squares = squares_of(out_total)
     squares = squares_of(f_part[...]) + out_squares[:, :256] + out_squares[:, 256:]
 
-    all_here(vt_dp.at[pl.ds(0, DP - 1)], vd_recv.at[0])
-    vec_total = jnp.sum(vt_dp[...], axis=0)
-    first = lax.rem(me, 2) * 64 + dm * 8
-    lanes = lane_iota(vec_total.shape)
-    vec_mine = jnp.where((lanes >= first) & (lanes < first + 8), vec_total, 0.0)
-    vec_squares = jnp.sum(vec_mine * vec_mine, axis=0, keepdims=True)
+    hg.tree.far_of_me()
+    total = gq_sums.total().reshape(SEQ, 8, 256)
+    weights = jnp.where(lane_iota(total.shape) < 192, total, 0.0)
+    squares = squares + squares_of(weights)
+    tile_a[0:8] = jnp.broadcast_to(squares[:, :128] + squares[:, 128:], (8, 128))
+    tile_a[8:24] = jnp.transpose(total[:, :, 128:].reshape(128, 128))[64:80]
+
+    def ta_copy(k, to, frm):
+        return remote(tile_a, got_a.at[frm], ta_send.at[0], ta_recv.at[0], {"seq": to})
+
+    @pl.loop(1, SEQ)
+    def _(k):
+        ta_copy(k, lax.rem(me + k, SEQ), me).start()
+
+    got_a[me] = tile_a[...]
+    q_part[...] = total
+    own_sums(q_part, q_sum, bq_send, bq_recv)
+    out_back.relay_on()
+    hg.of_mate()
+    hg.tree.near_late()
+    all_here(got_a.at[pl.ds(0, SEQ - 1)], ta_recv.at[0])
+    sums = jnp.sum(got_a[...], axis=0)
+    vec_total = sums[8:24]
+    row = sums[0:1] + jnp.sum(vec_total * vec_total, axis=0, keepdims=True)
+    tile_b[...] = jnp.broadcast_to(jnp.sum(row, axis=1, keepdims=True), (8, 128))
+
+    def tb_copy(k, to, frm):
+        return remote(tile_b, got_b.at[frm], tb_send.at[0], tb_recv.at[0], {"dp": to})
+
+    @pl.loop(1, DP)
+    def _(k):
+        tb_copy(k, lax.rem(dm + k, DP), dm).start()
+
+    got_b[dm] = tile_b[...]
     small[...] = jnp.zeros((128, 128), F32)
     small[0:16] = vec_total
     small[...] = jnp.transpose(small[...])
-    vec_grad[...] = small[pl.ds(pl.multiple_of(first, 8), 8)]
+    vec_grad[...] = small[pl.ds(pl.multiple_of(8 * me, 8), 8)]
     vec_store.start()
-    total = gq_sums.total().reshape(SEQ, 8, 256)
-    squares = squares + squares_of(total)
-    row = squares[:, :128] + squares[:, 128:] + vec_squares
-    mine = jnp.sum(row, axis=1, keepdims=True)
-    tile_a[...] = jnp.broadcast_to(mine, (8, 128))
-
-    def ta_copy(k, to, frm):
-        return remote(tile_a, got_a.at[frm], ta_send.at[0], ta_recv.at[0], {"seq": to})
-
-    @pl.loop(1, SEQ)
-    def _(k):
-        ta_copy(k, lax.rem(me + k, SEQ), me).start()
-
-    got_a[me] = tile_a[...]
-    q_part[...] = total
-    own_sums(q_part, q_sum, bq_send, bq_recv)
-    hg.tree.of_mate()
-    hg.tree.near_late()
-    all_here(got_a.at[pl.ds(0, SEQ - 1)], ta_recv.at[0])
-    tile_b[...] = jnp.sum(got_a[...], axis=0)
-
-    def tb_copy(k, to, frm):
-        return remote(tile_b, got_b.at[frm], tb_send.at[0], tb_recv.at[0], {"dp": to})
-
-    @pl.loop(1, DP)
-    def _(k):
-        tb_copy(k, lax.rem(dm + k, DP), dm).start()
-
-    got_b[dm] = tile_b[...]
     own_arrived(f_part, f_sum, bf_send, bf_recv)
     f_store.start()
     x_rows, x_hat, inv_std = own_rows()
@@ -1209,7 +1279,7 @@
     block_store.start()
     own_arrived(q_part, q_sum, bq_send, bq_recv)
     q_store.start()
-    trades(lambda u, s, d, slot: back_in(u).wait_recv())
+    out_back.end()
     wout_store.start()
 
     all_here(got_b.at[pl.ds(0, DP - 1)], tb_recv.at[0])
@@ -1226,15 +1296,13 @@
     grad_store.start()
     po.sent()
     hg.sent()
-    trades(lambda u, s, d, slot: trade_out(u, s, d, slot).wait_send())
-    trades(lambda u, s, d, slot: back_out(u, s, d, slot).wait_send())
+    out_trade.sent()
+    out_back.sent()
     for sums in (gf_sums, gq_sums, go_sums):
         sums.sent()
     all_sent(win_all.at[pl.ds(0, 7)], l_send.at[0])
     all_sent(wout_all.at[pl.ds(0, 35)], o_send.at[0])
     all_sent(win_own.at[pl.ds(0, SEQ - 1)], a_send.at[0])
-    all_sent(vt_seq.at[pl.ds(0, SEQ - 1)], vs_send.at[0])
-    all_sent(vt_dp.at[pl.ds(0, DP - 1)], vd_send.at[0])
     all_sent(got_a.at[pl.ds(0, SEQ - 1)], ta_send.at[0])
     all_sent(got_b.at[pl.ds(0, DP - 1)], tb_send.at[0])
     all_sent(f_part.at[pl.ds(0, SEQ - 1)], bf_send.at[0])
@@ -1292,6 +1360,8 @@
             buf((DP, SEQ, 16, 256)),
             buf((40, 16, 512)),
             buf((5, 16, 512)),
+            buf((2, 5, 16, 512)),
+            buf((2, 5, 16, 512), F32),
             buf((128, 128), F32),
             buf((16, D), F32),
             buf((ROW, D)),
@@ -1329,16 +1399,12 @@
             buf((7, 2, SPAN, D)),
             buf((8, 8, 16, 256)),
             buf((8, 8, 16, 256)),
-            buf((8, 16, 128), F32),
-            buf((SEQ, 16, 128), F32),
-            buf((16, 128), F32),
-            buf((DP, 16, 128), F32),
             buf((8, 5, 16, 512)),
             buf((SEQ, 8, 256), F32),
             buf((SEQ, 8, 256), F32),
+            buf((24, 128), F32),
             buf((8, 128), F32),
-            buf((8, 128), F32),
-            buf((SEQ, 8, 128), F32),
+            buf((SEQ, 24, 128), F32),
             buf((DP, 8, 128), F32),
             dma((1,)),
             dma((1,)),
@@ -1353,8 +1419,8 @@
             dma((DP, 2)),
             dma((1,)),
             dma((DP, 2)),
-            dma((5,)),
-            dma((5,)),
+            dma((3, 5)),
+            dma((3, 5)),
             dma((1,)),
             dma((8,)),
             dma((1,)),
@@ -1369,12 +1435,8 @@
             dma((3,)),
             dma((1,)),
             dma((3,)),
-            dma((5,)),
-            dma((5,)),
-            dma((1,)),
-            dma((1,)),
-            dma((1,)),
-            dma((1,)),
+            dma((3, 5)),
+            dma((3, 5)),
             dma((1,)),
             dma((1,)),
             dma((1,)),

time: 116 us -> 104 us (0.90)
  Pallas kernels: 115 us -> 102 us
    pallas_call x1, Pallas kernels: 111 us -> 98.4 us  [layer_call(): pl.pallas_call(layer_kernel, out_shape=(sds((TOK, D), BF16), sds((TOK, D)...]
where the time goes in v5:
time: 104 us
  Pallas kernels  102 us (98%)
  between operations  1.48 us (1%)
    pallas_call x1, Pallas kernels, layer_call(): pl.pallas_call(layer_kernel, out_shape=(sds((TOK, D), BF16), sds((TOK, D)...  98.4 us
    pallas_call x1, Pallas kernels, update_call(): pl.pallas_call(update_kernel, out_shape=(sds((1, 1), F32),) + tuple((sds(...  4.06 us

profile of v5, /device:TPU:1, one launch (start us, length us, event | category | flops | bytes accessed | tf_op | source)
XLA Modules:
  0.0 103.9 jit_solution(3668252267343699622)
XLA Ops:
  1.3 98.4 %layer_of_one_row.1 = (bf16[128,1024]{1,0:T(8,128)(2,1)}, bf16[128,1024]{1,0:T(8,128)(2,1)}, f32[16,8,256]{2,1,0:T(8,128)}, f32[16,8,256]{2,1,0:T(8,128)}, f32[5...) custom-call(s32[2,16]{1,0:T(2,128)} %bitcast.19, s32[1]{0:T(128)S(6)} %copy.30.len_ref, ...), custom_call_target="tpu_custom_call" | custom-call | tf_op jit(solution)/shard_map/layer_of_one_row/pallas_call | solution.py:1326
  99.7 4.1 %clipped_update.1 = (f32[1,1]{1,0:T(1,128)}, bf16[128,1024]{1,0:T(8,128)(2,1)}, bf16[128,1024]{1,0:T(8,128)(2,1)}, f32[8,7168]{1,0:T(8,128)}, f32[40,1024]{1,0:T...) custom-call(bf16[128,1024]{1,0:T(8,128)(2,1)} %get-tuple-element.37., ...), custom_call_target="tpu_custom_call" | custom-call | tf_op jit(solution)/shard_map/clipped_update/pallas_call | solution.py:1571

commit v6 on v5

--- a/solution.py
+++ b/solution.py
@@ -137,9 +137,8 @@
         ).wait_recv()
 
     def own_to_ring(self):
-        for h in range(2):
-            for k in (1, 3):
-                self.put(self.me, h, self.turn(self.me, k))
+        for h, k in ((0, 1), (1, 3), (1, 1), (0, 3)):
+            self.put(self.me, h, self.turn(self.me, k))
 
     def own_to_mate(self):
         for h in range(2):
@@ -147,21 +146,29 @@
         for h in range(2):
             self.hand(self.me, h)
 
-    def of_mate(self):
-        for h in range(2):
+    def of_mate(self, halves=(0, 1)):
+        for h in halves:
             self.got(self.mate, h)
             for k in (1, 3):
                 self.put(self.mate, h, self.turn(self.me, k))
             self.hand(self.mate, h)
 
+    def near_first(self, base):
+        for h, k in ((0, 3), (1, 1)):
+            slot = self.turn(base, k)
+            self.got(slot, h)
+            self.put(slot, h, self.turn(self.me, 4 - k))
+            self.hand(slot, h)
+
+    def near_rest(self, base):
+        for h, k in ((1, 3), (0, 1)):
+            slot = self.turn(base, k)
+            self.got(slot, h)
+            self.hand(slot, h)
+
     def near(self, base):
-        for h in range(2):
-            for k in (3, 1):
-                slot = self.turn(base, k)
-                self.got(slot, h)
-                if (k == 3) == (h == 0):
-                    self.put(slot, h, self.turn(self.me, 4 - k))
-                self.hand(slot, h)
+        self.near_first(base)
+        self.near_rest(base)
 
     def near_of_me(self):
         self.near(self.me)
@@ -191,37 +198,31 @@
 
 
 class SumTree:
-    def __init__(self, axis, piece, land, me, turn, mate, send, recv):
-        self.axis, self.piece, self.land, self.me, self.turn, self.mate = (
-            axis,
-            piece,
-            land,
-            me,
-            turn,
-            mate,
-        )
-        self.send, self.recv = send, recv
+    def __init__(self, axis, piece, landing, me, turn, mate, send, recv):
+        self.axis, self.piece, self.me, self.turn, self.mate = (axis, piece, me, turn, mate)
+        self.landing, self.send, self.recv = landing, send, recv
+
+    def land(self, kind, h):
+        return self.landing.at[kind, h]
+
+    def arrival(self, kind, h):
+        return self.recv.at[(h, 2, 2, 3 + h, 5, 5, 5)[kind]]
 
     def put(self, slot, kind, h, to):
         copy = remote(
             self.piece(slot, h),
             self.land(kind, h),
             self.send,
-            self.recv.at[kind, h],
+            self.arrival(kind, h),
             {self.axis: to},
         )
         copy.start()
-
-    def got(self, kind, h):
-        part = self.land(kind, h)
-        remote(part, part, self.send, self.recv.at[kind, h], {self.axis: self.mate}).wait_recv()
-        return part[...].astype(F32)
 
     def add(self, slot, h, *kinds):
         part = self.piece(slot, h)
         total = part[...].astype(F32)
         for kind in kinds:
-            total = total + self.got(kind, h)
+            total = total + self.land(kind, h)[...].astype(F32)
         part[...] = total.astype(BF16)
 
     def far_of_mate(self):
@@ -239,6 +240,7 @@
     def far_of_me(self):
         slot = self.turn(self.me, 2)
         for h in range(2):
+            all_here(self.land(0, h), self.arrival(0, h))
             self.add(slot, h, 0)
             self.put(slot, 3, h, self.turn(self.me, 3 - 2 * h))
 
@@ -246,10 +248,12 @@
         for h in range(2):
             k = 3 - 2 * h
             slot = self.turn(self.me, k)
+            all_here(self.land(3, h), self.arrival(3, h))
             self.add(slot, h, 3)
             self.put(slot, 4 + h, h, self.turn(self.me, k))
 
     def of_mate(self):
+        all_here(self.landing.at[pl.ds(1, 2)], self.arrival(1, 0))
         for h in range(2):
             self.add(self.mate, h, 1, 2)
             self.put(self.mate, 6, h, self.mate)
@@ -261,11 +265,15 @@
         for k in (1, 3):
             self.near_early(k)
 
-    def total(self, h):
-        value = self.piece(self.me, h)[...].astype(F32)
-        for kind in (4, 5, 6):
-            value = value + self.got(kind, h)
-        return value
+    def total(self):
+        all_here(self.landing.at[pl.ds(4, 3)], self.arrival(4, 0))
+        parts = []
+        for h in range(2):
+            value = self.piece(self.me, h)[...].astype(F32)
+            for kind in (4, 5, 6):
+                value = value + self.land(kind, h)[...].astype(F32)
+            parts.append(value)
+        return jnp.concatenate(parts, axis=0)
 
 
 class ColumnSums:
@@ -355,9 +363,8 @@
     sin_any,
     block_out_any,
     input_grad_any,
-    f_sum_any,
-    q_sum_any,
-    wout_sum_any,
+    grad_in_any,
+    grad_out_any,
     square_any,
     vec_grad_any,
     x_ref,
@@ -369,6 +376,8 @@
     sin_ref,
     block_out,
     input_grad,
+    grad_in,
+    grad_out,
     f_sum,
     q_sum,
     wout_sum,
@@ -491,15 +500,14 @@
             )
         )
     ]
-    block_store, grad_store, f_store, q_store, wout_store, square_store, vec_store = stores = [
+    block_store, grad_store, in_store, out_store, square_store, vec_store = stores = [
         pltpu.make_async_copy(a, b, store_sem.at[i])
         for i, (a, b) in enumerate(
             (
                 (block_out, block_out_any),
                 (input_grad, input_grad_any),
-                (f_sum, f_sum_any),
-                (q_sum, q_sum_any),
-                (wout_sum, wout_sum_any),
+                (grad_in, grad_in_any),
+                (grad_out, grad_out_any),
                 (square_ref, square_any),
                 (vec_grad, vec_grad_any),
             )
@@ -557,7 +565,7 @@
                     self.src.at[u],
                     self.relay.at[0, u],
                     self.send.at[0, u],
-                    self.recv.at[1, u],
+                    self.recv.at[0, u],
                     {"seq": to},
                 ).start()
 
@@ -567,7 +575,7 @@
                 self.src.at[u],
                 self.relay.at[1, at],
                 self.send.at[0, u],
-                self.recv.at[2, at],
+                self.recv.at[1, at],
                 {"dp": far // 5},
             )
 
@@ -595,7 +603,7 @@
             return remote(
                 self.relay.at[0, u],
                 self.dst.at[base + at],
-                self.send.at[2, u],
+                self.send.at[0, u],
                 self.recv.at[0, at],
                 {"dp": far // 5},
             )
@@ -614,9 +622,9 @@
 
         def relay_on(self):
             def between(u, i, far):
-                self.arrived(self.relay.at[0, u], self.recv.at[1, u])
+                self.arrived(self.relay.at[0, u], self.recv.at[0, u])
                 self.on_to_many(u, far).start()
-                self.arrived(self.relay.at[1, u], self.recv.at[2, u])
+                self.arrived(self.relay.at[1, u], self.recv.at[1, u])
                 self.on_to_few(u).start()
 
             class Step:
@@ -646,7 +654,7 @@
 
             def between(u, i, far):
                 done(1, u)
-                done(2, u)
+                done(0, u)
 
             class Step:
                 few = staticmethod(lambda u, i: done(0, u))
@@ -791,6 +799,7 @@
 
     out_trade = Trade(wout_own, wout_all, w_relay, 5 * dm, w_send, w_recv)
     out_trade.whole = True
+    out_trade.begin()
     x_tree.own_to_mate()
     x_tree.own_to_ring()
     keep.wait()
@@ -799,13 +808,15 @@
 
     in_tree.own_to_mate()
     in_tree.own_to_ring()
-    out_trade.begin()
-    x_tree.near_of_me()
-    x_tree.of_mate()
-    in_tree.near_of_me()
+    out_trade.relay_on()
+    x_tree.near_first(me)
+    x_tree.of_mate((0,))
+    in_tree.near_first(dm)
+    x_tree.near_rest(me)
+    x_tree.of_mate((1,))
+    in_tree.near_rest(dm)
     in_tree.of_mate()
     x_tree.far_of_me()
-    out_trade.relay_on()
     in_tree.far_of_me()
     cot_tree.own_to_ring()
 
@@ -862,12 +873,6 @@
 
     all_here(xh_all.at[pl.ds(0, 16)], x_given.at[0])
 
-    @pl.loop(0, 32)
-    def _(i):
-        rows = pl.ds(pl.multiple_of(i * SPAN, SPAN), SPAN)
-        xs[rows] = xh_all[inv_ref[i]]
-
-
     aug = jnp.where(lax.broadcasted_iota(jnp.int32, (64, CH), 0) == 0, 1.0, 0.0)
     zeros_aug = jnp.zeros((64, CH), F32)
 
@@ -885,7 +890,8 @@
     def project(i):
         start = pl.multiple_of(i * CH, CH)
         rows = pl.ds(start, CH)
-        xh = xs[rows]
+        xh = jnp.concatenate([xh_all[inv_ref[8 * i + k]] for k in range(8)], axis=0)
+        xs[rows] = xh
         first = dot(xh, wp[...])
         qkv = jnp.transpose(first[:, 256:] + cq)
         cosine, sine = cos_ref[:, rows], sin_ref[:, rows]
@@ -921,29 +927,43 @@
     cot_tree.far_of_me()
     out_tree.near_of_mate()
     out_tree.far_of_me()
-    causal = lax.broadcasted_iota(jnp.int32, (CH, CH), 0) <= lane_iota((CH, CH))
-
-    def scores(kc, qi):
-        s = dot(kn[kc * CH : (kc + 1) * CH], qt[:, qi * CH : (qi + 1) * CH])
-        if kc == qi:
-            s = jnp.where(causal, s, NEG_FILL)
+    half = CH // 2
+
+    def tiles(qi):
+        below = [(kc * CH, CH, qi * CH, CH) for kc in range(qi)]
+        return below + [(qi * CH, half, qi * CH, CH), (qi * CH + half, half, qi * CH + half, half)]
+
+    def scores(k0, keys, q0, queries):
+        s = dot(kn[k0 : k0 + keys], qt[:, q0 : q0 + queries])
+        if k0 >= q0:
+            shape = (keys, queries)
+            seen = lax.broadcasted_iota(jnp.int32, shape, 0) <= lane_iota(shape)
+            s = jnp.where(seen, s, NEG_FILL)
         return s
+
+    def spread(value, queries, fill):
+        if queries == CH:
+            return value
+        return jnp.concatenate([jnp.full_like(value, fill), value], axis=1)
 
     for qi in range(NCH):
         lanes = slice(qi * CH, (qi + 1) * CH)
-        parts = [scores(kc, qi) for kc in range(qi + 1)]
-        top = functools.reduce(jnp.maximum, [jnp.max(s, axis=0, keepdims=True) for s in parts])
+        parts = [(t, scores(*t)) for t in tiles(qi)]
+        tops = [spread(jnp.max(s, axis=0, keepdims=True), t[3], NEG_FILL) for t, s in parts]
+        top = functools.reduce(jnp.maximum, tops)
         total = jnp.zeros((1, CH), F32)
         out = jnp.zeros((64, CH), F32)
-        for kc, s in enumerate(parts):
-            p = jnp.exp(s - top)
-            total = total + jnp.sum(p, axis=0, keepdims=True)
-            out = out + dot(vt[:, kc * CH : (kc + 1) * CH], p.astype(BF16))
+        for (k0, keys, _, queries), s in parts:
+            p = jnp.exp(s - top[:, CH - queries :])
+            total = total + spread(jnp.sum(p, axis=0, keepdims=True), queries, 0.0)
+            out = out + spread(dot(vt[:, k0 : k0 + keys], p.astype(BF16)), queries, 0.0)
         out = out / total
         ot[:, lanes] = out
         lse[:, lanes] = jnp.broadcast_to(top + jnp.log(total), (8, CH))
         joined_t[256:320, lanes] = out.astype(BF16)
-        joined[8 * qi : 8 * qi + 8, :, 256:320] = jnp.transpose(out).astype(BF16).reshape(8, SPAN, HEAD)
+        joined[8 * qi : 8 * qi + 8, :, 256:320] = (
+            jnp.transpose(out).astype(BF16).reshape(8, SPAN, HEAD)
+        )
     out_tree.far_of_mate()
 
     def put_units(base, at, count):
@@ -971,7 +991,7 @@
             self.tree = SumTree(
                 "seq",
                 lambda slot, h: buf.at[2 * slot + h],
-                lambda kind, h: land.at[kind, h],
+                land,
                 me,
                 seq_turn,
                 mate,
@@ -1024,7 +1044,7 @@
             self.pair(7)
 
         def total(self):
-            return jnp.concatenate([self.tree.total(h) for h in range(2)], axis=0)
+            return self.tree.total()
 
         def sent(self):
             all_sent(self.land, self.tree.send)
@@ -1051,18 +1071,14 @@
         h_recv,
     )
     all_sent(xh_all.at[pl.ds(0, 30)], x_send.at[0])
-    po.begin(((4, cot_tree.near_of_mate), (5, cot_tree.far_of_mate)))
+    po.begin(((2, cot_tree.near_of_mate), (4, cot_tree.far_of_mate)))
     all_here(cot_all.at[pl.ds(0, 16)], c_given.at[0])
-
-    @pl.loop(0, 32)
-    def _(i):
-        rows = pl.ds(pl.multiple_of(i * SPAN, SPAN), SPAN)
-        cs[rows] = cot_all[inv_ref[i]]
 
     @pl.loop(0, NCH, unroll=True)
     def _(i):
         rows = pl.ds(pl.multiple_of(i * CH, CH), CH)
-        cot = cs[rows]
+        cot = jnp.concatenate([cot_all[inv_ref[8 * i + k]] for k in range(8)], axis=0)
+        cs[rows] = cot
         back = dot_nt(cot, wo[...])
         ag = back[:, 256:].astype(BF16).astype(F32)
         ag_t = jnp.transpose(ag)
@@ -1074,8 +1090,6 @@
         pg = back[:, :256] * dact[rows]
         mixed[pl.ds(8 * i, 8), :, 0:256] = pg.astype(BF16).reshape(8, SPAN, 256)
         mixed_t[0:256, rows] = jnp.transpose(pg).astype(BF16)
-
-    po.tree.far_of_me()
 
     @pl.loop(0, 2, unroll=True)
     def _(i):
@@ -1153,28 +1167,29 @@
     po.of_mate()
 
     go_sums.start()
+    po.tree.far_of_me()
 
     for qi in reversed(range(NCH)):
         lanes = slice(qi * CH, (qi + 1) * CH)
         dq = jnp.zeros((64, CH), F32)
-        for kc in range(qi + 1):
-            keys = slice(kc * CH, (kc + 1) * CH)
-            p = jnp.exp(scores(kc, qi) - lse[0:1, lanes])
-            dp = dot(vn[keys, 0:64], dot_t[:, lanes])
-            ds = (p * (dp - delta[0:1, lanes])).astype(BF16)
-            dv = dot(p.astype(BF16), dot_n[lanes])
-            dk = dot(ds, qn[lanes, 0:64])
-            dq = dq + dot(kt[:, keys], ds)
+        for k0, keys, q0, queries in tiles(qi):
+            at, cols = slice(k0, k0 + keys), slice(q0, q0 + queries)
+            p = jnp.exp(scores(k0, keys, q0, queries) - lse[0:1, cols])
+            dp = dot(vn[at, 0:64], dot_t[:, cols])
+            ds = (p * (dp - delta[0:1, cols])).astype(BF16)
+            dv = dot(p.astype(BF16), dot_n[cols])
+            dk = dot(ds, qn[cols, 0:64])
+            dq = dq + spread(dot(kt[:, at], ds), queries, 0.0)
             if qi == NCH - 1:
-                dvn[keys] = dv
-                dkn[keys] = dk
+                dvn[at] = dv
+                dkn[at] = dk
             else:
-                dvn[keys] += dv
-                dkn[keys] += dk
+                dvn[at] += dv
+                dkn[at] += dk
         dqt[:, lanes] = dq * 0.125
-        if qi == 2:
+        if qi == 1:
             po.tree.near_late()
-        if qi == 1:
+        if qi == 0:
             gf_sums.middle()
 
     @pl.loop(0, NCH, unroll=True)
@@ -1216,7 +1231,7 @@
         f_part[...] = gf_sums.total().reshape(SEQ, 8, 256)
         own_sums(f_part, f_sum, bf_send, bf_recv)
 
-    hg.begin(((1, hidden_on), (2, go_sums.middle)))
+    hg.begin(((2, go_sums.middle), (4, hidden_on)))
     gq_sums.middle()
     out_total = go_sums.total()
     out_part[...] = out_total
@@ -1236,8 +1251,8 @@
     total = gq_sums.total().reshape(SEQ, 8, 256)
     weights = jnp.where(lane_iota(total.shape) < 192, total, 0.0)
     squares = squares + squares_of(weights)
-    tile_a[0:8] = jnp.broadcast_to(squares[:, :128] + squares[:, 128:], (8, 128))
-    tile_a[8:24] = jnp.transpose(total[:, :, 128:].reshape(128, 128))[64:80]
+    tile_a[...] = jnp.transpose(total[:, :, 128:].reshape(128, 128))[64:80]
+    tile_a[15:16] = squares[:, :128] + squares[:, 128:]
 
     def ta_copy(k, to, frm):
         return remote(tile_a, got_a.at[frm], ta_send.at[0], ta_recv.at[0], {"seq": to})
@@ -1249,13 +1264,13 @@
     got_a[me] = tile_a[...]
     q_part[...] = total
     own_sums(q_part, q_sum, bq_send, bq_recv)
-    out_back.relay_on()
     hg.of_mate()
     hg.tree.near_late()
+    out_back.relay_on()
     all_here(got_a.at[pl.ds(0, SEQ - 1)], ta_recv.at[0])
     sums = jnp.sum(got_a[...], axis=0)
-    vec_total = sums[8:24]
-    row = sums[0:1] + jnp.sum(vec_total * vec_total, axis=0, keepdims=True)
+    vec_total = jnp.where(lax.broadcasted_iota(jnp.int32, sums.shape, 0) < VEC_ROWS, sums, 0.0)
+    row = sums[15:16] + jnp.sum(vec_total * vec_total, axis=0, keepdims=True)
     tile_b[...] = jnp.broadcast_to(jnp.sum(row, axis=1, keepdims=True), (8, 128))
 
     def tb_copy(k, to, frm):
@@ -1272,15 +1287,23 @@
     vec_grad[...] = small[pl.ds(pl.multiple_of(8 * me, 8), 8)]
     vec_store.start()
     own_arrived(f_part, f_sum, bf_send, bf_recv)
-    f_store.start()
     x_rows, x_hat, inv_std = own_rows()
     cot_own = own_cot()
     block_out[...] = (x_rows + po.total() + (vec_ref[7:8] + vec_ref[8:9])).astype(BF16)
     block_store.start()
     own_arrived(q_part, q_sum, bq_send, bq_recv)
-    q_store.start()
+    for s in range(SEQ):
+        for j, p in enumerate(PIECES[s]):
+            at = 64 * int(p)
+            if j < 3:
+                grad_in[:, at : at + 64] = q_sum[s, :, 64 * j : 64 * j + 64]
+            else:
+                grad_in[:, at : at + 64] = f_sum[s, :, 64 * j - 192 : 64 * j - 128]
+    in_store.start()
     out_back.end()
-    wout_store.start()
+    for u in range(5):
+        grad_out[8 * u : 8 * u + 8] = unfold(wout_sum[u])
+    out_store.start()
 
     all_here(got_b.at[pl.ds(0, DP - 1)], tb_recv.at[0])
     everything = jnp.sum(got_b[...], axis=0)
@@ -1328,14 +1351,13 @@
         out_shape=(
             sds((TOK, D), BF16),
             sds((TOK, D), BF16),
-            sds((SEQ, 8, 256), F32),
-            sds((SEQ, 8, 256), F32),
-            sds((5, 16, 512), F32),
+            sds((8, 7 * D), F32),
+            sds((40, D), F32),
             sds((8, 128), F32),
             sds((8, 128), F32),
         ),
         in_specs=[smem] * 2 + [anywhere] * 7,
-        out_specs=[anywhere] * 7,
+        out_specs=[anywhere] * 6,
         scratch_shapes=[
             buf((TOK, D)),
             buf((TOK, D)),
@@ -1346,13 +1368,15 @@
             buf((8, ROW), F32),
             buf((TOK, D)),
             buf((TOK, D)),
+            buf((8, 7 * D), F32),
+            buf((40, D), F32),
             buf((SEQ, 8, 256), F32),
             buf((SEQ, 8, 256), F32),
             buf((5, 16, 512), F32),
             buf((8, 128), F32),
             buf((8, 128), F32),
             dma((7,)),
-            dma((7,)),
+            dma((6,)),
             pltpu.SMEM((32,), jnp.int32),
             buf((32, SPAN, D)),
             buf((32, SPAN, D)),
@@ -1402,9 +1426,9 @@
             buf((8, 5, 16, 512)),
             buf((SEQ, 8, 256), F32),
             buf((SEQ, 8, 256), F32),
-            buf((24, 128), F32),
+            buf((16, 128), F32),
             buf((8, 128), F32),
-            buf((SEQ, 24, 128), F32),
+            buf((SEQ, 16, 128), F32),
             buf((DP, 8, 128), F32),
             dma((1,)),
             dma((1,)),
@@ -1419,24 +1443,24 @@
             dma((DP, 2)),
             dma((1,)),
             dma((DP, 2)),
-            dma((3, 5)),
-            dma((3, 5)),
+            dma((2, 5)),
+            dma((2, 5)),
             dma((1,)),
             dma((8,)),
             dma((1,)),
-            dma((7, 2)),
+            dma((6,)),
             dma((1,)),
             dma((8,)),
             dma((1,)),
-            dma((7, 2)),
+            dma((6,)),
             dma((1,)),
             dma((3,)),
             dma((1,)),
             dma((3,)),
             dma((1,)),
             dma((3,)),
-            dma((3, 5)),
-            dma((3, 5)),
+            dma((2, 5)),
+            dma((2, 5)),
             dma((1,)),
             dma((1,)),
             dma((1,)),
@@ -1469,12 +1493,11 @@
     ("block_out", (TOK, D), BF16),
     ("input_grad", (TOK, D), BF16),
     ("square", (8, 128), F32),
-    ("f_sum", (SEQ, 8, 256), F32),
-    ("q_sum", (SEQ, 8, 256), F32),
+    ("grad_in", (8, 7 * D), F32),
     ("w_in", (8, 7 * D), F32),
     ("in_first", (8, 7 * D), F32),
     ("in_second", (8, 7 * D), F32),
-    ("wout_sum", (5, 16, 512), F32),
+    ("grad_out", (40, D), F32),
     ("w_out", (40, D), F32),
     ("out_first", (40, D), F32),
     ("out_second", (40, D), F32),
@@ -1506,7 +1529,7 @@
     norm_ref, refs = refs[0], refs[1:]
     outs, refs = refs[: len(UPDATE_OUT)], refs[len(UPDATE_OUT) :]
     in_bufs, refs = refs[: len(UPDATE_IN)], refs[len(UPDATE_IN) :]
-    out_bufs, (in_sem, out_sem, grad_in) = refs[: len(UPDATE_OUT)], refs[len(UPDATE_OUT) :]
+    out_bufs, (in_sem, out_sem) = refs[: len(UPDATE_OUT)], refs[len(UPDATE_OUT) :]
     loads = [
         pltpu.make_async_copy(a, b, in_sem.at[i]) for i, (a, b) in enumerate(zip(ins, in_bufs))
     ]
@@ -1535,16 +1558,6 @@
     for i in range(2):
         loads[i].wait()
         stores[i].start()
-    f_sum, q_sum = take("f_sum"), take("q_sum")
-    for s in range(SEQ):
-        for j, p in enumerate(PIECES[s]):
-            p = int(p)
-            piece = (
-                q_sum[s, :, 64 * j : 64 * j + 64]
-                if j < 3
-                else f_sum[s, :, 64 * (j - 3) : 64 * (j - 3) + 64]
-            )
-            grad_in[:, 64 * p : 64 * p + 64] = piece
 
     def matrix(at, grad, weight, first, second, rate, decay):
         values = adam(
@@ -1553,10 +1566,8 @@
         for k, value in enumerate(values):
             give(at + 3 * k, value)
 
-    matrix(2, grad_in[...], "w_in", "in_first", "in_second", RATE_MATRIX, DECAY_RATE)
-    sums = take("wout_sum")
-    grad_out = jnp.concatenate([unfold(sums[u]) for u in range(5)], axis=0)
-    matrix(3, grad_out, "w_out", "out_first", "out_second", RATE_MATRIX, DECAY_RATE)
+    matrix(2, take("grad_in")[...], "w_in", "in_first", "in_second", RATE_MATRIX, DECAY_RATE)
+    matrix(3, take("grad_out")[...], "w_out", "out_first", "out_second", RATE_MATRIX, DECAY_RATE)
     grad_vec = take("vec_grad")[:, 0:VEC_ROWS]
     matrix(4, grad_vec, "vectors", "vec_first", "vec_second", RATE_VECTOR, 0.0)
 
@@ -1575,7 +1586,7 @@
         out_specs=[pl.BlockSpec(memory_space=pltpu.SMEM)] + [anywhere] * len(UPDATE_OUT),
         scratch_shapes=[pltpu.VMEM(shape, kind) for _, shape, kind in UPDATE_IN]
         + [pltpu.VMEM(shape, kind) for shape, kind in UPDATE_OUT]
-        + [dma((len(UPDATE_IN),)), dma((len(UPDATE_OUT),)), pltpu.VMEM((8, 7 * D), F32)],
+        + [dma((len(UPDATE_IN),)), dma((len(UPDATE_OUT),))],
         compiler_params=pltpu.CompilerParams(vmem_limit_bytes=UPDATE_LIMIT),
         name="clipped_update",
     )(*args)
@@ -1596,19 +1607,18 @@
     lengths,
     span_of,
 ):
-    block_out, input_grad, f_sum, q_sum, wout_sum, squares, vec_grad = layer_call(
+    block_out, input_grad, grad_in, grad_out, squares, vec_grad = layer_call(
         span_of.T, lengths, hidden_in[0], out_cot[0], in_weight, out_weight, vectors.T
     )
     norm, block_out, input_grad, *rest = update_call(
         block_out,
         input_grad,
         squares,
-        f_sum,
-        q_sum,
+        grad_in,
         in_weight,
         in_first,
         in_second,
-        wout_sum,
+        grad_out,
         out_weight,
         out_first,
         out_second,

time: 104 us -> 99.8 us (0.960)
  Pallas kernels: 102 us -> 97.8 us
    pallas_call x1, Pallas kernels: 98.4 us -> 93.9 us  [layer_call(): pl.pallas_call(layer_kernel, out_shape=(sds((TOK, D), BF16), sds((TOK, D)...]
where the time goes in v6:
time: 99.8 us; the launch traced here: 99.2 us
  Pallas kernels  97.8 us (98%)
  between operations  1.48 us (1%)
    pallas_call x1, Pallas kernels, layer_call(): pl.pallas_call(layer_kernel, out_shape=(sds((TOK, D), BF16), sds((TOK, D)...  93.9 us
    pallas_call x1, Pallas kernels, update_call(): pl.pallas_call(update_kernel, out_shape=(sds((1, 1), F32),) + tuple((sds(...  3.9 us

profile of v6, /device:TPU:1, one launch (start us, length us, event | category | flops | bytes accessed | tf_op | source)
XLA Modules:
  0.0 99.2 jit_solution(17540198587572163390)
XLA Ops:
  1.3 93.9 %layer_of_one_row.1 = (bf16[128,1024]{1,0:T(8,128)(2,1)}, bf16[128,1024]{1,0:T(8,128)(2,1)}, f32[8,7168]{1,0:T(8,128)}, f32[40,1024]{1,0:T(8,128)}, f32[8,128]{1,0:T(8,128)}, /*index=5*/f32[8,128]{1,0:T(8,128)}) custom-call(s32[2,16]{1,0:T(2,128)} %bitcast.19, s32[1]{0:T(128)S(6)} %copy.30.len_ref, bf16[128,1024]{1,0:T(8,128)(2,1)} %bitcast.13, ...), custom_call_target="tpu_custom_call" | custom-call | tf_op jit(solution)/shard_map/layer_of_one_row/pallas_call | solution.py:1349
  95.2 3.9 %clipped_update.1 = (f32[1,1]{1,0:T(1,128)}, bf16[128,1024]{1,0:T(8,128)(2,1)}, bf16[128,1024]{1,0:T(8,128)(2,1)}, f32[8,7168]{1,0:T(8,128)}, f32[40,1024]{1,0:T...) custom-call(bf16[128,1024]{1,0:T(8,128)(2,1)} %get-tuple-element.36., ...), custom_call_target="tpu_custom_call" | custom-call | tf_op jit(solution)/shard_map/clipped_update/pallas_call | solution.py:1582

commit v7 on v6

--- a/solution.py
+++ b/solution.py
@@ -410,7 +410,8 @@
     dot_t,
     dot_n,
     ot,
-    lse,
+    scale,
+    exps,
     delta,
     joined,
     joined_t,
@@ -839,7 +840,9 @@
         return step
 
     zero_row = jnp.zeros((1, 256), F32)
-    sums = lax.fori_loop(0, SEQ, unpack(dm // 4), (zero_row, zero_row))
+    sums = (zero_row, zero_row)
+    for sb in range(SEQ):
+        sums = unpack(dm // 4)(sb, sums)
     in_tree.near_of_mate()
     x_tree.near_of_mate()
     out_trade.end()
@@ -848,7 +851,9 @@
     cot_tree.own_to_mate()
     in_tree.far_of_mate()
     x_tree.far_of_mate()
-    cq, cf = lax.fori_loop(0, SEQ, unpack(dp_mate // 4), sums)
+    for sb in range(SEQ):
+        sums = unpack(dp_mate // 4)(sb, sums)
+    cq, cf = sums
 
     slab = jnp.transpose(wr[:, 384:512].astype(F32))
     vec_ref[...] = slab[64:80]
@@ -941,6 +946,11 @@
             s = jnp.where(seen, s, NEG_FILL)
         return s
 
+    def held(k0, keys, q0, queries):
+        qi, kc = q0 // CH, k0 // CH
+        rows, cols = slice(k0 % CH, k0 % CH + keys), slice(q0 % CH, q0 % CH + queries)
+        return exps.at[qi * (qi + 1) // 2 + kc, rows, cols]
+
     def spread(value, queries, fill):
         if queries == CH:
             return value
@@ -953,13 +963,16 @@
         top = functools.reduce(jnp.maximum, tops)
         total = jnp.zeros((1, CH), F32)
         out = jnp.zeros((64, CH), F32)
-        for (k0, keys, _, queries), s in parts:
+        for (k0, keys, q0, queries), s in parts:
             p = jnp.exp(s - top[:, CH - queries :])
             total = total + spread(jnp.sum(p, axis=0, keepdims=True), queries, 0.0)
-            out = out + spread(dot(vt[:, k0 : k0 + keys], p.astype(BF16)), queries, 0.0)
-        out = out / total
+            p = p.astype(BF16)
+            held(k0, keys, q0, queries)[...] = p
+            out = out + spread(dot(vt[:, k0 : k0 + keys], p), queries, 0.0)
+        one_over = 1.0 / total
+        out = out * one_over
         ot[:, lanes] = out
-        lse[:, lanes] = jnp.broadcast_to(top + jnp.log(total), (8, CH))
+        scale[:, lanes] = jnp.broadcast_to(one_over, (8, CH))
         joined_t[256:320, lanes] = out.astype(BF16)
         joined[8 * qi : 8 * qi + 8, :, 256:320] = (
             jnp.transpose(out).astype(BF16).reshape(8, SPAN, HEAD)
@@ -967,7 +980,7 @@
     out_tree.far_of_mate()
 
     def put_units(base, at, count):
-        @pl.loop(0, count // 2)
+        @pl.loop(0, count // 2, unroll=True)
         def _(i):
             pair = [unfold(wout_all[base + 2 * i + j].astype(F32)) for j in range(2)]
             rows = pl.ds(pl.multiple_of(at + i * 16, 16), 16)
@@ -1074,31 +1087,9 @@
     po.begin(((2, cot_tree.near_of_mate), (4, cot_tree.far_of_mate)))
     all_here(cot_all.at[pl.ds(0, 16)], c_given.at[0])
 
-    @pl.loop(0, NCH, unroll=True)
+    @pl.loop(0, 32, unroll=True)
     def _(i):
-        rows = pl.ds(pl.multiple_of(i * CH, CH), CH)
-        cot = jnp.concatenate([cot_all[inv_ref[8 * i + k]] for k in range(8)], axis=0)
-        cs[rows] = cot
-        back = dot_nt(cot, wo[...])
-        ag = back[:, 256:].astype(BF16).astype(F32)
-        ag_t = jnp.transpose(ag)
-        dot_n[rows] = ag.astype(BF16)
-        dot_t[:, rows] = ag_t.astype(BF16)
-        delta[:, rows] = jnp.broadcast_to(
-            jnp.sum(ag_t * ot[:, rows], axis=0, keepdims=True), (8, CH)
-        )
-        pg = back[:, :256] * dact[rows]
-        mixed[pl.ds(8 * i, 8), :, 0:256] = pg.astype(BF16).reshape(8, SPAN, 256)
-        mixed_t[0:256, rows] = jnp.transpose(pg).astype(BF16)
-
-    @pl.loop(0, 2, unroll=True)
-    def _(i):
-        left = dot(joined_t[...], cs[:, pl.ds(pl.multiple_of(i * 256, 256), 256)])
-        right = dot(joined_t[...], cs[:, pl.ds(pl.multiple_of(i * 256 + 512, 256), 256)])
-        units = jnp.concatenate([left.reshape(40, 8, 256), right.reshape(40, 8, 256)], axis=1)
-        lanes = pl.ds(pl.multiple_of(i * 256, 256), 256)
-        go_buf[pl.ds(8 * (1 - late), 32), :, lanes] = units[:32].astype(BF16)
-        go_buf[pl.ds(32 * late, 8), :, lanes] = units[32:].astype(BF16)
+        cs[pl.ds(SPAN * i, SPAN)] = cot_all[inv_ref[i]]
 
     def grads_by_owner(dst, base, columns):
         sums = jnp.sum(
@@ -1154,6 +1145,33 @@
         go_send.at[0],
         go_recv,
     )
+    @pl.loop(0, 2, unroll=True)
+    def _(i):
+        left = dot(joined_t[...], cs[:, pl.ds(pl.multiple_of(i * 256, 256), 256)])
+        right = dot(joined_t[...], cs[:, pl.ds(pl.multiple_of(i * 256 + 512, 256), 256)])
+        units = jnp.concatenate([left.reshape(40, 8, 256), right.reshape(40, 8, 256)], axis=1)
+        lanes = pl.ds(pl.multiple_of(i * 256, 256), 256)
+        go_buf[pl.ds(8 * (1 - late), 32), :, lanes] = units[:32].astype(BF16)
+        go_buf[pl.ds(32 * late, 8), :, lanes] = units[32:].astype(BF16)
+
+    go_sums.start()
+
+    @pl.loop(0, NCH, unroll=True)
+    def _(i):
+        rows = pl.ds(pl.multiple_of(i * CH, CH), CH)
+        cot = cs[rows]
+        back = dot_nt(cot, wo[...])
+        ag = back[:, 256:].astype(BF16).astype(F32)
+        ag_t = jnp.transpose(ag)
+        dot_n[rows] = ag.astype(BF16)
+        dot_t[:, rows] = ag_t.astype(BF16)
+        delta[:, rows] = jnp.broadcast_to(
+            jnp.sum(ag_t * ot[:, rows], axis=0, keepdims=True), (8, CH)
+        )
+        pg = back[:, :256] * dact[rows]
+        mixed[pl.ds(8 * i, 8), :, 0:256] = pg.astype(BF16).reshape(8, SPAN, 256)
+        mixed_t[0:256, rows] = jnp.transpose(pg).astype(BF16)
+
     lanes_d = lane_iota((D, 128))
     vg[...] = jnp.where((lanes_d == 71) | (lanes_d == 72), vg[...], 0.0)
     lanes_h = lane_iota((64, 128))
@@ -1164,17 +1182,15 @@
         vg[rows] += jnp.where(lanes_h == 64 + 9 + w // 16, cols_f[64 * r : 64 * r + 64], 0.0)
     grads_by_owner(gf, 0, 2)
     gf_sums.start()
+    po.tree.far_of_me()
     po.of_mate()
-
-    go_sums.start()
-    po.tree.far_of_me()
 
     for qi in reversed(range(NCH)):
         lanes = slice(qi * CH, (qi + 1) * CH)
         dq = jnp.zeros((64, CH), F32)
         for k0, keys, q0, queries in tiles(qi):
             at, cols = slice(k0, k0 + keys), slice(q0, q0 + queries)
-            p = jnp.exp(scores(k0, keys, q0, queries) - lse[0:1, cols])
+            p = held(k0, keys, q0, queries)[...].astype(F32) * scale[0:1, cols]
             dp = dot(vn[at, 0:64], dot_t[:, cols])
             ds = (p * (dp - delta[0:1, cols])).astype(BF16)
             dv = dot(p.astype(BF16), dot_n[cols])
@@ -1187,10 +1203,6 @@
                 dvn[at] += dv
                 dkn[at] += dk
         dqt[:, lanes] = dq * 0.125
-        if qi == 1:
-            po.tree.near_late()
-        if qi == 0:
-            gf_sums.middle()
 
     @pl.loop(0, NCH, unroll=True)
     def _(i):
@@ -1206,8 +1218,11 @@
     cols_q = jnp.sum(mixed_t[256:448].astype(F32), axis=1, keepdims=True)
     for i in range(3):
         vg[head_rows] += jnp.where(lanes_h == 68 + i, cols_q[64 * i : 64 * i + 64], 0.0)
+    go_sums.middle()
     grads_by_owner(gq, 256, 0)
     gq_sums.start()
+    po.tree.near_late()
+    gf_sums.middle()
 
     all_sent(cot_all.at[pl.ds(0, 30)], c_send.at[0])
 
@@ -1227,11 +1242,18 @@
     def squares_of(value):
         return jnp.sum(jnp.sum(value * value, axis=0), axis=0, keepdims=True)
 
+    def fold_rows(value):
+        return jnp.concatenate([value[:, :, :128], value[:, :, 128:]], axis=1).astype(BF16)
+
+    f_squares = []
+
     def hidden_on():
-        f_part[...] = gf_sums.total().reshape(SEQ, 8, 256)
-        own_sums(f_part, f_sum, bf_send, bf_recv)
-
-    hg.begin(((2, go_sums.middle), (4, hidden_on)))
+        value = gf_sums.total().reshape(SEQ, 8, 256)
+        f_squares.append(squares_of(value))
+        f_part[...] = fold_rows(value)
+
+
+    hg.begin(((6, hidden_on),))
     gq_sums.middle()
     out_total = go_sums.total()
     out_part[...] = out_total
@@ -1245,7 +1267,7 @@
     out_back.begin()
     kept(keep_total)
     out_squares = squares_of(out_total)
-    squares = squares_of(f_part[...]) + out_squares[:, :256] + out_squares[:, 256:]
+    squares = f_squares[0] + out_squares[:, :256] + out_squares[:, 256:]
 
     hg.tree.far_of_me()
     total = gq_sums.total().reshape(SEQ, 8, 256)
@@ -1262,8 +1284,9 @@
         ta_copy(k, lax.rem(me + k, SEQ), me).start()
 
     got_a[me] = tile_a[...]
-    q_part[...] = total
+    q_part[...] = fold_rows(total)
     own_sums(q_part, q_sum, bq_send, bq_recv)
+    own_sums(f_part, f_sum, bf_send, bf_recv)
     hg.of_mate()
     hg.tree.near_late()
     out_back.relay_on()
@@ -1295,10 +1318,9 @@
     for s in range(SEQ):
         for j, p in enumerate(PIECES[s]):
             at = 64 * int(p)
-            if j < 3:
-                grad_in[:, at : at + 64] = q_sum[s, :, 64 * j : 64 * j + 64]
-            else:
-                grad_in[:, at : at + 64] = f_sum[s, :, 64 * j - 192 : 64 * j - 128]
+            ref, k = (q_sum, j) if j < 3 else (f_sum, j - 3)
+            both = ref[s].astype(F32)
+            grad_in[:, at : at + 64] = both[8 * (k // 2) : 8 * (k // 2) + 8, 64 * (k % 2) : 64 * (k % 2) + 64]
     in_store.start()
     out_back.end()
     for u in range(5):
@@ -1370,8 +1392,8 @@
             buf((TOK, D)),
             buf((8, 7 * D), F32),
             buf((40, D), F32),
-            buf((SEQ, 8, 256), F32),
-            buf((SEQ, 8, 256), F32),
+            buf((SEQ, 16, 128)),
+            buf((SEQ, 16, 128)),
             buf((5, 16, 512), F32),
             buf((8, 128), F32),
             buf((8, 128), F32),
@@ -1403,6 +1425,7 @@
             buf((ROW, 64)),
             buf((64, ROW), F32),
             buf((8, ROW), F32),
+            buf((10, CH, CH)),
             buf((8, ROW), F32),
             buf((32, SPAN, 320)),
             buf((320, ROW)),
@@ -1424,8 +1447,8 @@
             buf((8, 8, 16, 256)),
             buf((8, 8, 16, 256)),
             buf((8, 5, 16, 512)),
-            buf((SEQ, 8, 256), F32),
-            buf((SEQ, 8, 256), F32),
+            buf((SEQ, 16, 128)),
+            buf((SEQ, 16, 128)),
             buf((16, 128), F32),
             buf((8, 128), F32),
             buf((SEQ, 16, 128), F32),

time: 99.8 us -> 97.6 us (0.978)
  Pallas kernels: 97.8 us -> 95.8 us
    pallas_call x1, Pallas kernels: 93.9 us -> 91.9 us  [layer_call(): pl.pallas_call(layer_kernel, out_shape=(sds((TOK, D), BF16), sds((TOK, D)...]
where the time goes in v7:
time: 97.6 us; the launch traced here: 97.2 us
  Pallas kernels  95.8 us (98%)
  between operations  1.48 us (2%)
    pallas_call x1, Pallas kernels, layer_call(): pl.pallas_call(layer_kernel, out_shape=(sds((TOK, D), BF16), sds((TOK, D)...  91.9 us
    pallas_call x1, Pallas kernels, update_call(): pl.pallas_call(update_kernel, out_shape=(sds((1, 1), F32),) + tuple((sds(...  3.9 us

profile of v7, /device:TPU:1, one launch (start us, length us, event | category | flops | bytes accessed | tf_op | source)
XLA Modules:
  0.0 97.2 jit_solution(3616876407904840152)
XLA Ops:
  1.3 91.9 %layer_of_one_row.1 = (bf16[128,1024]{1,0:T(8,128)(2,1)}, bf16[128,1024]{1,0:T(8,128)(2,1)}, f32[8,7168]{1,0:T(8,128)}, f32[40,1024]{1,0:T(8,128)}, f32[8,128]{1,0:T(8,128)}, /*index=5*/f32[8,128]{1,0:T(8,128)}) custom-call(s32[2,16]{1,0:T(2,128)} %bitcast.19, s32[1]{0:T(128)S(6)} %copy.30.len_ref, bf16[128,1024]{1,0:T(8,128)(2,1)} %bitcast.13, ...), custom_call_target="tpu_custom_call" | custom-call | tf_op jit(solution)/shard_map/layer_of_one_row/pallas_call | solution.py:1371
  93.2 3.9 %clipped_update.1 = (f32[1,1]{1,0:T(1,128)}, bf16[128,1024]{1,0:T(8,128)(2,1)}, bf16[128,1024]{1,0:T(8,128)(2,1)}, f32[8,7168]{1,0:T(8,128)}, f32[40,1024]{1,0:T...) custom-call(bf16[128,1024]{1,0:T(8,128)(2,1)} %get-tuple-element.36., ...), custom_call_target="tpu_custom_call" | custom-call | tf_op jit(solution)/shard_map/clipped_update/pallas_call | solution.py:1605

commit v8 on v7

--- a/solution.py
+++ b/solution.py
@@ -1040,16 +1040,21 @@
             elif n in (4, 5):
                 self.tree.near_early(order[n][1])
 
-        def begin(self, between=()):
+        def begin(self, between=(), pairs=6):
             for n in range(8):
                 if n % 2 == 0:
                     self.compute(n)
                 for at, step in between:
                     if at == n:
                         step()
-                if n > 2:
+                if 2 < n < pairs + 3:
                     self.pair(n - 3)
-            self.pair(5)
+            if pairs == 6:
+                self.pair(5)
+
+        def pair_rest(self, pairs):
+            for n in range(pairs, 6):
+                self.pair(n)
 
         def of_mate(self):
             self.pair(6)
@@ -1084,7 +1089,7 @@
         h_recv,
     )
     all_sent(xh_all.at[pl.ds(0, 30)], x_send.at[0])
-    po.begin(((2, cot_tree.near_of_mate), (4, cot_tree.far_of_mate)))
+    po.begin(((2, cot_tree.near_of_mate), (3, cot_tree.far_of_mate)), 3)
     all_here(cot_all.at[pl.ds(0, 16)], c_given.at[0])
 
     @pl.loop(0, 32, unroll=True)
@@ -1155,6 +1160,7 @@
         go_buf[pl.ds(32 * late, 8), :, lanes] = units[32:].astype(BF16)
 
     go_sums.start()
+    po.pair_rest(3)
 
     @pl.loop(0, NCH, unroll=True)
     def _(i):
@@ -1269,7 +1275,6 @@
     out_squares = squares_of(out_total)
     squares = f_squares[0] + out_squares[:, :256] + out_squares[:, 256:]
 
-    hg.tree.far_of_me()
     total = gq_sums.total().reshape(SEQ, 8, 256)
     weights = jnp.where(lane_iota(total.shape) < 192, total, 0.0)
     squares = squares + squares_of(weights)
@@ -1284,11 +1289,11 @@
         ta_copy(k, lax.rem(me + k, SEQ), me).start()
 
     got_a[me] = tile_a[...]
+    hg.tree.far_of_me()
     q_part[...] = fold_rows(total)
     own_sums(q_part, q_sum, bq_send, bq_recv)
     own_sums(f_part, f_sum, bf_send, bf_recv)
     hg.of_mate()
-    hg.tree.near_late()
     out_back.relay_on()
     all_here(got_a.at[pl.ds(0, SEQ - 1)], ta_recv.at[0])
     sums = jnp.sum(got_a[...], axis=0)
@@ -1303,6 +1308,7 @@
     def _(k):
         tb_copy(k, lax.rem(dm + k, DP), dm).start()
 
+    hg.tree.near_late()
     got_b[dm] = tile_b[...]
     small[...] = jnp.zeros((128, 128), F32)
     small[0:16] = vec_total

time: 97.6 us -> 96.5 us (0.989)
  Pallas kernels: 95.8 us -> 94.8 us
where the time goes in v8:
time: 96.5 us; the launch traced here: 96.3 us
  Pallas kernels  94.8 us (98%)
  between operations  1.48 us (2%)
    pallas_call x1, Pallas kernels, layer_call(): pl.pallas_call(layer_kernel, out_shape=(sds((TOK, D), BF16), sds((TOK, D)...  90.9 us
    pallas_call x1, Pallas kernels, update_call(): pl.pallas_call(update_kernel, out_shape=(sds((1, 1), F32),) + tuple((sds(...  3.9 us

profile of v8, /device:TPU:1, one launch (start us, length us, event | category | flops | bytes accessed | tf_op | source)
XLA Modules:
  0.0 96.3 jit_solution(8613735782636032389)
XLA Ops:
  1.3 90.9 %layer_of_one_row.1 = (bf16[128,1024]{1,0:T(8,128)(2,1)}, bf16[128,1024]{1,0:T(8,128)(2,1)}, f32[8,7168]{1,0:T(8,128)}, f32[40,1024]{1,0:T(8,128)}, f32[8,128]{1,0:T(8,128)}, /*index=5*/f32[8,128]{1,0:T(8,128)}) custom-call(s32[2,16]{1,0:T(2,128)} %bitcast.19, s32[1]{0:T(128)S(6)} %copy.30.len_ref, bf16[128,1024]{1,0:T(8,128)(2,1)} %bitcast.13, ...), custom_call_target="tpu_custom_call" | custom-call | tf_op jit(solution)/shard_map/layer_of_one_row/pallas_call | solution.py:1377
  92.2 3.9 %clipped_update.1 = (f32[1,1]{1,0:T(1,128)}, bf16[128,1024]{1,0:T(8,128)(2,1)}, bf16[128,1024]{1,0:T(8,128)(2,1)}, f32[8,7168]{1,0:T(8,128)}, f32[40,1024]{1,0:T...) custom-call(bf16[128,1024]{1,0:T(8,128)(2,1)} %get-tuple-element.36., ...), custom_call_target="tpu_custom_call" | custom-call | tf_op jit(solution)/shard_map/clipped_update/pallas_call | solution.py:1611

commit v9 on v8

--- a/solution.py
+++ b/solution.py
@@ -1022,8 +1022,8 @@
             )
 
         def compute(self, n):
-            chips = [seq_turn(*order[m]) // 2 for m in (n, n + 1)]
-            value = self.part(chips).astype(BF16).reshape(8, SPAN, D)
+            chips = [seq_turn(*order[m]) // 2 for m in range(n, min(n + (2 if n else 1), 8))]
+            value = self.part(chips).astype(BF16).reshape(4 * len(chips), SPAN, D)
             for m, j in enumerate(chips):
                 self.buf[pl.ds(4 * j, 4)] = value[4 * m : 4 * m + 4]
                 self.to_sib(j).start()
@@ -1042,15 +1042,13 @@
 
         def begin(self, between=(), pairs=6):
             for n in range(8):
-                if n % 2 == 0:
+                if n == 0 or n % 2 == 1:
                     self.compute(n)
                 for at, step in between:
                     if at == n:
                         step()
-                if 2 < n < pairs + 3:
-                    self.pair(n - 3)
-            if pairs == 6:
-                self.pair(5)
+                if 1 < n < pairs + 2:
+                    self.pair(n - 2)
 
         def pair_rest(self, pairs):
             for n in range(pairs, 6):
@@ -1278,8 +1276,9 @@
     total = gq_sums.total().reshape(SEQ, 8, 256)
     weights = jnp.where(lane_iota(total.shape) < 192, total, 0.0)
     squares = squares + squares_of(weights)
-    tile_a[...] = jnp.transpose(total[:, :, 128:].reshape(128, 128))[64:80]
-    tile_a[15:16] = squares[:, :128] + squares[:, 128:]
+    vec_rows = jnp.transpose(total[:, :, 128:].reshape(128, 128))[64:80]
+    row_of = lax.broadcasted_iota(jnp.int32, vec_rows.shape, 0)
+    tile_a[...] = jnp.where(row_of == 15, squares[:, :128] + squares[:, 128:], vec_rows).astype(BF16)
 
     def ta_copy(k, to, frm):
         return remote(tile_a, got_a.at[frm], ta_send.at[0], ta_recv.at[0], {"seq": to})
@@ -1296,7 +1295,7 @@
     hg.of_mate()
     out_back.relay_on()
     all_here(got_a.at[pl.ds(0, SEQ - 1)], ta_recv.at[0])
-    sums = jnp.sum(got_a[...], axis=0)
+    sums = jnp.sum(got_a[...].astype(F32), axis=0)
     vec_total = jnp.where(lax.broadcasted_iota(jnp.int32, sums.shape, 0) < VEC_ROWS, sums, 0.0)
     row = sums[15:16] + jnp.sum(vec_total * vec_total, axis=0, keepdims=True)
     tile_b[...] = jnp.broadcast_to(jnp.sum(row, axis=1, keepdims=True), (8, 128))
@@ -1455,9 +1454,9 @@
             buf((8, 5, 16, 512)),
             buf((SEQ, 16, 128)),
             buf((SEQ, 16, 128)),
-            buf((16, 128), F32),
+            buf((16, 128)),
             buf((8, 128), F32),
-            buf((SEQ, 16, 128), F32),
+            buf((SEQ, 16, 128)),
             buf((DP, 8, 128), F32),
             dma((1,)),
             dma((1,)),

time: 96.5 us -> 95.8 us (level)
  no operation moved by 1% of the time
where the time goes in v9:
time: 95.8 us; the launch traced here: 95.6 us
  Pallas kernels  94.2 us (98%)
  between operations  1.48 us (2%)
    pallas_call x1, Pallas kernels, layer_call(): pl.pallas_call(layer_kernel, out_shape=(sds((TOK, D), BF16), sds((TOK, D)...  90.3 us
    pallas_call x1, Pallas kernels, update_call(): pl.pallas_call(update_kernel, out_shape=(sds((1, 1), F32),) + tuple((sds(...  3.9 us

profile of v9, /device:TPU:1, one launch (start us, length us, event | category | flops | bytes accessed | tf_op | source)
XLA Modules:
  0.0 95.6 jit_solution(13540987605686869644)
XLA Ops:
  1.3 90.3 %layer_of_one_row.1 = (bf16[128,1024]{1,0:T(8,128)(2,1)}, bf16[128,1024]{1,0:T(8,128)(2,1)}, f32[8,7168]{1,0:T(8,128)}, f32[40,1024]{1,0:T(8,128)}, f32[8,128]{1,0:T(8,128)}, /*index=5*/f32[8,128]{1,0:T(8,128)}) custom-call(s32[2,16]{1,0:T(2,128)} %bitcast.19, s32[1]{0:T(128)S(6)} %copy.30.len_ref, bf16[128,1024]{1,0:T(8,128)(2,1)} %bitcast.13, ...), custom_call_target="tpu_custom_call" | custom-call | tf_op jit(solution)/shard_map/layer_of_one_row/pallas_call | solution.py:1376
  91.6 3.9 %clipped_update.1 = (f32[1,1]{1,0:T(1,128)}, bf16[128,1024]{1,0:T(8,128)(2,1)}, bf16[128,1024]{1,0:T(8,128)(2,1)}, f32[8,7168]{1,0:T(8,128)}, f32[40,1024]{1,0:T...) custom-call(bf16[128,1024]{1,0:T(8,128)(2,1)} %get-tuple-element.36., ...), custom_call_target="tpu_custom_call" | custom-call | tf_op jit(solution)/shard_map/clipped_update/pallas_call | solution.py:1610
